TPU v7x, 32 devices: a whole 2x2x4 slice. The times are simulated.
32 devices in a mesh: rows: 8 (over z, y), seq: 4 (over x, core).
Axes of the slice: x: 2, y: 2, z: 4, core: 2. Of those that a mesh axis runs over, the one named last changes fastest.
Arguments:
- hidden_in: bfloat16 [2, 16, 1024, 768], P(None, 'rows', 'seq'), may hold values from -6 to 6
- segments: int32 [2, 16, 1024], P(None, 'rows', 'seq'), may hold values from 0 to 1, as said below
- grad_mask: int32 [2, 16, 1024], P(None, 'rows', 'seq'), may hold values 0 or 1
- grad_out: bfloat16 [2, 16, 1024, 768], P(None, 'rows', 'seq'), may hold values from -6 to 6
- query_proj: bfloat16 [768, 768], replicated, may hold values from -0.21875 to 0.21875
- query_bias: bfloat16 [768], replicated, may hold values from -3 to 3
- key_proj: bfloat16 [768, 768], replicated, may hold values from -0.21875 to 0.21875
- value_proj: bfloat16 [768, 768], replicated, may hold values from -0.21875 to 0.21875
- value_bias: bfloat16 [768], replicated, may hold values from -3 to 3
- output_proj: bfloat16 [768, 768], replicated, may hold values from -0.875 to 0.875
- output_bias: bfloat16 [768], replicated, may hold values from -1.75 to 1.75
- first_gain: bfloat16 [768], replicated, may hold values from 0.25 to 1.75
- first_shift: bfloat16 [768], replicated, may hold values from -3 to 3
- expand_proj: bfloat16 [768, 3072], replicated, may hold values from -0.21875 to 0.21875
- expand_bias: bfloat16 [3072], replicated, may hold values from -3 to 3
- shrink_proj: bfloat16 [3072, 768], replicated, may hold values from -0.109375 to 0.109375
- shrink_bias: bfloat16 [768], replicated, may hold values from -1.75 to 1.75
- second_gain: bfloat16 [768], replicated, may hold values from 0.25 to 1.75
- second_shift: bfloat16 [768], replicated, may hold values from -3 to 3
Outputs:
- layer_out: bfloat16 [2, 16, 1024, 768], P(None, 'rows', 'seq')
- grad_in: bfloat16 [2, 16, 1024, 768], P(None, 'rows', 'seq')
- query_proj_grad: float32 [768, 768], replicated
- query_bias_grad: float32 [768], replicated
- key_proj_grad: float32 [768, 768], replicated
- value_proj_grad: float32 [768, 768], replicated
- value_bias_grad: float32 [768], replicated
- output_proj_grad: float32 [768, 768], replicated
- output_bias_grad: float32 [768], replicated
- first_gain_grad: float32 [768], replicated
- first_shift_grad: float32 [768], replicated
- expand_proj_grad: float32 [768, 3072], replicated
- expand_bias_grad: float32 [3072], replicated
- shrink_proj_grad: float32 [3072, 768], replicated
- shrink_bias_grad: float32 [768], replicated
- second_gain_grad: float32 [768], replicated
- second_shift_grad: float32 [768], replicated
Inputs may be any that keep to these rules, and one draw needn't show every extreme that they name: `segments`: in every row the segment numbers are 0 up to a cut and 1 after it; both occur in every row.
All inputs are finite; a program needn't handle non-finite values. No bound on the sum of `grad_mask` on one device may be relied on, other than what follows from the above.
Results may differ from a plain program's by a relative error of at most 0.013.
Values may be sent and summed in bfloat16 or wider, within the bound.
No kernel may reach another device: no remote copies, remote signals or barrier semaphores. Data moves between devices by JAX's collectives and lax.ppermute only.
A program may use at most 320 MiB of HBM per device.

v0:
```python
import jax
import jax.numpy as jnp
from jax import lax
from jax.sharding import PartitionSpec as P

H = 12
DH = 64


def left_dot(first, second):
    return lax.dot_general(
        first, second, (((0,), (0,)), ((), ())), preferred_element_type=jnp.float32
    )


def right_dot(first, second):
    return lax.dot_general(
        first, second, (((1,), (1,)), ((), ())), preferred_element_type=jnp.float32
    )


def layer_norm(values, gain, shift):
    centred = values - jnp.mean(values, -1, keepdims=True)
    spread = jnp.mean(centred * centred, -1, keepdims=True)
    return gain * centred * lax.rsqrt(spread + 1e-06) + shift


def gelu_exact(values):
    return jax.nn.gelu(values, approximate=False)


def scores_of(query_heads, key_heads, seg_query, seg_keys):
    raw = (
        jnp.einsum("bqhd,bkhd->bhqk", query_heads, key_heads, preferred_element_type=jnp.float32)
        * 0.125
    )
    same = seg_query[:, None, :, None] == seg_keys[:, None, None, :]
    return jnp.where(same, raw, -1e30)


def add_pair(first, second):
    return first + second


def column_sum(values):
    return jnp.sum(values.astype(jnp.float32), 0)


def body(
    hidden_in,
    segments,
    grad_mask,
    grad_out,
    query_proj,
    query_bias,
    key_proj,
    value_proj,
    value_bias,
    output_proj,
    output_bias,
    first_gain,
    first_shift,
    expand_proj,
    expand_bias,
    shrink_proj,
    shrink_bias,
    second_gain,
    second_shift,
):
    rows_here = hidden_in.shape[1]
    piece_len = hidden_in.shape[2]
    width = hidden_in.shape[3]
    tokens = rows_here * piece_len
    head_count = H
    head_size = DH
    query_add = query_bias.astype(jnp.float32)
    value_add = value_bias.astype(jnp.float32)
    output_add = output_bias.astype(jnp.float32)
    expand_add = expand_bias.astype(jnp.float32)
    shrink_add = shrink_bias.astype(jnp.float32)
    gain_one = first_gain.astype(jnp.float32)
    shift_one = first_shift.astype(jnp.float32)
    gain_two = second_gain.astype(jnp.float32)
    shift_two = second_shift.astype(jnp.float32)
    outputs = []
    input_grads = []
    totals = None
    for micro_step in range(hidden_in.shape[0]):
        inputs = hidden_in[micro_step].reshape(tokens, width)
        queries = (
            jnp.dot(inputs, query_proj, preferred_element_type=jnp.float32) + query_add
        ).astype(jnp.bfloat16)
        keys_own = jnp.dot(inputs, key_proj, preferred_element_type=jnp.float32).astype(
            jnp.bfloat16
        )
        values_own = (
            jnp.dot(inputs, value_proj, preferred_element_type=jnp.float32) + value_add
        ).astype(jnp.bfloat16)
        keys_own = keys_own.reshape(rows_here, piece_len, width)
        values_own = values_own.reshape(rows_here, piece_len, width)
        seg_query = segments[micro_step]
        keys_all, values_all, seg_keys = (
            lax.all_gather(keys_own, "seq", axis=1, tiled=True),
            lax.all_gather(values_own, "seq", axis=1, tiled=True),
            lax.all_gather(seg_query, "seq", axis=1, tiled=True),
        )
        query_heads = queries.reshape(rows_here, piece_len, head_count, head_size)
        key_heads = keys_all.reshape(rows_here, -1, head_count, head_size)
        value_heads = values_all.reshape(rows_here, -1, head_count, head_size)
        scores = scores_of(query_heads, key_heads, seg_query, seg_keys)
        peak = jnp.max(scores, -1, keepdims=True)
        raised = jnp.exp(scores - peak)
        total = jnp.sum(raised, -1, keepdims=True)
        probs = raised / total
        log_total = peak + jnp.log(total)
        mixed = jnp.einsum(
            "bhqk,bkhd->bqhd",
            probs.astype(jnp.bfloat16),
            value_heads,
            preferred_element_type=jnp.float32,
        )
        mixed = mixed.reshape(tokens, width).astype(jnp.bfloat16)
        first_sum = (
            inputs.astype(jnp.float32)
            + jnp.dot(mixed, output_proj, preferred_element_type=jnp.float32)
            + output_add
        )
        normed, first_back = jax.vjp(layer_norm, first_sum, gain_one, shift_one)
        normed_low = normed.astype(jnp.bfloat16)
        expanded = jnp.dot(normed_low, expand_proj, preferred_element_type=jnp.float32) + expand_add
        activated, gelu_back = jax.vjp(gelu_exact, expanded)
        active_low = activated.astype(jnp.bfloat16)
        second_sum = (
            normed
            + jnp.dot(active_low, shrink_proj, preferred_element_type=jnp.float32)
            + shrink_add
        )
        result, second_back = jax.vjp(layer_norm, second_sum, gain_two, shift_two)
        outputs.append(result.astype(jnp.bfloat16).reshape(rows_here, piece_len, width))
        upstream = grad_out[micro_step].reshape(tokens, width).astype(jnp.float32)
        upstream = upstream * grad_mask[micro_step].reshape(tokens, 1).astype(jnp.float32)
        d_second, d_gain_two, d_shift_two = second_back(upstream)
        d_down = d_second.astype(jnp.bfloat16)
        d_active = right_dot(d_down, shrink_proj)
        (d_expand,) = gelu_back(d_active)
        d_expand_low = d_expand.astype(jnp.bfloat16)
        d_normed = d_second + right_dot(d_expand_low, expand_proj)
        d_first, d_gain_one, d_shift_one = first_back(d_normed)
        d_attn = d_first.astype(jnp.bfloat16)
        d_mixed = right_dot(d_attn, output_proj).astype(jnp.bfloat16)
        scores = scores_of(query_heads, key_heads, seg_query, seg_keys)
        probs = jnp.exp(scores - log_total)
        d_mixed_heads = d_mixed.reshape(rows_here, piece_len, head_count, head_size)
        d_probs = jnp.einsum(
            "bqhd,bkhd->bhqk", d_mixed_heads, value_heads, preferred_element_type=jnp.float32
        )
        correction = jnp.sum(probs * d_probs, -1, keepdims=True)
        d_scores = (probs * (d_probs - correction)).astype(jnp.bfloat16)
        d_query = (
            jnp.einsum("bhqk,bkhd->bqhd", d_scores, key_heads, preferred_element_type=jnp.float32)
            * 0.125
        )
        d_query = d_query.reshape(tokens, width).astype(jnp.bfloat16)
        d_keys_all = (
            jnp.einsum("bhqk,bqhd->bkhd", d_scores, query_heads, preferred_element_type=jnp.float32)
            * 0.125
        )
        d_values_all = jnp.einsum(
            "bhqk,bqhd->bkhd",
            probs.astype(jnp.bfloat16),
            d_mixed_heads,
            preferred_element_type=jnp.float32,
        )
        d_keys, d_values = (
            lax.psum_scatter(
                d_keys_all.reshape(rows_here, -1, width), "seq", scatter_dimension=1, tiled=True
            ),
            lax.psum_scatter(
                d_values_all.reshape(rows_here, -1, width), "seq", scatter_dimension=1, tiled=True
            ),
        )
        d_key_low = d_keys.reshape(tokens, width).astype(jnp.bfloat16)
        d_value_low = d_values.reshape(tokens, width).astype(jnp.bfloat16)
        d_input = (
            d_first
            + right_dot(d_query, query_proj)
            + right_dot(d_key_low, key_proj)
            + right_dot(d_value_low, value_proj)
        )
        input_grads.append(d_input.astype(jnp.bfloat16).reshape(rows_here, piece_len, width))
        micro_grads = (
            left_dot(inputs, d_query),
            column_sum(d_query),
            left_dot(inputs, d_key_low),
            left_dot(inputs, d_value_low),
            column_sum(d_value_low),
            left_dot(mixed, d_attn),
            column_sum(d_attn),
            d_gain_one,
            d_shift_one,
            left_dot(normed_low, d_expand_low),
            column_sum(d_expand_low),
            left_dot(active_low, d_down),
            column_sum(d_down),
            d_gain_two,
            d_shift_two,
        )
        totals = micro_grads if totals is None else jax.tree.map(add_pair, totals, micro_grads)
    totals = lax.psum(totals, ("rows", "seq"))
    return (
        jnp.stack(outputs),
        jnp.stack(input_grads),
        totals[0],
        totals[1],
        totals[2],
        totals[3],
        totals[4],
        totals[5],
        totals[6],
        totals[7],
        totals[8],
        totals[9],
        totals[10],
        totals[11],
        totals[12],
        totals[13],
        totals[14],
    )


def solution(mesh):
    return jax.shard_map(
        body,
        mesh=mesh,
        in_specs=(
            P(None, "rows", "seq", None),
            P(None, "rows", "seq"),
            P(None, "rows", "seq"),
            P(None, "rows", "seq", None),
            P(),
            P(),
            P(),
            P(),
            P(),
            P(),
            P(),
            P(),
            P(),
            P(),
            P(),
            P(),
            P(),
            P(),
            P(),
        ),
        out_specs=(
            P(None, "rows", "seq", None),
            P(None, "rows", "seq", None),
            P(),
            P(),
            P(),
            P(),
            P(),
            P(),
            P(),
            P(),
            P(),
            P(),
            P(),
            P(),
            P(),
            P(),
            P(),
        ),
        check_vma=False,
    )
```

profile of v0, /device:TPU:0, one launch (start us, length us, event | category | flops | bytes accessed | tf_op | source)
XLA Modules:
  0.0 1015.5 jit_solution(9023951649618591085)
XLA Ops:
  49.2 12.9 %fusion.13 = (f32[2,12,256]{2,1,0:T(8,128)S(1)}, f32[2,12,256,1024]{3,2,1,0:T(8,128)}) fusion(pred[2,256,1024]{2,1,0:T(8,128)(4,1)S(1)} %broadcast_compare_fusion, bf16[2,1024,12,64]{1,3,2,0:T(8,128)(2,1)} %bitcast.192, bf16[2,256,12,64]{1,0,3,2:T(2,128)(2,1)S(1)} %reshape.319), kind=kOutput, calls=%fused_computation.25 | convolution fusion | flops 824174592 | bytes 29646848 | tf_op jit(solution)/shard_map/bqhd,bkhd->bhqk/dot_general | solution.py:34
  62.1 11.8 %fusion.1 = f32[2,12,256]{2,1,0:T(8,128)S(1)} fusion(f32[2,12,256]{2,1,0:T(8,128)S(1)} %get-tuple-element.136, f32[2,12,256,1024]{3,2,1,0:T(8,128)} %get-tuple-element.137, pred[2,256,1024]{2,1,0:T(8,128)(4,1)S(1)} %broadcast_compare_fusion), kind=kLoop, calls=%fused_computation.13 | loop fusion | flops 25159680 | bytes 25739264 | tf_op jit(solution)/shard_map/reduce_sum | solution.py:113
  78.7 13.5 %fusion.33 = bf16[2,256,12,64]{1,3,2,0:T(8,128)(2,1)S(1)} fusion(bf16[2,1024,12,64]{1,3,2,0:T(8,128)(2,1)} %bitcast.212, f32[2,12,256]{2,1,0:T(8,128)S(1)} %fusion.1, f32[2,12,256]{2,1,0:T(8,128)S(1)} %get-tuple-element.136, f32[2,12,256,1024]{3,2,1,0:T(8,128)} %get-tuple-element.137, pred[2,256,1024]{2,1,0:T(8,128)(4,1)S(1)} %broadcast_compare_fusion), kind=kOutput, calls=%fused_computation.131 | convolution fusion | flops 837156864 | bytes 29671424 | tf_op jit(solution)/shard_map/bhqk,bkhd->bqhd/dot_general | solution.py:116
  94.1 9.6 all-gather.9.cloned.1.call-done
  111.9 10.8 %fusion.12 = (f32[2,12,256]{2,1,0:T(8,128)S(1)}, f32[2,12,256,1024]{3,2,1,0:T(8,128)}) fusion(pred[2,256,1024]{2,1,0:T(8,128)(4,1)S(1)} %broadcast_compare_fusion.1, bf16[2,1024,12,64]{1,3,2,0:T(8,128)(2,1)S(1)} %bitcast.194, bf16[2,256,12,64]{1,0,3,2:T(2,128)(2,1)S(1)} %copy-done.26), kind=kOutput, calls=%fused_computation.24 | convolution fusion | flops 824174592 | bytes 29646848 | tf_op jit(solution)/shard_map/bqhd,bkhd->bhqk/dot_general | solution.py:34
  122.7 11.8 %fusion = f32[2,12,256]{2,1,0:T(8,128)S(1)} fusion(f32[2,12,256]{2,1,0:T(8,128)S(1)} %get-tuple-element.132, f32[2,12,256,1024]{3,2,1,0:T(8,128)} %get-tuple-element.133, pred[2,256,1024]{2,1,0:T(8,128)(4,1)S(1)} %broadcast_compare_fusion.1), kind=kLoop, calls=%fused_computation.12 | loop fusion | flops 25159680 | bytes 25739264 | tf_op jit(solution)/shard_map/reduce_sum | solution.py:113
  139.3 12.5 %fusion.32 = bf16[2,256,12,64]{1,3,2,0:T(8,128)(2,1)S(1)} fusion(bf16[2,1024,12,64]{1,3,2,0:T(8,128)(2,1)} %bitcast.210, f32[2,12,256]{2,1,0:T(8,128)S(1)} %fusion, f32[2,12,256]{2,1,0:T(8,128)S(1)} %get-tuple-element.132, f32[2,12,256,1024]{3,2,1,0:T(8,128)} %get-tuple-element.133, pred[2,256,1024]{2,1,0:T(8,128)(4,1)S(1)} %broadcast_compare_fusion.1), kind=kOutput, calls=%fused_computation.130 | convolution fusion | flops 837156864 | bytes 29671424 | tf_op jit(solution)/shard_map/bhqk,bkhd->bqhd/dot_general | solution.py:116
  159.7 34.8 %multiply_convert_fusion.3 = (bf16[512,3072]{1,0:T(8,128)(2,1)S(1)}, f32[512,3072]{1,0:T(8,128)}, bf16[512,3072]{1,0:T(8,128)(2,1)S(1)}, f32[512,3072]{1,0:T(8,128)}, f32[512,3072]{1,0:T(8,128)}) fusion(f32[3072]{0:T(1024)S(1)} %convert_element_type.286, f32[512,3072]{1,0:T(8,128)S(1)} %fusion.61, bf16[768,3072]{1,0:T(8,128)(2,1)S(1)} %bitcast.255, ...), kind=kOutput, calls=%fused_computation.45 | convolution fusion | flops 2625503232 | bytes 37771264 | tf_op jit(solution)/shard_map/dot_general | solution.py:130
  213.5 18.1 %convert_reduce_fusion.1 = (f32[3072]{0:T(1024)}, bf16[512,3072]{1,0:T(8,128)(2,1)}, f32[3072]{0:T(1024)}, bf16[512,3072]{1,0:T(8,128)(2,1)}) fusion(f32[512,3072]{1,0:T(8,128)} %get-tuple-element.105, f32[512,3072]{1,0:T(8,128)} %get-tuple-element.140, f32[3072]{0:T(1024)S(1)} %copy-done.102, f32[512,3072]{1,0:T(8,128)} %fusion.80, ...), kind=kOutput, calls=%fused_computation.29 | convolution fusion | flops 2469390336 | bytes 43290624 | tf_op jit(solution)/shard_map/dot_general | solution.py:17
  250.9 19.5 %multiply_reduce_fusion = (f32[2,12,256]{2,1,0:T(8,128)S(1)}, f32[2,12,256,1024]{3,2,1,0:T(8,128)}) fusion(f32[2,12,256]{2,1,0:T(8,128)S(1)} %copy-done.67, f32[2,12,256,1024]{3,2,1,0:T(8,128)} %get-tuple-element.137, pred[2,256,1024]{2,1,0:T(8,128)(4,1)S(1)} %copy-done.14, bf16[2,1024,12,64]{1,3,2,0:T(8,128)(2,1)} %bitcast.213, ...), kind=kOutput, calls=%fused_computation.1 | convolution fusion | flops 836757504 | bytes 54837248 | tf_op jit(solution)/shard_map/bqhd,bkhd->bhqk/dot_general | solution.py:154
  270.5 16.9 %multiply_convert_fusion = bf16[2,12,256,1024]{3,2,1,0:T(8,128)(2,1)S(1)} fusion(f32[2,12,256,1024]{3,2,1,0:T(8,128)} %get-tuple-element.147, f32[2,12,256]{2,1,0:T(8,128)S(1)} %get-tuple-element.146, f32[2,12,256]{2,1,0:T(8,128)S(1)} %copy-done.67, f32[2,12,256,1024]{3,2,1,0:T(8,128)} %get-tuple-element.137, pred[2,256,1024]{2,1,0:T(8,128)(4,1)S(1)} %copy-done.14), kind=kLoop, calls=%fused_computation | loop fusion | flops 37748736 | bytes 63488000 | tf_op jit(solution)/shard_map/convert_element_type | solution.py:158
  307.9 21.8 %multiply_reduce_fusion.1 = (f32[2,12,256]{2,1,0:T(8,128)S(1)}, f32[2,12,256,1024]{3,2,1,0:T(8,128)}) fusion(f32[2,12,256]{2,1,0:T(8,128)S(1)} %log_add_fusion.1, f32[2,12,256,1024]{3,2,1,0:T(8,128)} %get-tuple-element.133, pred[2,256,1024]{2,1,0:T(8,128)(4,1)S(1)} %copy-done.16, bf16[2,1024,12,64]{1,3,2,0:T(8,128)(2,1)} %bitcast.211, ...), kind=kOutput, calls=%fused_computation.4 | convolution fusion | flops 836757504 | bytes 54837248 | tf_op jit(solution)/shard_map/bqhd,bkhd->bhqk/dot_general | solution.py:154
  329.8 17.1 %multiply_convert_fusion.1 = bf16[2,12,256,1024]{3,2,1,0:T(8,128)(2,1)S(1)} fusion(f32[2,12,256,1024]{3,2,1,0:T(8,128)} %get-tuple-element.149, f32[2,12,256]{2,1,0:T(8,128)S(1)} %get-tuple-element.148, f32[2,12,256]{2,1,0:T(8,128)S(1)} %log_add_fusion.1, f32[2,12,256,1024]{3,2,1,0:T(8,128)} %get-tuple-element.133, pred[2,256,1024]{2,1,0:T(8,128)(4,1)S(1)} %copy-done.16), kind=kLoop, calls=%fused_computation.3 | loop fusion | flops 37748736 | bytes 63488000 | tf_op jit(solution)/shard_map/convert_element_type | solution.py:158
  353.3 6.6 copy.65
  361.1 15.4 %fusion.6 = f32[2,12,64,1024]{3,2,1,0:T(8,128)} fusion(f32[2,12,256]{2,1,0:T(8,128)S(1)} %log_add_fusion.1, f32[2,12,256,1024]{3,2,1,0:T(8,128)} %get-tuple-element.133, pred[2,256,1024]{2,1,0:T(8,128)(4,1)S(1)} %copy-done.16, bf16[2,256,12,64]{1,0,3,2:T(2,128)(2,1)S(1)} %copy-done.59), kind=kOutput, calls=%fused_computation.17 | convolution fusion | flops 830472192 | bytes 32792576 | tf_op jit(solution)/shard_map/bhqk,bqhd->bkhd/dot_general | solution.py:168
  376.5 6.7 copy.67
  384.5 12.9 %fusion.4 = f32[2,12,64,1024]{3,2,1,0:T(8,128)} fusion(f32[2,12,256]{2,1,0:T(8,128)S(1)} %copy-done.67, f32[2,12,256,1024]{3,2,1,0:T(8,128)} %get-tuple-element.137, pred[2,256,1024]{2,1,0:T(8,128)(4,1)S(1)} %copy-done.14, bf16[2,256,12,64]{1,0,3,2:T(2,128)(2,1)S(1)} %copy-done.58), kind=kOutput, calls=%fused_computation.16 | convolution fusion | flops 830472192 | bytes 32792576 | tf_op jit(solution)/shard_map/bhqk,bqhd->bkhd/dot_general | solution.py:168
  404.5 9.6 convert_reduce_fusion.8
  416.0 9.8 convert_reduce_fusion.9
  456.3 24.7 %reduce-scatter.7.cloned.1.call-done = f32[2,256,768]{2,1,0:T(8,128)} async-done(((f32[2,1024,768]{2,1,0:T(8,128)}), f32[2,256,768]{2,1,0:T(8,128)}) %reduce-scatter.7.cloned.1.call-update) | async-done | bytes 1572880 | tf_op jit(solution)/shard_map/reduce_scatter | solution.py:178
  487.7 54.5 %reduce-scatter.11.cloned.1.call-done = f32[2,256,768]{2,1,0:T(8,128)} async-done(((f32[2,1024,768]{2,1,0:T(8,128)}), f32[2,256,768]{2,1,0:T(8,128)}) %reduce-scatter.11.cloned.1.call-update) | async-done | bytes 1572880 | tf_op jit(solution)/shard_map/reduce_scatter | solution.py:178
  567.3 42.5 %all-reduce = (f32[768]{0:T(1024)}, f32[768]{0:T(1024)}, f32[768]{0:T(1024)}, f32[768]{0:T(1024)}, f32[768]{0:T(1024)}, /*index=5*/f32[3072]{0:T(1024)}, f32[768]{0:T(1024)}, f32[768]{0:T(1024)}, f32[768]{0:T(1024)}) all-reduce(f32[768]{0:T(1024)S(1)} %copy-done.95, ...), channel_id=1, replica_groups=mesh['rows'=8,'seq'=4] {'rows','seq'}, use_global_device_ids=true, to_apply=%region_29.30 | all-reduce | flops 9216 | bytes 73728 | tf_op jit(solution)/shard_map/psum | solution.py:209
  618.6 367.3 %all-reduce.4.cloned.1.call-done = (f32[768,768]{0,1:T(8,128)}, f32[768,768]{0,1:T(8,128)}, f32[768,768]{0,1:T(8,128)}, f32[768,768]{1,0:T(8,128)}, f32[768,3072]{1,0:T(8,128)}, /*index=5*/f32[3072,768]{1,0:T(8,128)}) async-done(((f32[768,768]{0,1:T(8,128)}, f32[768,768]{0,1:T(8,128)}, f32[768,768]{0,1:T(8,128)}, f32[768,768]{1,0:T(8,128)}, f32[768,3072]{1,0:T(8,128)}, /*index=5*/f32[3072,768]{1,0:T(8,128)}), ...) | async-done | bytes 28311568 | tf_op jit(solution)/shard_map/psum | solution.py:209
  995.6 9.3 copy.115
  (422 shorter events, 229.3 us)
Async XLA Ops:
  7.2 101.1 %copy-start = (bf16[768,768]{1,0:T(8,128)(2,1)S(1)}, bf16[768,768]{1,0:T(8,128)(2,1)}, u32[]{:S(2)}) copy-start(bf16[768,768]{1,0:T(8,128)(2,1)} %param.28) | copy-start | bytes 3538948
  7.2 37.1 %all-gather.13.cloned.1.call-start = ((), (), s32[]{:S(2)}) async-start(), calls=%async_computation.7 | async-start | bytes 3932160 | tf_op jit(solution)/shard_map/all_gather | solution.py:103
  10.8 63.2 %all-gather.11.cloned.1.call-start = ((), (), s32[]{:S(2)}) async-start(), calls=%async_computation.6 | async-start | bytes 3932160 | tf_op jit(solution)/shard_map/all_gather | solution.py:104
  13.8 89.9 %all-gather.9.cloned.1.call-start = ((), (), s32[]{:S(2)}) async-start(), calls=%async_computation.5 | async-start | bytes 3932160 | tf_op jit(solution)/shard_map/all_gather | solution.py:103
  16.8 117.8 %all-gather.7.cloned.1.call-start = ((), (), s32[]{:S(2)}) async-start(), calls=%async_computation.4 | async-start | bytes 3932160 | tf_op jit(solution)/shard_map/all_gather | solution.py:104
  19.8 432.5 %reduce-scatter.9.cloned.1.call-start = ((), (), s32[]{:S(2)}) async-start(), calls=%async_computation.10 | async-start | bytes 7864320 | tf_op jit(solution)/shard_map/reduce_scatter | solution.py:175
  25.4 134.2 %copy-start.101 = (f32[3072]{0:T(1024)}, f32[3072]{0:T(1024)S(1)}, u32[]{:S(2)}) copy-start(f32[3072]{0:T(1024)S(1)} %convert_element_type.286) | copy-start | bytes 36868
  32.2 165.5 %copy-start.72 = (f32[768]{0:T(1024)}, f32[768]{0:T(1024)S(1)}, u32[]{:S(2)}) copy-start(f32[768]{0:T(1024)S(1)} %convert_element_type.284) | copy-start | bytes 9220
  44.3 95.0 %copy-start.15 = (pred[2,256,1024]{2,1,0:T(8,128)(4,1)}, pred[2,256,1024]{2,1,0:T(8,128)(4,1)S(1)}, u32[]{:S(2)}) copy-start(pred[2,256,1024]{2,1,0:T(8,128)(4,1)S(1)} %broadcast_compare_fusion.1) | copy-start | bytes 1572868
  110.8 133.8 %copy-start.5 = (f32[512,768]{1,0:T(8,128)}, f32[512,768]{1,0:T(8,128)S(1)}, u32[]{:S(2)}) copy-start(f32[512,768]{1,0:T(8,128)S(1)} %get-tuple-element.139) | copy-start | bytes 4718596
  110.8 133.8 %copy-start.74 = (f32[512]{0:T(512)}, f32[512]{0:T(512)S(1)}, u32[]{:S(2)}) copy-start(f32[512]{0:T(512)S(1)} %broadcast_multiply_fusion.3) | copy-start | bytes 6148
  111.1 133.5 %copy-start.77 = (f32[512]{0:T(512)}, f32[512]{0:T(512)S(1)}, u32[]{:S(2)}) copy-start(f32[512]{0:T(512)S(1)} %fusion.50) | copy-start | bytes 6148
  153.9 40.6 %copy-start.35 = (f32[512,768]{1,0:T(8,128)}, f32[512,768]{1,0:T(8,128)S(1)}, u32[]{:S(2)}) copy-start(f32[512,768]{1,0:T(8,128)S(1)} %get-tuple-element.135) | copy-start | bytes 4718596
  154.3 40.3 %copy-start.103 = (f32[512]{0:T(512)}, f32[512]{0:T(512)S(1)}, u32[]{:S(2)}) copy-start(f32[512]{0:T(512)S(1)} %fusion.48) | copy-start | bytes 6148
  154.3 40.3 %slice-start.3 = ((s8[4718592]{0:T(1024)(128)(4,1)}), s8[4194304]{0:T(1024)(128)(4,1)S(1)}, s32[]{:S(2)}) async-start(s8[4718592]{0:T(1024)(128)(4,1)} %bitcast.252), calls=%async_computation.16 | async-start | bytes 8388608
  159.7 34.8 %copy-start.125 = (f32[512,3072]{1,0:T(8,128)}, f32[512,3072]{1,0:T(8,128)S(1)}, u32[]{:S(2)}) copy-start(f32[512,3072]{1,0:T(8,128)S(1)} %fusion.61) | copy-start | bytes 18874372
  159.7 34.9 %copy-start.111 = (f32[768]{0:T(1024)S(1)}, f32[768]{0:T(1024)}, u32[]{:S(2)}) copy-start(f32[768]{0:T(1024)} %convert_element_type.288) | copy-start | bytes 9220
  159.7 34.9 %slice-start.4 = ((s8[4718592]{0:T(1024)(128)(4,1)}), s8[524288]{0:T(1024)(128)(4,1)S(1)}, s32[]{:S(2)}) async-start(s8[4718592]{0:T(1024)(128)(4,1)} %bitcast.252), calls=%async_computation.17 | async-start | bytes 1048576
  300.4 154.3 %reduce-scatter.5.cloned.1.call-start = ((), (), s32[]{:S(2)}) async-start(), calls=%async_computation.8 | async-start | bytes 7864320 | tf_op jit(solution)/shard_map/reduce_scatter | solution.py:175
  360.0 121.1 %reduce-scatter.7.cloned.1.call-start = ((), (), s32[]{:S(2)}) async-start(), calls=%async_computation.9 | async-start | bytes 7864320 | tf_op jit(solution)/shard_map/reduce_scatter | solution.py:178
  383.2 158.9 %reduce-scatter.11.cloned.1.call-start = ((), (), s32[]{:S(2)}) async-start(), calls=%async_computation.11 | async-start | bytes 7864320 | tf_op jit(solution)/shard_map/reduce_scatter | solution.py:178
  404.0 581.9 %all-reduce.4.cloned.1.call-start = ((), (), s32[]{:S(2)}) async-start(), calls=%async_computation.12 | async-start | bytes 56623104 | tf_op jit(solution)/shard_map/psum | solution.py:209
  563.1 46.6 %copy-start.48 = (bf16[2,256,768]{2,1,0:T(8,128)(2,1)S(1)}, bf16[2,256,768]{2,1,0:T(8,128)(2,1)}, u32[]{:S(2)}) copy-start(bf16[2,256,768]{2,1,0:T(8,128)(2,1)} %convert_element_type.332) | copy-start | bytes 2359300
  565.2 46.9 %copy-start.39 = (bf16[2,256,768]{2,1,0:T(8,128)(2,1)S(1)}, bf16[2,256,768]{2,1,0:T(8,128)(2,1)}, u32[]{:S(2)}) copy-start(bf16[2,256,768]{2,1,0:T(8,128)(2,1)} %copy-done.38) | copy-start | bytes 2359300
  (120 other events, 647.8 us)
Sparse Core Ops, SparseCore 0:
  10.9 31.3 all-gather.12
  44.4 28.5 all-gather.10
  75.1 28.5 all-gather.8
  105.7 28.5 all-gather.6
  300.6 58.5 reduce-scatter.8
  361.7 58.3 reduce-scatter.4
  422.6 58.3 reduce-scatter.6
  483.8 58.3 reduce-scatter.10
  549.7 436.0 all-reduce.3
where the time goes:
time: 1020 us
  waiting for transfers between devices  456 us (45%)
  matrix products  293 us (29%)
  local copies, waits for them, and re-layouts  101 us (10%)
  other arithmetic  94.8 us (9%)
  blocking collectives  54.6 us (5%)
  between operations  15.7 us (2%)
    psum x1, waiting for transfers between devices, body(): totals = lax.psum(totals, ('rows', 'seq'))  367 us
    reduce_scatter x2, waiting for transfers between devices, body(): lax.psum_scatter(d_values_all.reshape(rows_here, -1, width), 'seq', scatt...  79.2 us
    dot_general x12, matrix products, right_dot(): lax.dot_general(first, second, (((1,), (1,)), ((), ())), preferred_elemen...  48.1 us
    unnamed x282, local copies, waits for them, and re-layouts  43.7 us
    psum x1, blocking collectives, body(): totals = lax.psum(totals, ('rows', 'seq'))  42.5 us
    dot_general x2, matrix products, body(): jnp.einsum('bqhd,bkhd->bhqk', d_mixed_heads, value_heads, preferred_eleme...  41.4 us
    dot_general x2, matrix products, body(): jnp.dot(normed_low, expand_proj, preferred_element_type=jnp.float32)  40.1 us
    convert_element_type x2, other arithmetic, body(): d_scores = (probs * (d_probs - correction)).astype(jnp.bfloat16)  34 us
  transfers between devices with their start and end apart: 9, of which 4 were waited for; matrix products, arithmetic and copies ran while one was open for 27% of the time, Pallas kernels for 0%

commit v1 on v0

v1 whole, which is shorter than its diff:
```python
import functools

import jax
import jax.numpy as jnp
from jax import lax
from jax.experimental import pallas as pl
from jax.experimental.pallas import tpu as pltpu
from jax.sharding import PartitionSpec as P

DH = 64
PAIR = 128
MASKED = 1e30
F32 = jnp.float32
BF16 = jnp.bfloat16
NT = (((1,), (1,)), ((), ()))
NN = (((1,), (0,)), ((), ()))


def left_dot(first, second):
    return lax.dot_general(first, second, (((0,), (0,)), ((), ())), preferred_element_type=F32)


def right_dot(first, second):
    return lax.dot_general(first, second, NT, preferred_element_type=F32)


def layer_norm(values, gain, shift):
    centred = values - jnp.mean(values, -1, keepdims=True)
    spread = jnp.mean(centred * centred, -1, keepdims=True)
    return gain * centred * lax.rsqrt(spread + 1e-06) + shift


def gelu_exact(values):
    return jax.nn.gelu(values, approximate=False)


def column_sum(values):
    return jnp.sum(values.astype(F32), 0)


def split_three(values):
    high = values.astype(BF16)
    rest = values - high.astype(F32)
    middle = rest.astype(BF16)
    low = (rest - middle.astype(F32)).astype(BF16)
    return high.astype(F32), middle.astype(F32), low.astype(F32)


def own_lanes(shape, head):
    lane = lax.broadcasted_iota(jnp.int32, shape, 1)
    own = lane < DH if head == 0 else lane >= DH
    return own, lane % DH


def key_features(lane, seg):
    return jnp.where(
        lane < 3,
        1.0,
        jnp.where(lane == 3, -MASKED * (1.0 - seg), jnp.where(lane == 4, -MASKED * seg, 0.0)),
    ).astype(BF16)


def forward_kernel(q_ref, k_ref, v_ref, seg_q_ref, seg_k_ref, mixed_ref, query_ref, *, block):
    queries = q_ref.shape[0]
    keys = k_ref.shape[0]
    for head in range(2):
        own_k, lane_k = own_lanes((keys, PAIR), head)
        key_side = jnp.where(own_k, k_ref[...], key_features(lane_k, seg_k_ref[...].astype(F32)))
        value_side = jnp.where(own_k, v_ref[...], jnp.ones((), BF16))
        own_q, lane_q = own_lanes((block, PAIR), head)
        for start in range(0, queries, block):
            here = slice(start, start + block)
            q = q_ref[here, :]
            seg = seg_q_ref[here, :].astype(F32)
            seg_side = jnp.where(lane_q == 3, seg, jnp.where(lane_q == 4, 1.0 - seg, 0.0))
            query_side = jnp.where(own_q, q, seg_side.astype(BF16))
            scores = lax.dot_general(query_side, key_side, NT, preferred_element_type=F32)
            peak = jnp.max(scores, -1, keepdims=True)
            raised = jnp.exp(scores - peak).astype(BF16)
            summed = lax.dot_general(raised, value_side, NN, preferred_element_type=F32)
            total = summed[:, DH : DH + 1] if head == 0 else summed[:, 0:1]
            mixed = (summed / total).astype(BF16)
            shift = jnp.broadcast_to(-(peak + jnp.log(total)), (block, PAIR))
            high, middle, low = split_three(shift)
            extra = jnp.where(
                lane_q == 0,
                high,
                jnp.where(lane_q == 1, middle, jnp.where(lane_q == 2, low, seg_side)),
            )
            query_ref[head, here, :] = jnp.where(own_q, q, extra.astype(BF16))
            if head == 0:
                mixed_ref[here, :] = mixed
            else:
                mixed_ref[here, :] = jnp.where(own_q, mixed, mixed_ref[here, :])


def attention_forward(q, k, v, seg_q, seg_k):
    queries, width = q.shape
    keys = k.shape[0]
    pairs = width // PAIR
    column = lambda i: (0, i)
    whole = lambda i: (0, 0)
    return pl.pallas_call(
        functools.partial(forward_kernel, block=min(512, queries)),
        grid=(pairs,),
        in_specs=[
            pl.BlockSpec((queries, PAIR), column),
            pl.BlockSpec((keys, PAIR), column),
            pl.BlockSpec((keys, PAIR), column),
            pl.BlockSpec((queries, PAIR), whole),
            pl.BlockSpec((keys, PAIR), whole),
        ],
        out_specs=[
            pl.BlockSpec((queries, PAIR), column),
            pl.BlockSpec((2, queries, PAIR), lambda i: (i, 0, 0)),
        ],
        out_shape=[
            jax.ShapeDtypeStruct((queries, width), BF16),
            jax.ShapeDtypeStruct((2 * pairs, queries, PAIR), BF16),
        ],
        compiler_params=pltpu.CompilerParams(vmem_limit_bytes=40 * 2**20),
        cost_estimate=pl.CostEstimate(
            flops=16 * queries * keys * width,
            bytes_accessed=10 * queries * width,
            transcendentals=2 * pairs * queries * keys,
        ),
        name="attention_forward",
    )(q, k, v, seg_q, seg_k)


def backward_kernel(
    query_ref, k_ref, v_ref, seg_k_ref, mixed_ref, d_mixed_ref, dq_ref, dk_ref, dv_ref, dqt, *, block
):
    queries = mixed_ref.shape[0]
    keys = k_ref.shape[0]
    d_mixed = d_mixed_ref[...]
    product = d_mixed.astype(F32) * mixed_ref[...].astype(F32)
    for head in range(2):
        own_q, lane_q = own_lanes((queries, PAIR), head)
        own_k, lane_k = own_lanes((block, PAIR), head)
        delta = -jnp.sum(jnp.where(own_q, product, 0.0), -1, keepdims=True)
        high, middle, low = split_three(jnp.broadcast_to(delta, (queries, PAIR)))
        extra = jnp.where(
            lane_q == 0, high, jnp.where(lane_q == 1, middle, jnp.where(lane_q == 2, low, 0.0))
        )
        d_side = jnp.where(own_q, d_mixed, extra.astype(BF16))
        query_side = query_ref[head]
        ones = jnp.where(lane_k < 3, 1.0, 0.0).astype(BF16)
        for start in range(0, keys, block):
            here = slice(start, start + block)
            k = k_ref[here, :]
            seg = seg_k_ref[here, :].astype(F32)
            key_side = jnp.where(own_k, k, key_features(lane_k, seg))
            value_side = jnp.where(own_k, v_ref[here, :], ones)
            shifted = lax.dot_general(key_side, query_side, NT, preferred_element_type=F32)
            probs = jnp.exp(shifted)
            d_probs = lax.dot_general(value_side, d_side, NT, preferred_element_type=F32)
            d_scores = (probs * d_probs).astype(BF16)
            dv = lax.dot_general(probs.astype(BF16), d_mixed, NN, preferred_element_type=F32)
            dk = lax.dot_general(d_scores, query_side, NN, preferred_element_type=F32)
            turned = k.T[head * DH : (head + 1) * DH, :]
            dq = lax.dot_general(turned, d_scores, NN, preferred_element_type=F32)
            mine = slice(head * DH, (head + 1) * DH)
            if start == 0:
                dqt[mine, :] = dq
            else:
                dqt[mine, :] += dq
            dv = dv.astype(dv_ref.dtype)
            dk = dk.astype(dk_ref.dtype)
            if head == 0:
                dk_ref[here, :] = dk
                dv_ref[here, :] = dv
            else:
                dk_ref[here, :] = jnp.where(own_k, dk, dk_ref[here, :])
                dv_ref[here, :] = jnp.where(own_k, dv, dv_ref[here, :])
    dq_ref[...] = (dqt[...] * 0.125).astype(BF16).T


def attention_backward(query_side, k, v, seg_k, mixed, d_mixed, kept):
    queries, width = mixed.shape
    keys = k.shape[0]
    pairs = width // PAIR
    column = lambda i: (0, i)
    return pl.pallas_call(
        functools.partial(backward_kernel, block=min(512, keys)),
        grid=(pairs,),
        in_specs=[
            pl.BlockSpec((2, queries, PAIR), lambda i: (i, 0, 0)),
            pl.BlockSpec((keys, PAIR), column),
            pl.BlockSpec((keys, PAIR), column),
            pl.BlockSpec((keys, PAIR), lambda i: (0, 0)),
            pl.BlockSpec((queries, PAIR), column),
            pl.BlockSpec((queries, PAIR), column),
        ],
        out_specs=[
            pl.BlockSpec((queries, PAIR), column),
            pl.BlockSpec((keys, PAIR), column),
            pl.BlockSpec((keys, PAIR), column),
        ],
        out_shape=[
            jax.ShapeDtypeStruct((queries, width), BF16),
            jax.ShapeDtypeStruct((keys, width), kept),
            jax.ShapeDtypeStruct((keys, width), kept),
        ],
        scratch_shapes=[pltpu.VMEM((PAIR, queries), F32)],
        compiler_params=pltpu.CompilerParams(vmem_limit_bytes=40 * 2**20),
        cost_estimate=pl.CostEstimate(
            flops=40 * queries * keys * width,
            bytes_accessed=14 * queries * width,
            transcendentals=2 * pairs * queries * keys,
        ),
        name="attention_backward",
    )(query_side, k, v, seg_k, mixed, d_mixed)


def swap(values, axis, size, bit):
    return lax.ppermute(values, axis, [(i, i ^ (1 << bit)) for i in range(size)])


def bit_of(axis, bit):
    return (lax.axis_index(axis) >> bit) & 1


def half_of(values, which):
    count = values.shape[0] // 2
    return lax.dynamic_slice_in_dim(values, which * count, count, 0)


def scatter_sum(values, stages):
    for axis, size, bit in stages:
        mine = bit_of(axis, bit)
        got = swap(half_of(values, 1 - mine), axis, size, bit)
        values = (half_of(values, mine).astype(F32) + got.astype(F32)).astype(BF16)
    return values


def gather_back(values, stages):
    for axis, size, bit in reversed(stages):
        mine = bit_of(axis, bit)
        got = swap(values, axis, size, bit)
        values = jnp.concatenate(
            [jnp.where(mine == 0, values, got), jnp.where(mine == 0, got, values)], 0
        )
    return values


def solution(mesh):
    seq_size = mesh.shape["seq"]
    rows_size = mesh.shape["rows"]
    seq_bits = seq_size.bit_length() - 1
    rows_bits = rows_size.bit_length() - 1
    x_stages = [("seq", seq_size, bit) for bit in range(1, seq_bits)]
    yz_stages = [("rows", rows_size, bit) for bit in range(rows_bits)]

    def all_sum(half, stages, axis):
        core = bit_of("seq", 0)
        got = swap(half(1 - core).astype(BF16), "seq", seq_size, 0)
        mine = (half(core) + got.astype(F32)).astype(BF16)
        mine = gather_back(scatter_sum(mine, stages), stages)
        got = swap(mine, "seq", seq_size, 0)
        return jnp.concatenate(
            [jnp.where(core == 0, mine, got), jnp.where(core == 0, got, mine)], axis
        ).astype(F32)

    def small_sum(values):
        for axis, size, bit in [("seq", seq_size, 0)] + x_stages + yz_stages:
            values = values + swap(values, axis, size, bit)
        return values

    def body(
        hidden_in,
        segments,
        grad_mask,
        grad_out,
        query_proj,
        query_bias,
        key_proj,
        value_proj,
        value_bias,
        output_proj,
        output_bias,
        first_gain,
        first_shift,
        expand_proj,
        expand_bias,
        shrink_proj,
        shrink_bias,
        second_gain,
        second_shift,
    ):
        micro, rows_here, piece, width = hidden_in.shape
        units = expand_proj.shape[1]
        held = micro * rows_here
        sharers = seq_size // held
        tokens = held * piece
        place = lax.axis_index("seq")
        source_at = place % held
        row_at = place // sharers

        def trade(to_rows, part):
            there = [(s, (s % held ^ part) * sharers + s // held) for s in range(seq_size)]
            return there if to_rows else [(b, a) for a, b in there]

        def to_rows(values):
            flat = values.reshape((held,) + values.shape[2:])
            parts = []
            for part in range(held):
                sent = lax.dynamic_index_in_dim(flat, source_at ^ part, 0, False)
                parts.append(lax.ppermute(sent, "seq", trade(True, part)))
            return jnp.concatenate(parts, 0)

        def to_pieces(values):
            back = jnp.zeros((held, piece) + values.shape[1:], values.dtype)
            for part in range(held):
                sent = values[part * piece : (part + 1) * piece]
                got = lax.ppermute(sent, "seq", trade(False, part))
                back = lax.dynamic_update_index_in_dim(back, got, source_at ^ part, 0)
            return back.reshape((micro, rows_here, piece) + values.shape[1:])

        same_row = [[r * sharers + g for g in range(sharers)] for r in range(held)]

        def all_keys(values):
            if sharers == 1:
                return values
            return lax.all_gather(values, "seq", axis=0, tiled=True, axis_index_groups=same_row)

        def own_keys(values):
            if sharers == 1:
                return values
            return lax.psum_scatter(
                values, "seq", scatter_dimension=0, tiled=True, axis_index_groups=same_row
            ).astype(BF16)

        query_add = query_bias.astype(F32)
        value_add = value_bias.astype(F32)
        output_add = output_bias.astype(F32)
        expand_add = expand_bias.astype(F32)
        shrink_add = shrink_bias.astype(F32)
        gain_one = first_gain.astype(F32)
        shift_one = first_shift.astype(F32)
        gain_two = second_gain.astype(F32)
        shift_two = second_shift.astype(F32)

        inputs = to_rows(hidden_in)
        seg = to_rows(segments)
        upstream = to_rows(grad_out * grad_mask[..., None].astype(BF16)).astype(F32)

        queries = ((jnp.dot(inputs, query_proj, preferred_element_type=F32) + query_add) * 0.125).astype(BF16)
        keys = all_keys(jnp.dot(inputs, key_proj, preferred_element_type=F32).astype(BF16))
        values = all_keys(
            (jnp.dot(inputs, value_proj, preferred_element_type=F32) + value_add).astype(BF16)
        )
        seg_q = jnp.broadcast_to(seg[:, None].astype(BF16), (tokens, PAIR))
        seg_k = all_keys(seg_q)
        mixed, query_side = attention_forward(queries, keys, values, seg_q, seg_k)
        first_sum = (
            inputs.astype(F32) + jnp.dot(mixed, output_proj, preferred_element_type=F32) + output_add
        )
        normed, first_back = jax.vjp(layer_norm, first_sum, gain_one, shift_one)
        normed_low = normed.astype(BF16)
        expanded = jnp.dot(normed_low, expand_proj, preferred_element_type=F32) + expand_add
        activated, gelu_back = jax.vjp(gelu_exact, expanded)
        active_low = activated.astype(BF16)
        second_sum = (
            normed + jnp.dot(active_low, shrink_proj, preferred_element_type=F32) + shrink_add
        )
        result, second_back = jax.vjp(layer_norm, second_sum, gain_two, shift_two)
        layer_out = to_pieces(result.astype(BF16))

        d_second, d_gain_two, d_shift_two = second_back(upstream)
        d_down = d_second.astype(BF16)

        def column_half(first, second):
            count = second.shape[1] // 2
            return lambda which: left_dot(
                first, lax.dynamic_slice_in_dim(second, which * count, count, 1)
            )

        def row_half(first, second):
            count = first.shape[1] // 2
            return lambda which: left_dot(
                lax.dynamic_slice_in_dim(first, which * count, count, 1), second
            )

        shrink_grad = all_sum(row_half(active_low, d_down), yz_stages + x_stages, 0)
        d_active = right_dot(d_down, shrink_proj)
        (d_expand,) = gelu_back(d_active)
        d_expand_low = d_expand.astype(BF16)
        expand_grad = all_sum(
            column_half(normed_low, d_expand_low), x_stages + yz_stages, 1
        )
        d_normed = d_second + right_dot(d_expand_low, expand_proj)
        d_first, d_gain_one, d_shift_one = first_back(d_normed)
        d_attn = d_first.astype(BF16)
        d_mixed = right_dot(d_attn, output_proj).astype(BF16)
        output_grad = all_sum(column_half(mixed, d_attn), yz_stages + x_stages, 1)
        d_query, d_keys, d_values = attention_backward(
            query_side, keys, values, seg_k, mixed, d_mixed, BF16 if sharers == 1 else F32
        )
        d_key = own_keys(d_keys)
        d_value = own_keys(d_values)
        d_input = (
            d_first
            + right_dot(d_query, query_proj)
            + right_dot(d_key, key_proj)
            + right_dot(d_value, value_proj)
        )
        grad_in = to_pieces(d_input.astype(BF16))

        def input_half(which):
            return jnp.concatenate(
                [column_half(inputs, d)(which) for d in (d_query, d_key, d_value)], 0
            )

        input_grad = all_sum(input_half, yz_stages + x_stages, 1)
        small = [
            column_sum(d_query),
            column_sum(d_value),
            column_sum(d_attn),
            d_gain_one,
            d_shift_one,
            column_sum(d_expand_low),
            column_sum(d_down),
            d_gain_two,
            d_shift_two,
        ]
        totals = small_sum(jnp.concatenate(small).reshape(-1, width)).reshape(-1)
        vectors = []
        at = 0
        for part in small:
            vectors.append(totals[at : at + part.shape[0]])
            at += part.shape[0]
        return (
            layer_out,
            grad_in,
            input_grad[:width],
            vectors[0],
            input_grad[width : 2 * width],
            input_grad[2 * width :],
            vectors[1],
            output_grad,
            vectors[2],
            vectors[3],
            vectors[4],
            expand_grad,
            vectors[5],
            shrink_grad,
            vectors[6],
            vectors[7],
            vectors[8],
        )

    split = P(None, "rows", "seq", None)
    whole = P()
    return jax.shard_map(
        body,
        mesh=mesh,
        in_specs=(split, P(None, "rows", "seq"), P(None, "rows", "seq"), split) + (whole,) * 15,
        out_specs=(split, split) + (whole,) * 15,
        check_vma=False,
    )
```

time: 1020 us -> 533 us (0.52)
  waiting for transfers between devices: 456 us -> 168 us
  matrix products: 293 us -> 123 us
  starting transfers between devices: 0.84 us -> 77.3 us
  Pallas kernels: 0 us -> 57.5 us
  local copies, waits for them, and re-layouts: 101 us -> 45.6 us
  blocking collectives: 54.6 us -> 0 us
  other arithmetic: 94.8 us -> 49.2 us
  between operations: 15.7 us -> 2.76 us
    psum x1 -> x0, waiting for transfers between devices: 367 us -> none  [body(): totals = lax.psum(totals, ('rows', 'seq'))]
    dot_general x36 -> x12, matrix products: 262 us -> 93.1 us  [the longest x6 42.6 us: right_dot(): return lax.dot_general(first, second, NT, preferred_element_type=F32)]
    ppermute x0 -> x65, waiting for transfers between devices: none -> 168 us  [the longest x45 166 us: swap(): return lax.ppermute(values, axis, [(i, i ^ 1 << bit) for i in range(size)])]
    reduce_scatter x4 -> x0, waiting for transfers between devices: 79.2 us -> none  [the longest x2 79.2 us: body(): lax.psum_scatter(d_values_all.reshape(rows_here, -1, width), 'seq', scatt...]
    ppermute x0 -> x65, starting transfers between devices: none -> 77.3 us  [the longest x45 54.3 us: swap(): return lax.ppermute(values, axis, [(i, i ^ 1 << bit) for i in range(size)])]
    pallas_call x0 -> x2, Pallas kernels: none -> 57.5 us  [the longest x1 35.9 us: attention_backward(): pl.pallas_call(functools.partial(backward_kernel, block=min(512, keys)),...]
    psum x1 -> x0, blocking collectives: 42.5 us -> none  [body(): totals = lax.psum(totals, ('rows', 'seq'))]
    reshape x8 -> x2, local copies, waits for them, and re-layouts: 29 us -> 0.02 us  [the longest x1 0.01 us: to_rows(): flat = values.reshape((held,) + values.shape[2:])]
  transfers between devices with their start and end apart: 9 -> 65, of which waited for: 4 -> 28; matrix products, arithmetic and copies ran while one was open for 27% -> 26% of each run, Pallas kernels for 0% -> 4%
where the time goes in v1:
time: 533 us; the launch traced here: 524 us
  waiting for transfers between devices  168 us (32%)
  matrix products  123 us (23%)
  starting transfers between devices  77.3 us (15%)
  Pallas kernels  57.5 us (11%)
  other arithmetic  49.2 us (9%)
  local copies, waits for them, and re-layouts  45.6 us (9%)
    ppermute x45, waiting for transfers between devices, swap(): return lax.ppermute(values, axis, [(i, i ^ 1 << bit) for i in range(size)])  166 us
    ppermute x45, starting transfers between devices, swap(): return lax.ppermute(values, axis, [(i, i ^ 1 << bit) for i in range(size)])  54.3 us
    dot_general x6, matrix products, right_dot(): return lax.dot_general(first, second, NT, preferred_element_type=F32)  42.6 us
    dot_general x1, matrix products, body(): jnp.dot(normed_low, expand_proj, preferred_element_type=F32) + expand_add  36.8 us
    pallas_call x1, Pallas kernels, attention_backward(): pl.pallas_call(functools.partial(backward_kernel, block=min(512, keys)),...  35.9 us
    dot_general x12, matrix products, left_dot(): lax.dot_general(first, second, (((0,), (0,)), ((), ())), preferred_elemen...  29.7 us
    pallas_call x1, Pallas kernels, attention_forward(): pl.pallas_call(functools.partial(forward_kernel, block=min(512, queries))...  21.6 us
    unnamed x149, local copies, waits for them, and re-layouts  17.9 us
  transfers between devices with their start and end apart: 65, of which 28 were waited for; matrix products, arithmetic and copies ran while one was open for 26% of the time, Pallas kernels for 4%

profile of v1, /device:TPU:0, one launch (start us, length us, event | category | flops | bytes accessed | tf_op | source)
XLA Modules:
  0.0 523.6 jit_solution(3918093642370587703)
XLA Ops:
  51.2 21.6 %attention_forward.1 = (bf16[1024,768]{1,0:T(8,128)(2,1)S(1)}, bf16[12,1024,128]{2,1,0:T(8,128)(2,1)S(1)}) custom-call(bf16[1024,768]{1,0:T(8,128)(2,1)S(1)} %multiply_convert_fusion.1.q_ref, bf16[1024,768]{1,0:T(8,128)(2,1)S(1)} %convolution_convert_fusion.3.k_ref, bf16[1024,768]{1,0:T(8,128)(2,1)S(1)} %add_convert_fusion.5.v_ref, ...), custom_call_target="tpu_custom_call" | custom-call | flops 12884901888 | bytes 7864320 | tf_op jit(solution)/shard_map/attention_forward/pallas_call | solution.py:103
  77.0 36.8 %multiply_convert_fusion = (bf16[1024,3072]{1,0:T(8,128)(2,1)}, f32[1024,3072]{1,0:T(8,128)}, f32[1024,3072]{1,0:T(8,128)}) fusion(f32[3072]{0:T(1024)S(1)} %copy-done.47, bf16[1024,768]{0,1:T(8,128)(2,1)S(1)} %fusion.21, bf16[768,3072]{1,0:T(8,128)(2,1)} %param.32), kind=kOutput, calls=%fused_computation.4 | convolution fusion | flops 5039456256 | bytes 37761024 | tf_op jit(solution)/shard_map/dot_general | solution.py:361
  113.9 7.7 %fusion.57 = (f32[1024]{0:T(1024)S(1)}, f32[1024,768]{0,1:T(8,128)S(1)}) fusion(f32[768]{0:T(1024)S(1)} %copy-done.49, bf16[1024,3072]{1,0:T(8,128)(2,1)} %get-tuple-element.49, bf16[3072,768]{1,0:T(8,128)(2,1)S(1)} %bitcast.76, f32[768]{0:T(1024)S(1)} %convert_element_type.290, f32[1024]{0:T(1024)S(1)} %fusion.48, f32[1024,768]{0,1:T(8,128)S(1)} %get-tuple-element.52, ...), kind=kOutput, calls=%fused_computation.242 | convolution fusion | flops 4837342208 | bytes 17323008 | tf_op jit(solution)/shard_map/dot_general | solution.py:365
  132.1 17.5 %convert_reduce_fusion = (f32[3072]{0:T(1024)S(1)}, bf16[1024,3072]{1,0:T(8,128)(2,1)}) fusion(f32[1024,3072]{1,0:T(8,128)} %get-tuple-element.50, bf16[1024,768]{0,1:T(8,128)(2,1)S(1)} %get-tuple-element.44, bf16[3072,768]{1,0:T(8,128)(2,1)} %param.34, f32[1024,3072]{1,0:T(8,128)} %get-tuple-element.119, f32[3072]{0:T(1024)S(1)} %copy-done.47), kind=kOutput, calls=%fused_computation.2 | convolution fusion | flops 4885312512 | bytes 37773312 | tf_op jit(solution)/shard_map/dot_general | solution.py:24
  149.6 11.6 %multiply_reduce_fusion = (f32[768]{0:T(1024)S(1)}, f32[1024]{0:T(1024)S(1)}, f32[768]{0:T(1024)S(1)}, f32[1024,768]{0,1:T(8,128)S(1)}) fusion(f32[1024,768]{0,1:T(8,128)} %copy-done.14, f32[1024]{0:T(1024)S(1)} %fusion.48, f32[1024]{0:T(1024)S(1)} %broadcast_multiply_fusion.2, f32[768]{0:T(1024)S(1)} %convert_element_type.282, ...), kind=kOutput, calls=%fused_computation.43 | convolution fusion | flops 4850709504 | bytes 22061056 | tf_op jit(solution)/shard_map/dot_general | solution.py:24
  166.8 35.9 %attention_backward.1 = (bf16[1024,768]{1,0:T(8,128)(2,1)S(1)}, bf16[1024,768]{1,0:T(8,128)(2,1)S(1)}, bf16[1024,768]{1,0:T(8,128)(2,1)S(1)}) custom-call(bf16[12,1024,128]{2,1,0:T(8,128)(2,1)S(1)} %get-tuple-element.23.query_ref, bf16[1024,768]{1,0:T(8,128)(2,1)S(1)} %copy-done.11, bf16[1024,768]{1,0:T(8,128)(2,1)S(1)} %copy-done.13, ...), custom_call_target="tpu_custom_call" | custom-call | flops 32212254720 | bytes 11010048 | tf_op jit(solution)/shard_map/attention_backward/pallas_call | solution.py:184
  231.4 5.7 %add_convert_fusion.3 = bf16[1024,768]{0,1:T(8,128)(2,1)S(1)} fusion(f32[1024,768]{0,1:T(8,128)} %fusion.59, f32[1024,768]{0,1:T(8,128)} %fusion.58, f32[1024,768]{0,1:T(8,128)} %copy-done.17, bf16[1024,768]{1,0:T(8,128)(2,1)S(1)} %get-tuple-element.26, bf16[768,768]{1,0:T(8,128)(2,1)} %param.26, f32[1024]{0:T(1024)S(1)} %negate_multiply_fusion.1), kind=kOutput, calls=%fused_computation.47 | convolution fusion | flops 1211891712 | bytes 13766656 | tf_op jit(solution)/shard_map/dot_general | solution.py:24
  290.5 8.5 %collective-permute-done.40 = bf16[48,384]{1,0:T(8,128)(2,1)S(1)} collective-permute-done((bf16[48,384]{1,0:T(8,128)(2,1)S(1)}, bf16[48,384]{1,0:T(8,128)(2,1)S(1)}, u32[]{:S(2)}, u32[]{:S(2)}) %collective-permute-start.40) | collective-permute-done | bytes 36896 | tf_op jit(solution)/shard_map/ppermute | solution.py:217
  323.5 17.1 %collective-permute-done.43 = bf16[384,384]{1,0:T(8,128)(2,1)} collective-permute-done((bf16[384,384]{1,0:T(8,128)(2,1)}, bf16[384,384]{1,0:T(8,128)(2,1)}, u32[]{:S(2)}, u32[]{:S(2)}) %collective-permute-start.43) | collective-permute-done | bytes 294944 | tf_op jit(solution)/shard_map/ppermute | solution.py:217
  344.0 5.3 %add_convert_fusion.2 = bf16[768,1536]{1,0:T(8,128)(2,1)S(1)} fusion(bf16[768,1536]{1,0:T(8,128)(2,1)} %collective-permute-done.45, bf16[1024,768]{0,1:T(8,128)(2,1)S(1)} %copy-done.25, bf16[1024,3072]{1,0:T(8,128)(2,1)} %get-tuple-element.124, s32[]{:T(128)S(6)} %select_n.452), kind=kOutput, calls=%fused_computation.26 | convolution fusion | flops 2419458048 | bytes 9437188 | tf_op jit(solution)/shard_map/dot_general | solution.py:20
  357.2 5.3 %add_convert_fusion.1 = bf16[1536,768]{1,0:T(8,128)(2,1)S(1)} fusion(bf16[1536,768]{1,0:T(8,128)(2,1)} %collective-permute-done.55, bf16[1024,768]{0,1:T(8,128)(2,1)S(1)} %copy-done.28, bf16[1024,3072]{1,0:T(8,128)(2,1)} %get-tuple-element.49, s32[]{:T(128)S(6)} %select_n.452), kind=kOutput, calls=%fused_computation.25 | convolution fusion | flops 2419458048 | bytes 9437188 | tf_op jit(solution)/shard_map/dot_general | solution.py:20
  368.6 9.6 %collective-permute-done.24 = bf16[144,384]{1,0:T(8,128)(2,1)S(1)} collective-permute-done((bf16[144,384]{1,0:T(8,128)(2,1)S(1)}, bf16[144,384]{1,0:T(8,128)(2,1)S(1)}, u32[]{:S(2)}, u32[]{:S(2)}) %collective-permute-start.24) | collective-permute-done | bytes 110624 | tf_op jit(solution)/shard_map/ppermute | solution.py:217
  388.7 7.0 %collective-permute-done.56 = bf16[768,768]{1,0:T(8,128)(2,1)S(1)} collective-permute-done((bf16[768,768]{1,0:T(8,128)(2,1)S(1)}, bf16[768,768]{1,0:T(8,128)(2,1)S(1)}, u32[]{:S(2)}, u32[]{:S(2)}) %collective-permute-start.56) | collective-permute-done | bytes 1179680 | tf_op jit(solution)/shard_map/ppermute | solution.py:217
  398.3 8.1 %collective-permute-done.47 = bf16[192,1536]{1,0:T(8,128)(2,1)S(1)} collective-permute-done((bf16[192,1536]{1,0:T(8,128)(2,1)S(1)}, bf16[192,1536]{1,0:T(8,128)(2,1)S(1)}, u32[]{:S(2)}, u32[]{:S(2)}) %collective-permute-start.47) | collective-permute-done | bytes 589856 | tf_op jit(solution)/shard_map/ppermute | solution.py:217
  406.7 8.8 %collective-permute-done.57 = bf16[384,768]{1,0:T(8,128)(2,1)S(1)} collective-permute-done((bf16[384,768]{1,0:T(8,128)(2,1)S(1)}, bf16[384,768]{1,0:T(8,128)(2,1)S(1)}, u32[]{:S(2)}, u32[]{:S(2)}) %collective-permute-start.57) | collective-permute-done | bytes 589856 | tf_op jit(solution)/shard_map/ppermute | solution.py:217
  416.6 10.1 %collective-permute-done.27 = bf16[576,384]{1,0:T(8,128)(2,1)S(1)} collective-permute-done((bf16[576,384]{1,0:T(8,128)(2,1)S(1)}, bf16[576,384]{1,0:T(8,128)(2,1)S(1)}, u32[]{:S(2)}, u32[]{:S(2)}) %collective-permute-start.27) | collective-permute-done | bytes 442400 | tf_op jit(solution)/shard_map/ppermute | solution.py:217
  432.6 8.2 %collective-permute-done.49 = bf16[48,1536]{1,0:T(8,128)(2,1)S(1)} collective-permute-done((bf16[48,1536]{1,0:T(8,128)(2,1)S(1)}, bf16[48,1536]{1,0:T(8,128)(2,1)S(1)}, u32[]{:S(2)}, u32[]{:S(2)}) %collective-permute-start.49) | collective-permute-done | bytes 147488 | tf_op jit(solution)/shard_map/ppermute | solution.py:217
  442.3 10.2 %collective-permute-done.50 = bf16[48,1536]{1,0:T(8,128)(2,1)S(1)} collective-permute-done((bf16[48,1536]{1,0:T(8,128)(2,1)S(1)}, bf16[48,1536]{1,0:T(8,128)(2,1)S(1)}, u32[]{:S(2)}, u32[]{:S(2)}) %collective-permute-start.50) | collective-permute-done | bytes 147488 | tf_op jit(solution)/shard_map/ppermute | solution.py:217
  455.2 10.3 %collective-permute-done.51 = bf16[96,1536]{1,0:T(8,128)(2,1)S(1)} collective-permute-done((bf16[96,1536]{1,0:T(8,128)(2,1)S(1)}, bf16[96,1536]{1,0:T(8,128)(2,1)S(1)}, u32[]{:S(2)}, u32[]{:S(2)}) %collective-permute-start.51) | collective-permute-done | bytes 294944 | tf_op jit(solution)/shard_map/ppermute | solution.py:217
  469.2 6.3 %collective-permute-done.52 = bf16[192,1536]{1,0:T(8,128)(2,1)S(1)} collective-permute-done((bf16[192,1536]{1,0:T(8,128)(2,1)S(1)}, bf16[192,1536]{1,0:T(8,128)(2,1)S(1)}, u32[]{:S(2)}, u32[]{:S(2)}) %collective-permute-start.52) | collective-permute-done | bytes 589856 | tf_op jit(solution)/shard_map/ppermute | solution.py:217
  481.3 10.8 %collective-permute-done.53 = bf16[384,1536]{1,0:T(8,128)(2,1)S(1)} collective-permute-done((bf16[384,1536]{1,0:T(8,128)(2,1)S(1)}, bf16[384,1536]{1,0:T(8,128)(2,1)S(1)}, u32[]{:S(2)}, u32[]{:S(2)}) %collective-permute-start.53) | collective-permute-done | bytes 1179680 | tf_op jit(solution)/shard_map/ppermute | solution.py:217
  492.8 13.5 %collective-permute-done.63 = bf16[768,768]{1,0:T(8,128)(2,1)S(1)} collective-permute-done((bf16[768,768]{1,0:T(8,128)(2,1)S(1)}, bf16[768,768]{1,0:T(8,128)(2,1)S(1)}, u32[]{:S(2)}, u32[]{:S(2)}) %collective-permute-start.63) | collective-permute-done | bytes 1179680 | tf_op jit(solution)/shard_map/ppermute | solution.py:217
  512.7 5.0 maximum_convert_fusion
  518.7 4.5 maximum_convert_fusion.1
  (422 shorter events, 235.4 us)
Async XLA Ops:
  7.9 28.8 %collective-permute-start = (bf16[256,768]{0,1:T(8,128)(2,1)}, bf16[256,768]{0,1:T(8,128)(2,1)}, u32[]{:S(2)}, u32[]{:S(2)}) collective-permute-start(bf16[256,768]{0,1:T(8,128)(2,1)} %bitcast.1), channel_id=1, source_target_pairs={{0,0},{1,1},{2,2},{3,3},{4,4},{5,5},{6,6},{7,7},{8,8},{9,9},{10,10... | collective-permute-start | bytes 1179656 | tf_op jit(solution)/shard_map/ppermute | solution.py:309
  13.7 24.6 %collective-permute-start.1 = (bf16[256,768]{0,1:T(8,128)(2,1)}, bf16[256,768]{0,1:T(8,128)(2,1)}, u32[]{:S(2)}, u32[]{:S(2)}) collective-permute-start(bf16[256,768]{0,1:T(8,128)(2,1)} %bitcast.2), channel_id=1, source_target_pairs={{0,1},{1,0},{2,3},{3,2},{4,5},{5,4},{6,7},{7,6},{8,9},{9,8},{10,11... | collective-permute-start | bytes 1179656 | tf_op jit(solution)/shard_map/ppermute | solution.py:309
  35.3 86.3 %collective-permute-start.15 = (bf16[256,768]{0,1:T(8,128)(2,1)}, bf16[256,768]{0,1:T(8,128)(2,1)}, u32[]{:S(2)}, u32[]{:S(2)}) collective-permute-start(bf16[256,768]{0,1:T(8,128)(2,1)} %bitcast.18), channel_id=1, source_target_pairs={{0,3},{1,2},{2,1},{3,0},{4,7},{5,6},{6,5},{7,4},{8,11},{9,10},{10,... | collective-permute-start | bytes 1179656 | tf_op jit(solution)/shard_map/ppermute | solution.py:309
  36.7 84.9 %collective-permute-start.14 = (bf16[256,768]{0,1:T(8,128)(2,1)}, bf16[256,768]{0,1:T(8,128)(2,1)}, u32[]{:S(2)}, u32[]{:S(2)}) collective-permute-start(bf16[256,768]{0,1:T(8,128)(2,1)} %bitcast.17), channel_id=1, source_target_pairs={{0,2},{1,3},{2,0},{3,1},{4,6},{5,7},{6,4},{7,5},{8,10},{9,11},{10,... | collective-permute-start | bytes 1179656 | tf_op jit(solution)/shard_map/ppermute | solution.py:309
  38.3 83.3 %collective-permute-start.13 = (bf16[256,768]{0,1:T(8,128)(2,1)}, bf16[256,768]{0,1:T(8,128)(2,1)}, u32[]{:S(2)}, u32[]{:S(2)}) collective-permute-start(bf16[256,768]{0,1:T(8,128)(2,1)} %bitcast.16), channel_id=1, source_target_pairs={{0,1},{1,0},{2,3},{3,2},{4,5},{5,4},{6,7},{7,6},{8,9},{9,8},{10,11... | collective-permute-start | bytes 1179656 | tf_op jit(solution)/shard_map/ppermute | solution.py:309
  39.5 82.2 %collective-permute-start.12 = (bf16[256,768]{0,1:T(8,128)(2,1)}, bf16[256,768]{0,1:T(8,128)(2,1)}, u32[]{:S(2)}, u32[]{:S(2)}) collective-permute-start(bf16[256,768]{0,1:T(8,128)(2,1)} %bitcast.15), channel_id=1, source_target_pairs={{0,0},{1,1},{2,2},{3,3},{4,4},{5,5},{6,6},{7,7},{8,8},{9,9},{10,10... | collective-permute-start | bytes 1179656 | tf_op jit(solution)/shard_map/ppermute | solution.py:309
  224.8 35.8 %collective-permute-start.8 = (bf16[256,768]{0,1:T(8,128)(2,1)}, bf16[256,768]{0,1:T(8,128)(2,1)}, u32[]{:S(2)}, u32[]{:S(2)}) collective-permute-start(bf16[256,768]{0,1:T(8,128)(2,1)} %get-tuple-element.76), channel_id=1, source_target_pairs={{0,0},{1,1},{2,2},{3,3},{4,4},{5,5},{6,6},{7,7},{8,8},{9,9},{10,10... | collective-permute-start | bytes 1179656 | tf_op jit(solution)/shard_map/ppermute | solution.py:316
  228.7 47.8 %collective-permute-start.10 = (bf16[256,768]{0,1:T(8,128)(2,1)}, bf16[256,768]{0,1:T(8,128)(2,1)}, u32[]{:S(2)}, u32[]{:S(2)}) collective-permute-start(bf16[256,768]{0,1:T(8,128)(2,1)} %get-tuple-element.74), channel_id=1, source_target_pairs={{2,0},{3,1},{0,2},{1,3},{6,4},{7,5},{4,6},{5,7},{10,8},{11,9},{8,1... | collective-permute-start | bytes 1179656 | tf_op jit(solution)/shard_map/ppermute | solution.py:316
  255.7 27.7 %collective-permute-start.11 = (bf16[256,768]{0,1:T(8,128)(2,1)}, bf16[256,768]{0,1:T(8,128)(2,1)}, u32[]{:S(2)}, u32[]{:S(2)}) collective-permute-start(bf16[256,768]{0,1:T(8,128)(2,1)} %get-tuple-element.73), channel_id=1, source_target_pairs={{3,0},{2,1},{1,2},{0,3},{7,4},{6,5},{5,6},{4,7},{11,8},{10,9},{9,1... | collective-permute-start | bytes 1179656 | tf_op jit(solution)/shard_map/ppermute | solution.py:316
  260.7 26.8 %collective-permute-start.16 = (bf16[256,768]{0,1:T(8,128)(2,1)}, bf16[256,768]{0,1:T(8,128)(2,1)S(1)}, u32[]{:S(2)}, u32[]{:S(2)}) collective-permute-start(bf16[256,768]{0,1:T(8,128)(2,1)} %get-tuple-element.72), channel_id=1, source_target_pairs={{0,0},{1,1},{2,2},{3,3},{4,4},{5,5},{6,6},{7,7},{8,8},{9,9},{10,10... | collective-permute-start | bytes 1179656 | tf_op jit(solution)/shard_map/ppermute | solution.py:316
  267.1 32.2 %collective-permute-start.17 = (bf16[256,768]{0,1:T(8,128)(2,1)S(1)}, bf16[256,768]{0,1:T(8,128)(2,1)S(1)}, u32[]{:S(2)}, u32[]{:S(2)}) collective-permute-start(bf16[256,768]{0,1:T(8,128)(2,1)S(1)} %copy-done.37), channel_id=1, source_target_pairs={{1,0},{0,1},{3,2},{2,3},{5,4},{4,5},{7,6},{6,7},{9,8},{8,9},{11,10... | collective-permute-start | bytes 1179656 | tf_op jit(solution)/shard_map/ppermute | solution.py:316
  274.6 40.7 %collective-permute-start.18 = (bf16[256,768]{0,1:T(8,128)(2,1)S(1)}, bf16[256,768]{0,1:T(8,128)(2,1)S(1)}, u32[]{:S(2)}, u32[]{:S(2)}) collective-permute-start(bf16[256,768]{0,1:T(8,128)(2,1)S(1)} %copy-done.36), channel_id=1, source_target_pairs={{2,0},{3,1},{0,2},{1,3},{6,4},{7,5},{4,6},{5,7},{10,8},{11,9},{8,1... | collective-permute-start | bytes 1179656 | tf_op jit(solution)/shard_map/ppermute | solution.py:316
  287.4 34.1 %collective-permute-start.19 = (bf16[256,768]{0,1:T(8,128)(2,1)}, bf16[256,768]{0,1:T(8,128)(2,1)}, u32[]{:S(2)}, u32[]{:S(2)}) collective-permute-start(bf16[256,768]{0,1:T(8,128)(2,1)} %get-tuple-element.69), channel_id=1, source_target_pairs={{3,0},{2,1},{1,2},{0,3},{7,4},{6,5},{5,6},{4,7},{11,8},{10,9},{9,1... | collective-permute-start | bytes 1179656 | tf_op jit(solution)/shard_map/ppermute | solution.py:316
  299.0 45.0 %collective-permute-start.45 = (bf16[768,1536]{1,0:T(8,128)(2,1)}, bf16[768,1536]{1,0:T(8,128)(2,1)}, u32[]{:S(2)}, u32[]{:S(2)}) collective-permute-start(bf16[768,1536]{1,0:T(8,128)(2,1)} %convolution_convert_fusion.1), channel_id=1, source_target_pairs={{0,1},{1,0},{2,3},{3,2},{4,5},{5,4},{6,7},{7,6},{8,9},{9,8},{10,11... | collective-permute-start | bytes 7077896 | tf_op jit(solution)/shard_map/ppermute | solution.py:217
  306.3 50.9 %collective-permute-start.55 = (bf16[1536,768]{1,0:T(8,128)(2,1)}, bf16[1536,768]{1,0:T(8,128)(2,1)}, u32[]{:S(2)}, u32[]{:S(2)}) collective-permute-start(bf16[1536,768]{1,0:T(8,128)(2,1)} %convolution_convert_fusion), channel_id=1, source_target_pairs={{0,1},{1,0},{2,3},{3,2},{4,5},{5,4},{6,7},{7,6},{8,9},{9,8},{10,11... | collective-permute-start | bytes 7077896 | tf_op jit(solution)/shard_map/ppermute | solution.py:217
  312.7 29.0 %collective-permute-start.21 = (bf16[1152,384]{1,0:T(8,128)(2,1)}, bf16[1152,384]{1,0:T(8,128)(2,1)}, u32[]{:S(2)}, u32[]{:S(2)}) collective-permute-start(bf16[1152,384]{1,0:T(8,128)(2,1)} %constant_dynamic-slice_fusion.15), channel_id=1, source_target_pairs={{0,4},{4,0},{8,12},{12,8},{16,20},{20,16},{24,28},{28,24},{1,5},{5... | collective-permute-start | bytes 2654216 | tf_op jit(solution)/shard_map/ppermute | solution.py:217
  315.3 25.3 %collective-permute-start.43 = (bf16[384,384]{1,0:T(8,128)(2,1)}, bf16[384,384]{1,0:T(8,128)(2,1)}, u32[]{:S(2)}, u32[]{:S(2)}) collective-permute-start(bf16[384,384]{1,0:T(8,128)(2,1)} %pad_maximum_fusion.12), channel_id=1, source_target_pairs={{0,4},{4,0},{8,12},{12,8},{16,20},{20,16},{24,28},{28,24},{1,5},{5... | collective-permute-start | bytes 884744 | tf_op jit(solution)/shard_map/ppermute | solution.py:217
  349.4 37.2 %collective-permute-start.46 = (bf16[384,1536]{1,0:T(8,128)(2,1)S(1)}, bf16[384,1536]{1,0:T(8,128)(2,1)S(1)}, u32[]{:S(2)}, u32[]{:S(2)}) collective-permute-start(bf16[384,1536]{1,0:T(8,128)(2,1)S(1)} %constant_dynamic-slice_fusion.7), channel_id=1, source_target_pairs={{0,2},{1,3},{2,0},{3,1},{4,6},{5,7},{6,4},{7,5},{8,10},{9,11},{10,... | collective-permute-start | bytes 3538952 | tf_op jit(solution)/shard_map/ppermute | solution.py:217
  366.7 29.0 %collective-permute-start.56 = (bf16[768,768]{1,0:T(8,128)(2,1)S(1)}, bf16[768,768]{1,0:T(8,128)(2,1)S(1)}, u32[]{:S(2)}, u32[]{:S(2)}) collective-permute-start(bf16[768,768]{1,0:T(8,128)(2,1)S(1)} %constant_dynamic-slice_fusion.3), channel_id=1, source_target_pairs={{0,4},{4,0},{8,12},{12,8},{16,20},{20,16},{24,28},{28,24},{1,5},{5... | collective-permute-start | bytes 3538952 | tf_op jit(solution)/shard_map/ppermute | solution.py:217
  379.7 99.9 %collective-permute-start.44 = (bf16[768,384]{1,0:T(8,128)(2,1)S(1)}, bf16[768,384]{1,0:T(8,128)(2,1)S(1)}, u32[]{:S(2)}, u32[]{:S(2)}) collective-permute-start(bf16[768,384]{1,0:T(8,128)(2,1)S(1)} %pad_maximum_fusion.8), channel_id=1, source_target_pairs={{0,1},{1,0},{2,3},{3,2},{4,5},{5,4},{6,7},{7,6},{8,9},{9,8},{10,11... | collective-permute-start | bytes 1769480 | tf_op jit(solution)/shard_map/ppermute | solution.py:217
  396.3 30.4 %collective-permute-start.27 = (bf16[576,384]{1,0:T(8,128)(2,1)S(1)}, bf16[576,384]{1,0:T(8,128)(2,1)S(1)}, u32[]{:S(2)}, u32[]{:S(2)}) collective-permute-start(bf16[576,384]{1,0:T(8,128)(2,1)S(1)} %pad_maximum_fusion.11), channel_id=1, source_target_pairs={{0,8},{4,12},{8,0},{12,4},{16,24},{20,28},{24,16},{28,20},{1,9},{5... | collective-permute-start | bytes 1327112 | tf_op jit(solution)/shard_map/ppermute | solution.py:217
  427.0 41.9 %collective-permute-start.28 = (bf16[1152,384]{1,0:T(8,128)(2,1)S(1)}, bf16[1152,384]{1,0:T(8,128)(2,1)S(1)}, u32[]{:S(2)}, u32[]{:S(2)}) collective-permute-start(bf16[1152,384]{1,0:T(8,128)(2,1)S(1)} %pad_maximum_fusion.7), channel_id=1, source_target_pairs={{0,4},{4,0},{8,12},{12,8},{16,20},{20,16},{24,28},{28,24},{1,5},{5... | collective-permute-start | bytes 2654216 | tf_op jit(solution)/shard_map/ppermute | solution.py:217
  477.5 29.5 %collective-permute-start.29 = (bf16[2304,384]{1,0:T(8,128)(2,1)S(1)}, bf16[2304,384]{1,0:T(8,128)(2,1)S(1)}, u32[]{:S(2)}, u32[]{:S(2)}) collective-permute-start(bf16[2304,384]{1,0:T(8,128)(2,1)S(1)} %pad_maximum_fusion.3), channel_id=1, source_target_pairs={{0,1},{1,0},{2,3},{3,2},{4,5},{5,4},{6,7},{7,6},{8,9},{9,8},{10,11... | collective-permute-start | bytes 5308424 | tf_op jit(solution)/shard_map/ppermute | solution.py:217
  477.9 28.4 %collective-permute-start.63 = (bf16[768,768]{1,0:T(8,128)(2,1)S(1)}, bf16[768,768]{1,0:T(8,128)(2,1)S(1)}, u32[]{:S(2)}, u32[]{:S(2)}) collective-permute-start(bf16[768,768]{1,0:T(8,128)(2,1)S(1)} %pad_maximum_fusion.6), channel_id=1, source_target_pairs={{0,4},{4,0},{8,12},{12,8},{16,20},{20,16},{24,28},{28,24},{1,5},{5... | collective-permute-start | bytes 3538952 | tf_op jit(solution)/shard_map/ppermute | solution.py:217
  (106 other events, 1276.6 us)

commit v2 on v1

v2 whole, which is shorter than its diff:
```python
import functools

import jax
import jax.numpy as jnp
from jax import lax
from jax.experimental import pallas as pl
from jax.experimental.pallas import tpu as pltpu
from jax.sharding import PartitionSpec as P

DH = 64
PAIR = 128
MASKED = 1e30
F32 = jnp.float32
BF16 = jnp.bfloat16
NT = (((1,), (1,)), ((), ()))
NN = (((1,), (0,)), ((), ()))


def left_dot(first, second):
    return lax.dot_general(first, second, (((0,), (0,)), ((), ())), preferred_element_type=F32)


def right_dot(first, second):
    return lax.dot_general(first, second, NT, preferred_element_type=F32)


def split_three(values):
    high = values.astype(BF16)
    rest = values - high.astype(F32)
    middle = rest.astype(BF16)
    low = (rest - middle.astype(F32)).astype(BF16)
    return high.astype(F32), middle.astype(F32), low.astype(F32)


def own_lanes(shape, head):
    lane = lax.broadcasted_iota(jnp.int32, shape, 1)
    own = lane < DH if head == 0 else lane >= DH
    return own, lane % DH


def key_features(lane, seg):
    return jnp.where(
        lane < 3,
        1.0,
        jnp.where(lane == 3, -MASKED * (1.0 - seg), jnp.where(lane == 4, -MASKED * seg, 0.0)),
    ).astype(BF16)


def forward_kernel(q_ref, k_ref, v_ref, seg_q_ref, seg_k_ref, mixed_ref, query_ref, *, block):
    queries = q_ref.shape[0]
    keys = k_ref.shape[0]
    for head in range(2):
        own_k, lane_k = own_lanes((keys, PAIR), head)
        key_side = jnp.where(own_k, k_ref[...], key_features(lane_k, seg_k_ref[...].astype(F32)))
        value_side = jnp.where(own_k, v_ref[...], jnp.ones((), BF16))
        own_q, lane_q = own_lanes((block, PAIR), head)
        for start in range(0, queries, block):
            here = slice(start, start + block)
            q = q_ref[here, :]
            seg = seg_q_ref[here, :].astype(F32)
            seg_side = jnp.where(lane_q == 3, seg, jnp.where(lane_q == 4, 1.0 - seg, 0.0))
            query_side = jnp.where(own_q, q, seg_side.astype(BF16))
            scores = lax.dot_general(query_side, key_side, NT, preferred_element_type=F32)
            peak = jnp.max(scores, -1, keepdims=True)
            raised = jnp.exp(scores - peak).astype(BF16)
            summed = lax.dot_general(raised, value_side, NN, preferred_element_type=F32)
            total = summed[:, DH : DH + 1] if head == 0 else summed[:, 0:1]
            mixed = (summed / total).astype(BF16)
            shift = jnp.broadcast_to(-(peak + jnp.log(total)), (block, PAIR))
            high, middle, low = split_three(shift)
            extra = jnp.where(
                lane_q == 0,
                high,
                jnp.where(lane_q == 1, middle, jnp.where(lane_q == 2, low, seg_side)),
            )
            query_ref[head, here, :] = jnp.where(own_q, q, extra.astype(BF16))
            if head == 0:
                mixed_ref[here, :] = mixed
            else:
                mixed_ref[here, :] = jnp.where(own_q, mixed, mixed_ref[here, :])


def attention_forward(q, k, v, seg_q, seg_k):
    queries, width = q.shape
    keys = k.shape[0]
    pairs = width // PAIR
    column = lambda i: (0, i)
    whole = lambda i: (0, 0)
    return pl.pallas_call(
        functools.partial(forward_kernel, block=min(512, queries)),
        grid=(pairs,),
        in_specs=[
            pl.BlockSpec((queries, PAIR), column),
            pl.BlockSpec((keys, PAIR), column),
            pl.BlockSpec((keys, PAIR), column),
            pl.BlockSpec((queries, PAIR), whole),
            pl.BlockSpec((keys, PAIR), whole),
        ],
        out_specs=[
            pl.BlockSpec((queries, PAIR), column),
            pl.BlockSpec((2, queries, PAIR), lambda i: (i, 0, 0)),
        ],
        out_shape=[
            jax.ShapeDtypeStruct((queries, width), BF16),
            jax.ShapeDtypeStruct((2 * pairs, queries, PAIR), BF16),
        ],
        compiler_params=pltpu.CompilerParams(vmem_limit_bytes=40 * 2**20),
        cost_estimate=pl.CostEstimate(
            flops=16 * queries * keys * width,
            bytes_accessed=10 * queries * width,
            transcendentals=2 * pairs * queries * keys,
        ),
        name="attention_forward",
    )(q, k, v, seg_q, seg_k)


def backward_kernel(
    query_ref, k_ref, v_ref, seg_k_ref, mixed_ref, d_mixed_ref, *refs, block
):
    dq_ref, dk_ref, dv_ref, dqt = refs[-4:]
    queries = mixed_ref.shape[0]
    keys = k_ref.shape[0]
    d_mixed = d_mixed_ref[...]
    product = d_mixed.astype(F32) * mixed_ref[...].astype(F32)
    for head in range(2):
        own_q, lane_q = own_lanes((queries, PAIR), head)
        own_k, lane_k = own_lanes((block, PAIR), head)
        delta = -jnp.sum(jnp.where(own_q, product, 0.0), -1, keepdims=True)
        high, middle, low = split_three(jnp.broadcast_to(delta, (queries, PAIR)))
        extra = jnp.where(
            lane_q == 0, high, jnp.where(lane_q == 1, middle, jnp.where(lane_q == 2, low, 0.0))
        )
        d_side = jnp.where(own_q, d_mixed, extra.astype(BF16))
        query_side = query_ref[head]
        ones = jnp.where(lane_k < 3, 1.0, 0.0).astype(BF16)
        for start in range(0, keys, block):
            here = slice(start, start + block)
            k = k_ref[here, :]
            seg = seg_k_ref[here, :].astype(F32)
            key_side = jnp.where(own_k, k, key_features(lane_k, seg))
            value_side = jnp.where(own_k, v_ref[here, :], ones)
            shifted = lax.dot_general(key_side, query_side, NT, preferred_element_type=F32)
            probs = jnp.exp(shifted)
            d_probs = lax.dot_general(value_side, d_side, NT, preferred_element_type=F32)
            d_scores = (probs * d_probs).astype(BF16)
            dv = lax.dot_general(probs.astype(BF16), d_mixed, NN, preferred_element_type=F32)
            dk = lax.dot_general(d_scores, query_side, NN, preferred_element_type=F32)
            turned = k.T[head * DH : (head + 1) * DH, :]
            dq = lax.dot_general(turned, d_scores, NN, preferred_element_type=F32)
            mine = slice(head * DH, (head + 1) * DH)
            if start == 0:
                dqt[mine, :] = dq
            else:
                dqt[mine, :] += dq
            dv = dv.astype(dv_ref.dtype)
            dk = dk.astype(dk_ref.dtype)
            if head == 0:
                dk_ref[here, :] = dk
                dv_ref[here, :] = dv
            else:
                dk_ref[here, :] = jnp.where(own_k, dk, dk_ref[here, :])
                dv_ref[here, :] = jnp.where(own_k, dv, dv_ref[here, :])
    dq_ref[...] = (dqt[...] * 0.125).astype(BF16).T


def attention_backward(query_side, k, v, seg_k, mixed, d_mixed, kept, first, count, before):
    queries, width = mixed.shape
    keys = k.shape[0]
    column = lambda i: (0, i + first)
    held = [] if before is None else list(before)
    return pl.pallas_call(
        functools.partial(backward_kernel, block=min(512, keys)),
        grid=(count,),
        in_specs=[
            pl.BlockSpec((2, queries, PAIR), lambda i: (i + first, 0, 0)),
            pl.BlockSpec((keys, PAIR), column),
            pl.BlockSpec((keys, PAIR), column),
            pl.BlockSpec((keys, PAIR), lambda i: (0, 0)),
            pl.BlockSpec((queries, PAIR), column),
            pl.BlockSpec((queries, PAIR), column),
        ]
        + [pl.BlockSpec(memory_space=pl.ANY)] * len(held),
        out_specs=[
            pl.BlockSpec((queries, PAIR), column),
            pl.BlockSpec((keys, PAIR), column),
            pl.BlockSpec((keys, PAIR), column),
        ],
        input_output_aliases={6 + i: i for i in range(len(held))},
        out_shape=[
            jax.ShapeDtypeStruct((queries, width), BF16),
            jax.ShapeDtypeStruct((keys, width), kept),
            jax.ShapeDtypeStruct((keys, width), kept),
        ],
        scratch_shapes=[pltpu.VMEM((PAIR, queries), F32)],
        compiler_params=pltpu.CompilerParams(vmem_limit_bytes=40 * 2**20),
        cost_estimate=pl.CostEstimate(
            flops=40 * queries * keys * PAIR * count,
            bytes_accessed=14 * queries * PAIR * count,
            transcendentals=2 * count * queries * keys,
        ),
        name="attention_backward",
    )(query_side, k, v, seg_k, mixed, d_mixed, *held)


def dot(first, second, dims=NN):
    return lax.dot_general(first, second, dims, preferred_element_type=F32)


def gelu_pair(values):
    below = 0.5 + 0.5 * lax.erf(values * 0.7071067811865476)
    density = jnp.exp(-0.5 * values * values) * 0.3989422804014327
    return values * below, below + values * density


def normalise(values):
    centred = values - jnp.mean(values, -1, keepdims=True)
    scale = lax.rsqrt(jnp.mean(centred * centred, -1, keepdims=True) + 1e-06)
    return centred * scale, scale


def norm_back(upstream, hat, scale, gain):
    d_hat = upstream * gain
    return scale * (
        d_hat
        - jnp.mean(d_hat, -1, keepdims=True)
        - hat * jnp.mean(d_hat * hat, -1, keepdims=True)
    )


def stack_rows(rows):
    filler = jnp.zeros((8 - len(rows), rows[0].shape[1]), F32)
    return jnp.concatenate(rows + [filler], 0)


def feed_forward_kernel(
    inputs_ref,
    mixed_ref,
    output_proj_ref,
    output_bias_ref,
    gain_one_ref,
    shift_one_ref,
    expand_ref,
    expand_bias_ref,
    shrink_ref,
    shrink_bias_ref,
    gain_two_ref,
    shift_two_ref,
    *refs,
    steps,
    held,
):
    upstream_refs = refs[:held]
    hat_ref, scale_ref, normed_ref, active_t_ref, slope_ref = refs[held : held + 5]
    d_second_ref, d_down_ref, sums_ref = refs[held + 5 : held + 8]
    out_refs = refs[held + 8 : -1]
    total = refs[-1]
    block = total.shape[0] // held
    step = pl.program_id(0)
    tokens = total.shape[0]
    pieces = [slice(start, start + block) for start in range(0, tokens, block)]

    @pl.when(step == 0)
    def _():
        for here in pieces:
            first_sum = (
                inputs_ref[here, :].astype(F32)
                + dot(mixed_ref[here, :], output_proj_ref[...])
                + output_bias_ref[...].astype(F32)
            )
            hat, scale = normalise(first_sum)
            hat_ref[here, :] = hat
            scale_ref[here, :] = jnp.broadcast_to(scale, (block, PAIR))
            normed = gain_one_ref[...].astype(F32) * hat + shift_one_ref[...].astype(F32)
            normed_ref[here, :] = normed.astype(BF16)
            total[here, :] = normed + shrink_bias_ref[...].astype(F32)

    for here in pieces:
        expanded = dot(normed_ref[here, :], expand_ref[...]) + expand_bias_ref[...].astype(F32)
        active, slope = gelu_pair(expanded)
        active = active.astype(BF16)
        slope_ref[here, :] = slope.astype(BF16)
        active_t_ref[:, here] = active.T
        total[here, :] += dot(active, shrink_ref[...])

    @pl.when(step == steps - 1)
    def _():
        gain = gain_two_ref[...].astype(F32)
        d_gain = jnp.zeros((1, total.shape[1]), F32)
        d_shift = d_gain
        d_bias = d_gain
        for here, upstream_ref, out_ref in zip(pieces, upstream_refs, out_refs):
            hat, scale = normalise(total[here, :])
            out_ref[...] = (gain * hat + shift_two_ref[...].astype(F32)).astype(BF16)
            upstream = upstream_ref[...].astype(F32)
            d_gain += jnp.sum(upstream * hat, 0, keepdims=True)
            d_shift += jnp.sum(upstream, 0, keepdims=True)
            d_second = norm_back(upstream, hat, scale, gain)
            d_second_ref[here, :] = d_second
            d_down = d_second.astype(BF16)
            d_down_ref[here, :] = d_down
            d_bias += jnp.sum(d_down.astype(F32), 0, keepdims=True)
        sums_ref[...] = stack_rows([d_gain, d_shift, d_bias])


def fixed(*shape):
    return pl.BlockSpec(shape, lambda i: (0,) * len(shape), pipeline_mode=pl.Buffered(1))


def shapes(*pairs):
    return [jax.ShapeDtypeStruct(shape, dtype) for shape, dtype in pairs]


def feed_forward(inputs, mixed, upstream, weights, block=512):
    tokens, width = inputs.shape
    units = weights[4].shape[1]
    steps = units // block
    held = len(upstream)
    piece = tokens // held
    row = fixed(1, width)
    return pl.pallas_call(
        functools.partial(feed_forward_kernel, steps=steps, held=held),
        grid=(steps,),
        in_specs=[fixed(tokens, width)] * 2
        + [fixed(width, width), row, row, row]
        + [
            pl.BlockSpec((width, block), lambda i: (0, i)),
            pl.BlockSpec((1, block), lambda i: (0, i)),
            pl.BlockSpec((block, width), lambda i: (i, 0)),
            row,
            row,
            row,
        ]
        + [fixed(piece, width)] * held,
        out_specs=[
            fixed(tokens, width),
            fixed(tokens, PAIR),
            fixed(tokens, width),
            pl.BlockSpec((block, tokens), lambda i: (i, 0)),
            pl.BlockSpec((tokens, block), lambda i: (0, i)),
            fixed(tokens, width),
            fixed(tokens, width),
            fixed(8, width),
        ]
        + [fixed(piece, width)] * held,
        out_shape=shapes(
            ((tokens, width), F32),
            ((tokens, PAIR), F32),
            ((tokens, width), BF16),
            ((units, tokens), BF16),
            ((tokens, units), BF16),
            ((tokens, width), F32),
            ((tokens, width), BF16),
            ((8, width), F32),
            *[((piece, width), BF16)] * held,
        ),
        scratch_shapes=[pltpu.VMEM((tokens, width), F32)],
        compiler_params=pltpu.CompilerParams(vmem_limit_bytes=36 * 2**20),
        cost_estimate=pl.CostEstimate(
            flops=6 * tokens * width * units, bytes_accessed=50 * 2**20, transcendentals=0
        ),
        name="feed_forward",
    )(inputs, mixed, *weights, *upstream)


def feed_back_kernel(
    which_ref,
    d_down_ref,
    before_ref,
    slope_ref,
    active_t_ref,
    shrink_ref,
    expand_ref,
    normed_ref,
    *refs,
    steps,
    block,
    last,
):
    if last:
        hat_ref, scale_ref, gain_ref, output_proj_ref = refs[:4]
        grads_ref, bias_ref, d_first_ref, d_attn_ref, d_mixed_ref, sums_ref, turned, total = refs[4:]
    else:
        grads_ref, bias_ref, total, turned = refs
    step = pl.program_id(0)
    tokens = total.shape[0]
    pieces = [slice(start, start + block) for start in range(0, tokens, block)]

    @pl.when(step == 0)
    def _():
        total[...] = before_ref[...]

    bias = jnp.zeros((1, slope_ref.shape[1]), F32)
    for here in pieces:
        d_active = dot(d_down_ref[here, :], shrink_ref[...], NT)
        d_expand = (d_active * slope_ref[here, :].astype(F32)).astype(BF16)
        turned[:, here] = d_expand.T
        bias += jnp.sum(d_expand.astype(F32), 0, keepdims=True)
        total[here, :] += dot(d_expand, expand_ref[...], NT)
    bias_ref[...] = bias
    grads_ref[0] = dot(active_t_ref[...], d_down_ref[...]).astype(BF16)
    grads_ref[1] = dot(turned[...], normed_ref[...]).astype(BF16)

    if last:

        @pl.when(step == steps - 1)
        def _():
            gain = gain_ref[...].astype(F32)
            d_gain = jnp.zeros((1, total.shape[1]), F32)
            d_shift = d_gain
            d_bias = d_gain
            for here in pieces:
                d_normed = total[here, :]
                hat = hat_ref[here, :]
                d_gain += jnp.sum(d_normed * hat, 0, keepdims=True)
                d_shift += jnp.sum(d_normed, 0, keepdims=True)
                d_first = norm_back(d_normed, hat, scale_ref[here, :][:, 0:1], gain)
                d_first_ref[here, :] = d_first
                d_attn = d_first.astype(BF16)
                d_attn_ref[here, :] = d_attn
                d_bias += jnp.sum(d_attn.astype(F32), 0, keepdims=True)
                d_mixed_ref[here, :] = dot(d_attn, output_proj_ref[...], NT).astype(BF16)
            sums_ref[...] = stack_rows([d_gain, d_shift, d_bias])


def feed_back(which, d_down, before, slope, active_t, shrink, expand, normed, norm, block=512):
    tokens, width = d_down.shape
    half = slope.shape[1] // 2
    steps = half // block
    last = norm is not None
    at = lambda i, which: which[0] * steps + i
    whole = lambda *shape: pl.BlockSpec(
        shape, lambda i, which: (0,) * len(shape), pipeline_mode=pl.Buffered(1)
    )
    in_specs = [
        whole(tokens, width),
        whole(tokens, width),
        pl.BlockSpec((tokens, block), lambda i, which: (0, at(i, which))),
        pl.BlockSpec((block, tokens), lambda i, which: (at(i, which), 0)),
        pl.BlockSpec((block, width), lambda i, which: (at(i, which), 0)),
        pl.BlockSpec((width, block), lambda i, which: (0, at(i, which))),
        whole(tokens, width),
    ]
    out_specs = [
        pl.BlockSpec((2, block, width), lambda i, which: (0, i, 0)),
        pl.BlockSpec((1, block), lambda i, which: (0, i)),
    ]
    out_shape = shapes(((2, half, width), BF16), ((1, half), F32))
    scratch = [pltpu.VMEM((block, tokens), BF16)]
    if last:
        in_specs += [whole(tokens, width), whole(tokens, PAIR), whole(1, width), whole(width, width)]
        out_specs += [whole(tokens, width)] * 3 + [whole(8, width)]
        out_shape += shapes(
            ((tokens, width), F32), ((tokens, width), BF16), ((tokens, width), BF16), ((8, width), F32)
        )
        scratch.append(pltpu.VMEM((tokens, width), F32))
    else:
        out_specs.append(whole(tokens, width))
        out_shape += shapes(((tokens, width), F32))
    return pl.pallas_call(
        functools.partial(feed_back_kernel, steps=steps, block=min(512, tokens), last=last),
        grid_spec=pltpu.PrefetchScalarGridSpec(
            num_scalar_prefetch=1,
            grid=(steps,),
            in_specs=in_specs,
            out_specs=out_specs,
            scratch_shapes=scratch,
        ),
        out_shape=out_shape,
        compiler_params=pltpu.CompilerParams(vmem_limit_bytes=36 * 2**20),
        cost_estimate=pl.CostEstimate(
            flops=8 * tokens * width * half, bytes_accessed=30 * 2**20, transcendentals=0
        ),
        name="feed_back_last" if last else "feed_back",
    )(which, d_down, before, slope, active_t, shrink, expand, normed, *(norm or ()))


def weight_kernel(which_ref, inputs_ref, mixed_ref, dq_ref, dk_ref, dv_ref, d_attn_ref, out_ref):
    count = inputs_ref.shape[1] // 2
    columns = pl.ds(pl.multiple_of(which_ref[0] * count, PAIR), count)
    inputs_t = inputs_ref[:, columns].T
    out_ref[0 * count : 1 * count, :] = dot(inputs_t, dq_ref[...]).astype(BF16)
    out_ref[1 * count : 2 * count, :] = dot(inputs_t, dk_ref[...]).astype(BF16)
    out_ref[2 * count : 3 * count, :] = dot(inputs_t, dv_ref[...]).astype(BF16)
    out_ref[3 * count : 4 * count, :] = dot(mixed_ref[:, columns].T, d_attn_ref[...]).astype(BF16)
    if out_ref.shape[0] > 4 * count:
        out_ref[4 * count :, :] = jnp.zeros((out_ref.shape[0] - 4 * count, out_ref.shape[1]), BF16)


def weight_halves(which, inputs, mixed, dq, dk, dv, d_attn, unit):
    tokens, width = inputs.shape
    rows = -(-2 * width // unit) * unit
    return pl.pallas_call(
        weight_kernel,
        grid_spec=pltpu.PrefetchScalarGridSpec(
            num_scalar_prefetch=1,
            grid=(1,),
            in_specs=[pl.BlockSpec((tokens, width), lambda i, which: (0, 0))] * 6,
            out_specs=pl.BlockSpec((rows, width), lambda i, which: (0, 0)),
        ),
        out_shape=jax.ShapeDtypeStruct((rows, width), BF16),
        compiler_params=pltpu.CompilerParams(vmem_limit_bytes=40 * 2**20),
        cost_estimate=pl.CostEstimate(
            flops=4 * tokens * width * width, bytes_accessed=12 * 2**20, transcendentals=0
        ),
        name="weight_halves",
    )(which, inputs, mixed, dq, dk, dv, d_attn)


def feed_out_kernel(core_ref, own_ref, got_ref, shrink_ref, expand_ref, *, steps):
    own = core_ref[0] == pl.program_id(0)
    step = pl.program_id(1)

    for mine, ref in ((True, own_ref), (False, got_ref)):

        @pl.when((own == mine) & (step < steps))
        def _(ref=ref):
            shrink_ref[...] = ref[...].astype(F32)

        @pl.when((own == mine) & (step >= steps))
        def _(ref=ref):
            expand_ref[...] = ref[...].T.astype(F32)


def feed_out(core, own, got, block=512):
    width = own.shape[1]
    half = own.shape[0] // 2
    steps = half // block

    def source(mine):
        def index(h, i, core):
            return (jnp.where((core[0] == h) == mine, i, 0), 0)

        return pl.BlockSpec((block, width), index)

    shrink_at = lambda h, i, core: (h * steps + jnp.minimum(i, steps - 1), 0)
    expand_at = lambda h, i, core: (0, h * steps + jnp.maximum(i - steps, 0))
    return pl.pallas_call(
        functools.partial(feed_out_kernel, steps=steps),
        grid_spec=pltpu.PrefetchScalarGridSpec(
            num_scalar_prefetch=1,
            grid=(2, 2 * steps),
            in_specs=[source(True), source(False)],
            out_specs=[
                pl.BlockSpec((block, width), shrink_at),
                pl.BlockSpec((width, block), expand_at),
            ],
        ),
        out_shape=shapes(((2 * half, width), F32), ((width, 2 * half), F32)),
        compiler_params=pltpu.CompilerParams(vmem_limit_bytes=24 * 2**20),
        cost_estimate=pl.CostEstimate(
            flops=half * width, bytes_accessed=24 * half * width, transcendentals=0
        ),
        name="feed_out",
    )(core, own, got)


def attn_out_kernel(core_ref, own_ref, got_ref, *out_refs):
    own = core_ref[0] == pl.program_id(1)
    for index, out_ref in enumerate(out_refs):
        for mine, ref in ((True, own_ref), (False, got_ref)):

            @pl.when((own == mine) & (pl.program_id(0) == index))
            def _(ref=ref, out_ref=out_ref):
                out_ref[...] = ref[...].astype(F32)


def attn_out(core, own, got, width):
    half = width // 2

    def source(mine):
        return pl.BlockSpec((half, width), lambda m, h, core: (m, 0))

    def target(index):
        at = lambda m, h, core: (jnp.where(m < index, 0, jnp.where(m == index, h, 1)), 0)
        return pl.BlockSpec((half, width), at)

    return pl.pallas_call(
        attn_out_kernel,
        grid_spec=pltpu.PrefetchScalarGridSpec(
            num_scalar_prefetch=1,
            grid=(4, 2),
            in_specs=[source(True), source(False)],
            out_specs=[target(index) for index in range(4)],
        ),
        out_shape=shapes(*[((width, width), F32)] * 4),
        compiler_params=pltpu.CompilerParams(vmem_limit_bytes=24 * 2**20),
        name="attn_out",
    )(core, own, got)


def rows_of(ref, which, count, base=0):
    return ref[pl.ds(pl.multiple_of(base + which * count, 16), count), :]


def sum_of(terms):
    return functools.reduce(lambda a, b: a + b, [t.astype(F32) for t in terms]).astype(BF16)


def scatter_kernel(bits_ref, *refs, groups):
    ins, outs = refs[: 2 * groups], refs[2 * groups :]
    for group in range(groups):
        terms = ins[2 * group : 2 * group + 2]
        sent_ref, kept_ref = outs[2 * group : 2 * group + 2]
        count = kept_ref.shape[0]
        here = bits_ref[group]
        sent_ref[...] = sum_of([rows_of(term, 1 - here, count) for term in terms])
        kept_ref[...] = sum_of([rows_of(term, here, count) for term in terms])


def local_call(kernel, bits, values, out_shape, name):
    vmem = pl.BlockSpec(memory_space=pltpu.VMEM)
    return pl.pallas_call(
        kernel,
        in_specs=[pl.BlockSpec(memory_space=pltpu.SMEM)] + [vmem] * len(values),
        out_specs=[vmem] * len(out_shape),
        out_shape=out_shape,
        compiler_params=pltpu.CompilerParams(vmem_limit_bytes=24 * 2**20),
        name=name,
    )(bits, *values)


def scatter_local(bits, pairs):
    groups = len(pairs)
    counts = [kept.shape[0] // 2 for kept, _ in pairs]
    width = pairs[0][0].shape[1]
    outs = local_call(
        functools.partial(scatter_kernel, groups=groups),
        bits,
        [value for pair in pairs for value in pair],
        shapes(*[((count, width), BF16) for count in counts for _ in range(2)]),
        "scatter_local",
    )
    return [outs[2 * i : 2 * i + 2] for i in range(groups)]


def scatter_first(bits, own, got, counts, blocks=2):
    width = own.shape[1]
    outs = []
    base = 0
    for group, count in enumerate(counts):
        block = count // 2 // blocks
        first = base // block

        def source(i, bits, group=group, first=first):
            kept = i // blocks
            return (first + jnp.where(kept == 1, bits[group], 1 - bits[group]) * blocks + i % blocks, 0)

        outs.append(
            pl.pallas_call(
                first_split_kernel,
                grid_spec=pltpu.PrefetchScalarGridSpec(
                    num_scalar_prefetch=1,
                    grid=(2 * blocks,),
                    in_specs=[pl.BlockSpec((block, width), source)] * 2,
                    out_specs=[
                        pl.BlockSpec((block, width), lambda i, bits: (jnp.minimum(i, blocks - 1), 0)),
                        pl.BlockSpec((block, width), lambda i, bits: (jnp.maximum(i - blocks, 0), 0)),
                    ],
                ),
                out_shape=shapes(*[((count // 2, width), BF16)] * 2),
                compiler_params=pltpu.CompilerParams(vmem_limit_bytes=16 * 2**20),
                name="scatter_first",
            )(bits, own, got)
        )
        base += count
    return outs


def first_split_kernel(bits_ref, own_ref, got_ref, sent_ref, kept_ref):
    del bits_ref
    sending = pl.program_id(0) < pl.num_programs(0) // 2
    value = sum_of([own_ref[...], got_ref[...]])

    @pl.when(sending)
    def _():
        sent_ref[...] = value

    @pl.when(jnp.logical_not(sending))
    def _():
        kept_ref[...] = value


def split_two(values):
    high = values.astype(BF16)
    return high, (values - high.astype(F32)).astype(BF16)


SMALL = 32


def put_small(ref, at, values):
    high, low = split_two(values)
    ref[at : at + SMALL // 2, :] = high
    ref[at + SMALL // 2 : at + SMALL, :] = low


def get_small(ref, at):
    half = SMALL // 2
    return ref[at : at + half, :].astype(F32) + ref[at + half : at + SMALL, :].astype(F32)


def settle_kernel(bits_ref, *refs, groups, small):
    del bits_ref
    ins, outs = refs[: 2 * groups], refs[2 * groups + small :]
    for group in range(groups):
        count = ins[2 * group].shape[0]
        outs[group][0:count, :] = sum_of([ins[2 * group][...], ins[2 * group + 1][...]])
        if small and group == 0:
            put_small(outs[group], count, refs[2 * groups][...])


def settle_local(bits, pairs, small):
    width = pairs[0][0].shape[1]
    counts = [kept.shape[0] for kept, _ in pairs]
    if small is not None:
        counts[0] += SMALL
    return local_call(
        functools.partial(settle_kernel, groups=len(pairs), small=int(small is not None)),
        bits,
        [value for pair in pairs for value in pair] + ([] if small is None else [small]),
        shapes(*[((count, width), BF16) for count in counts]),
        "settle_local",
    )


def join_kernel(bits_ref, *refs, groups, small, merged):
    ins, outs = refs[: 2 * groups], refs[2 * groups :]
    base = 0
    for group in range(groups):
        own_ref, got_ref = ins[2 * group : 2 * group + 2]
        extra = SMALL if small and group == 0 else 0
        count = own_ref.shape[0] - extra
        out_ref = outs[0 if merged else group]
        here = bits_ref[group]
        for half, ref in ((here, own_ref), (1 - here, got_ref)):
            out_ref[pl.ds(pl.multiple_of(base + half * count, 16), count), :] = ref[0:count, :]
        if extra:
            at = out_ref.shape[0] - SMALL if merged else base + 2 * count
            put_small(out_ref, at, get_small(own_ref, count) + get_small(got_ref, count))
        if merged:
            base += 2 * count


def join_local(bits, pairs, small, merged):
    width = pairs[0][0].shape[1]
    counts = [2 * own.shape[0] for own, _ in pairs]
    if small:
        counts[0] -= SMALL
    if merged:
        counts = [sum(counts)]
    return local_call(
        functools.partial(join_kernel, groups=len(pairs), small=small, merged=merged),
        bits,
        [value for pair in pairs for value in pair],
        shapes(*[((count, width), BF16) for count in counts]),
        "join_local",
    )


def tie(*values):
    return lax.optimization_barrier(values)


def pick(which, parts):
    if len(parts) == 1:
        return parts[0]
    half = len(parts) // 2
    return jnp.where(which < half, pick(which, parts[:half]), pick(which - half, parts[half:]))


def column_sum(values):
    return jnp.sum(values.astype(F32), 0)


class Stage:
    def __init__(self, sizes, bits):
        self.bits = bits
        rows, seq = sizes
        self.pairs = []
        for index in range(rows * seq):
            axis, bit = bits[index & 1]
            self.pairs.append((index, index ^ ((1 << bit) * (seq if axis == "rows" else 1))))

    def here(self):
        first, second = [(lax.axis_index(axis) >> bit) & 1 for axis, bit in self.bits]
        if self.bits[0] == self.bits[1]:
            return first
        return jnp.where(lax.axis_index("seq") & 1 == 0, first, second)

    def swap(self, values):
        return lax.ppermute(values, ("rows", "seq"), self.pairs)


def total_over_chips(own, got, core_stage, orders, small=None):
    depth = len(orders[0][1])
    groups = range(len(orders))

    def bits_at(step):
        return jnp.stack([stages[step].here() for _, stages in orders]).astype(jnp.int32)

    def pairs_of(flat):
        return [flat[i : i + 2] for i in range(0, len(flat), 2)]

    def send(step, values, keep):
        flat = []
        for group in groups:
            flat += [keep[group], orders[group][1][step].swap(values[group])]
        return flat

    parts = scatter_first(bits_at(0), own, got, [count for count, _ in orders])
    for step in range(1, depth + 1):
        flat = yield send(step - 1, [p[0] for p in parts], [p[1] for p in parts])
        if step < depth:
            parts = scatter_local(bits_at(step), pairs_of(flat))
    values = settle_local(bits_at(0), pairs_of(flat), small)
    for step in reversed(range(depth)):
        flat = yield send(step, values, values)
        values = join_local(bits_at(step), pairs_of(flat), small is not None, step == 0)
    both = yield [values[0], core_stage.swap(values[0])]
    return both


def arriving(values):
    values = yield values
    return values


class Flow:
    def __init__(self, steps):
        self.steps = steps
        self.pending = next(steps)
        self.result = None


def advance(flows, *values):
    flows = [flow for flow in flows if flow.result is None]
    count = len(values)
    tied = tie(*values, *[value for flow in flows for value in flow.pending])
    at = count
    for flow in flows:
        arrived = list(tied[at : at + len(flow.pending)])
        at += len(flow.pending)
        try:
            flow.pending = flow.steps.send(arrived)
        except StopIteration as end:
            flow.pending = []
            flow.result = end.value
    return tied[:count]


def solution(mesh):
    seq_size = mesh.shape["seq"]
    rows_size = mesh.shape["rows"]
    seq_bits = seq_size.bit_length() - 1
    rows_bits = rows_size.bit_length() - 1
    off_chip = [("seq", bit) for bit in range(1, seq_bits)]
    off_chip += [("rows", bit) for bit in range(rows_bits)]
    first, *middle, ahead, final = off_chip
    sizes = (rows_size, seq_size)
    core_stage = Stage(sizes, [("seq", 0)] * 2)
    straight = [first] + middle + [ahead, final]
    turned = middle + [ahead, first, final]
    spun = [ahead, first] + middle + [final]
    wide = [Stage(sizes, bits) for bits in zip(straight, turned)]
    slim = [Stage(sizes, bits) for bits in zip(spun, spun)]

    def body(
        hidden_in,
        segments,
        grad_mask,
        grad_out,
        query_proj,
        query_bias,
        key_proj,
        value_proj,
        value_bias,
        output_proj,
        output_bias,
        first_gain,
        first_shift,
        expand_proj,
        expand_bias,
        shrink_proj,
        shrink_bias,
        second_gain,
        second_shift,
    ):
        micro, rows_here, piece, width = hidden_in.shape
        held = micro * rows_here
        sharers = seq_size // held
        tokens = held * piece
        source_at = lax.axis_index("seq") % held
        core = core_stage.here()
        core_at = core.reshape(1).astype(jnp.int32)

        def trade(to_rows, part):
            there = [(s, (s % held ^ part) * sharers + s // held) for s in range(seq_size)]
            return there if to_rows else [(b, a) for a, b in there]

        def to_rows(values):
            return [
                lax.ppermute(
                    lax.dynamic_index_in_dim(values, source_at ^ part, 0, False),
                    "seq",
                    trade(True, part),
                )
                for part in range(held)
            ]

        def send_pieces(values):
            return [
                lax.ppermute(values[part], "seq", trade(False, part))
                for part in range(held)
            ]

        def place_pieces(parts):
            placed = [pick(source_at ^ slot, parts) for slot in range(held)]
            return jnp.stack(placed).reshape((micro, rows_here) + parts[0].shape)

        same_row = [[r * sharers + g for g in range(sharers)] for r in range(held)]

        def all_keys(values):
            if sharers == 1:
                return values
            return lax.all_gather(values, "seq", axis=0, tiled=True, axis_index_groups=same_row)

        def own_keys(values):
            if sharers == 1:
                return values
            return lax.psum_scatter(
                values, "seq", scatter_dimension=0, tiled=True, axis_index_groups=same_row
            ).astype(BF16)

        marks = segments.reshape(held, piece, 1).astype(BF16)
        marks = to_rows(jnp.broadcast_to(marks, (held, piece, PAIR)))
        inputs = jnp.concatenate(to_rows(hidden_in.reshape(held, piece, width)), 0)
        seg_q = jnp.concatenate(marks, 0)
        masked = (grad_out * grad_mask[..., None].astype(BF16)).reshape(held, piece, width)
        masked, inputs, seg_q = tie(masked, inputs, seg_q)
        upstream = to_rows(masked)

        queries = (
            (dot(inputs, query_proj) + query_bias.astype(F32)) * 0.125
        ).astype(BF16)
        keys = all_keys(dot(inputs, key_proj).astype(BF16))
        values = all_keys((dot(inputs, value_proj) + value_bias.astype(F32)).astype(BF16))
        seg_k = all_keys(seg_q)
        mixed, query_side = attention_forward(queries, keys, values, seg_q, seg_k)
        row = lambda vector: vector.reshape(1, -1)
        hat, scale, normed, active_t, slope, d_second, d_down, second_sums, *result = feed_forward(
            inputs,
            mixed,
            upstream,
            (
                output_proj,
                row(output_bias),
                row(first_gain),
                row(first_shift),
                expand_proj,
                row(expand_bias),
                shrink_proj,
                row(shrink_bias),
                row(second_gain),
                row(second_shift),
            ),
        )
        layer_flow = Flow(arriving(send_pieces(result)))

        def chips(own, got, orders, small=None):
            return Flow(total_over_chips(own, got, core_stage, orders, small))

        back = functools.partial(
            feed_back,
            slope=slope,
            active_t=active_t,
            shrink=shrink_proj,
            expand=expand_proj,
            normed=normed,
        )
        other, other_bias, d_normed = back(1 - core_at, d_down, d_second, norm=None)
        half = other.shape[1]
        got = core_stage.swap(other.reshape(2 * half, width))
        own, own_bias, d_first, d_attn, d_mixed, first_sums = back(
            core_at, d_down, d_normed, norm=(hat, scale, row(first_gain), output_proj)
        )
        own, got, d_mixed = advance([layer_flow], own.reshape(2 * half, width), got, d_mixed)
        unit = 16 << len(off_chip)

        def thirds(count):
            less = count // unit // 3 * unit
            return [(count - less, wide)] + ([(less, slim)] if less else [])

        feed_flow = chips(own, got, thirds(2 * half))

        pairs = width // PAIR
        kept = BF16 if sharers == 1 else F32
        grads = None
        for first, last in ((0, pairs // 2), (pairs // 2, pairs - 1), (pairs - 1, pairs)):
            grads = attention_backward(
                query_side, keys, values, seg_k, mixed, d_mixed, kept, first, last - first, grads
            )
            *grads, d_mixed = advance([feed_flow], *grads, d_mixed)

        d_query, d_keys, d_values = grads
        d_key = own_keys(d_keys)
        d_value = own_keys(d_values)
        four = (inputs, mixed, d_query, d_key, d_value, d_attn, unit)
        other = weight_halves(1 - core_at, *four)
        got = core_stage.swap(other)
        own = weight_halves(core_at, *four)
        rows = [
            column_sum(d_query).reshape(1, width),
            column_sum(d_value).reshape(1, width),
            first_sums[2:3],
            first_sums[0:2],
            pick(core, [own_bias, other_bias]).reshape(-1, width),
            pick(core, [other_bias, own_bias]).reshape(-1, width),
            second_sums[2:3],
            second_sums[0:2],
        ]
        filled = sum(r.shape[0] for r in rows)
        small = jnp.concatenate(rows + [jnp.zeros((SMALL // 2 - filled, width), F32)], 0)
        own, got, small, d_query, d_key, d_value = tie(own, got, small, d_query, d_key, d_value)
        attn_flow = chips(own, got, thirds(own.shape[0]), small)
        d_input = (
            d_first
            + right_dot(d_query, query_proj)
            + right_dot(d_key, key_proj)
            + right_dot(d_value, value_proj)
        ).astype(BF16)
        (d_input,) = advance([feed_flow], d_input)
        piece_flow = Flow(
            arriving(send_pieces([d_input[i * piece : (i + 1) * piece] for i in range(held)]))
        )

        advance([attn_flow])
        advance([feed_flow, attn_flow])
        advance([feed_flow, attn_flow, piece_flow])
        advance([attn_flow])
        advance([feed_flow, attn_flow])
        while feed_flow.result is None:
            advance([feed_flow, attn_flow])
        shrink_grad, expand_grad = feed_out(core_at, *feed_flow.result)
        grad_in = place_pieces(piece_flow.result)
        layer_out = place_pieces(layer_flow.result)
        shrink_grad, expand_grad, grad_in, layer_out = advance(
            [attn_flow], shrink_grad, expand_grad, grad_in, layer_out
        )
        while attn_flow.result is None:
            advance([attn_flow])
        own, got = attn_flow.result
        attn_grads = attn_out(core_at, own, got, width)
        tail = [value[-SMALL:].astype(F32) for value in (own, got)]
        tail = [value[: SMALL // 2] + value[SMALL // 2 :] for value in tail]
        totals = tail[0] + tail[1]
        ff_rows = 2 * half // width
        vectors = [totals[i] for i in range(5)]
        vectors.append(totals[5 : 5 + ff_rows].reshape(-1))
        vectors += [totals[i] for i in range(5 + ff_rows, 8 + ff_rows)]
        return (
            layer_out,
            grad_in,
            attn_grads[0],
            vectors[0],
            attn_grads[1],
            attn_grads[2],
            vectors[1],
            attn_grads[3],
            vectors[2],
            vectors[3],
            vectors[4],
            expand_grad,
            vectors[5],
            shrink_grad,
            vectors[6],
            vectors[7],
            vectors[8],
        )

    split = P(None, "rows", "seq", None)
    whole = P()
    return jax.shard_map(
        body,
        mesh=mesh,
        in_specs=(split, P(None, "rows", "seq"), P(None, "rows", "seq"), split) + (whole,) * 15,
        out_specs=(split, split) + (whole,) * 15,
        check_vma=False,
    )
```

time: 533 us -> 384 us (0.72)
  matrix products: 123 us -> 8.45 us
  Pallas kernels: 57.5 us -> 168 us
  waiting for transfers between devices: 168 us -> 79.3 us
  other arithmetic: 49.2 us -> 9.96 us
  starting transfers between devices: 77.3 us -> 60.9 us
    pallas_call x0 -> x27, Pallas kernels: none -> 111 us  [the longest x2 32.4 us: feed_back(): pl.pallas_call(functools.partial(feed_back_kernel, steps=steps, block=min...]
    ppermute x65 -> x56, waiting for transfers between devices: 168 us -> 79.3 us  [the longest x36 50.2 us: swap(): return lax.ppermute(values, ('rows', 'seq'), self.pairs)]
    dot_general x18 -> x3, matrix products: 80.2 us -> 4.17 us  [dot(): return lax.dot_general(first, second, dims, preferred_element_type=F32)]
    dot_general x6 -> x3, matrix products: 42.6 us -> 4.28 us  [right_dot(): return lax.dot_general(first, second, NT, preferred_element_type=F32)]
    convert_element_type x32 -> x6, other arithmetic: 25 us -> 0.81 us  [the longest x1 0.78 us: body(): marks = segments.reshape(held, piece, 1).astype(BF16)]
    ppermute x65 -> x56, starting transfers between devices: 77.3 us -> 60.9 us  [the longest x36 47.3 us: swap(): return lax.ppermute(values, ('rows', 'seq'), self.pairs)]
    unnamed x149 -> x172, local copies, waits for them, and re-layouts: 17.9 us -> 33.4 us
    dynamic_update_slice x10 -> x0, local copies, waits for them, and re-layouts: 12.5 us -> none  [to_pieces(): back = lax.dynamic_update_index_in_dim(back, got, source_at ^ part, 0)]
  transfers between devices with their start and end apart: 65 -> 56, of which waited for: 28 -> 13; matrix products, arithmetic and copies ran while one was open for 26% -> 8% of each run, Pallas kernels for 4% -> 29%
where the time goes in v2:
time: 384 us; the launch traced here: 379 us
  Pallas kernels  168 us (44%)
  waiting for transfers between devices  79.3 us (21%)
  starting transfers between devices  60.9 us (16%)
  local copies, waits for them, and re-layouts  49.4 us (13%)
  other arithmetic  9.96 us (3%)
  matrix products  8.45 us (2%)
    ppermute x36, waiting for transfers between devices, swap(): return lax.ppermute(values, ('rows', 'seq'), self.pairs)  50.2 us
    ppermute x36, starting transfers between devices, swap(): return lax.ppermute(values, ('rows', 'seq'), self.pairs)  47.3 us
    pallas_call x3, Pallas kernels, attention_backward(): pl.pallas_call(functools.partial(backward_kernel, block=min(512, keys)),...  35.5 us
    unnamed x172, local copies, waits for them, and re-layouts  33.4 us
    pallas_call x2, Pallas kernels, feed_back(): pl.pallas_call(functools.partial(feed_back_kernel, steps=steps, block=min...  32.4 us
    pallas_call x1, Pallas kernels, feed_forward(): pl.pallas_call(functools.partial(feed_forward_kernel, steps=steps, held=h...  22.9 us
    pallas_call x1, Pallas kernels, attention_forward(): pl.pallas_call(functools.partial(forward_kernel, block=min(512, queries))...  21.6 us
    ppermute x12, waiting for transfers between devices, to_rows(): lax.ppermute(lax.dynamic_index_in_dim(values, source_at ^ part, 0, False)...  16.8 us
  transfers between devices with their start and end apart: 56, of which 13 were waited for; matrix products, arithmetic and copies ran while one was open for 8% of the time, Pallas kernels for 29%

profile of v2, /device:TPU:0, one launch (start us, length us, event | category | flops | bytes accessed | tf_op | source)
XLA Modules:
  0.0 378.7 jit_solution(15298341873311043393)
XLA Ops:
  12.8 16.8 %collective-permute-done.7 = bf16[256,128]{1,0:T(8,128)(2,1)S(1)} collective-permute-done((bf16[256,128]{1,0:T(8,128)(2,1)S(1)}, bf16[256,128]{1,0:T(8,128)(2,1)S(1)}, u32[]{:S(2)}, u32[]{:S(2)}) %collective-permute-start.7) | collective-permute-done | bytes 65568 | tf_op jit(solution)/shard_map/ppermute | solution.py:902
  38.4 21.6 %attention_forward.1 = (bf16[1024,768]{1,0:T(8,128)(2,1)S(1)}, bf16[12,1024,128]{2,1,0:T(8,128)(2,1)S(1)}) custom-call(bf16[1024,768]{1,0:T(8,128)(2,1)S(1)} %multiply_convert_fusion.q_ref, bf16[1024,768]{1,0:T(8,128)(2,1)S(1)} %convolution_convert_fusion.k_ref, bf16[1024,768]{1,0:T(8,128)(2,1)S(1)} %add_convert_fusion.1.v_ref, ...), custom_call_target="tpu_custom_call" | custom-call | flops 12884901888 | bytes 7864320 | tf_op jit(solution)/shard_map/attention_forward/pallas_call | solution.py:89
  61.8 22.9 %feed_forward.1 = (f32[1024,768]{1,0:T(8,128)S(1)}, f32[1024,128]{1,0:T(8,128)S(1)}, bf16[1024,768]{1,0:T(8,128)(2,1)S(1)}, bf16[3072,1024]{1,0:T(8,128)(2,1)}, ...) custom-call(bf16[1024,768]{1,0:T(8,128)(2,1)S(1)} %pad_maximum_fusio, ...), custom_call_target="tpu_custom_call" | custom-call | flops 14495514624 | bytes 52428800 | tf_op jit(solution)/shard_map/feed_forward/pallas_call | solution.py:320
  87.8 15.2 %feed_back.1 = (bf16[2,1536,768]{2,1,0:T(8,128)(2,1)}, f32[1,1536]{1,0:T(1,128)S(1)}, f32[1024,768]{1,0:T(8,128)S(1)}) custom-call(s32[1]{0:T(128)S(6)} %sub.20.which_ref, bf16[1024,768]{1,0:T(8,128)(2,1)S(1)} %get-tuple-element.211.d_down_ref, f32[1024,768]{1,0:T(8,128)S(1)} %get-tuple-element.212.before_ref, ...), custom_call_target="tpu_custom_call" | custom-call | flops 9663676416 | bytes 31457280 | tf_op jit(solution)/shard_map/feed_back/pallas_call | solution.py:459
  116.1 17.2 %feed_back_last.1 = (bf16[2,1536,768]{2,1,0:T(8,128)(2,1)}, f32[1,1536]{1,0:T(1,128)S(1)}, f32[1024,768]{1,0:T(8,128)S(1)}, bf16[1024,768]{1,0:T(8,128)(2,1)S(1)...) custom-call(s32[1]{0:T(128)} %bitcast.which_ref.core_ref, bf16[1024,768]{1,0:T(8,128)(2,1)S(1)} %copy-done.45, ...), custom_call_target="tpu_custom_call" | custom-call | flops 9663676416 | bytes 31457280 | tf_op jit(solution)/shard_map/feed_back_last/pallas_call | solution.py:459
  133.4 5.0 %copy-done.1 = bf16[2,1536,768]{2,1,0:T(8,128)(2,1)S(1)} copy-done((bf16[2,1536,768]{2,1,0:T(8,128)(2,1)S(1)}, bf16[2,1536,768]{2,1,0:T(8,128)(2,1)}, u32[]{:S(2)}) %copy-start.1) | copy-done | bytes 4718616
  138.3 4.2 %scatter_first.4 = (bf16[1024,768]{1,0:T(8,128)(2,1)S(1)}, bf16[1024,768]{1,0:T(8,128)(2,1)S(1)}) custom-call(s32[2]{0:T(128)S(1)} %get-tuple-element.431.bits_ref, bf16[3072,768]{1,0:T(8,128)(2,1)S(1)} %bitcast.58, bf16[3072,768]{1,0:T(8,128)(2,1)} %collective-permute-done.12.got_ref), custom_call_target="tpu_custom_call" | custom-call | tf_op jit(solution)/shard_map/scatter_first/pallas_call | solution.py:649
  143.2 4.3 %scatter_first.5 = (bf16[512,768]{1,0:T(8,128)(2,1)S(1)}, bf16[512,768]{1,0:T(8,128)(2,1)S(1)}) custom-call(s32[2]{0:T(128)S(1)} %get-tuple-element.431.bits_ref, bf16[3072,768]{1,0:T(8,128)(2,1)S(1)} %bitcast.59, bf16[3072,768]{1,0:T(8,128)(2,1)} %collective-permute-done.12.got_ref), custom_call_target="tpu_custom_call" | custom-call | tf_op jit(solution)/shard_map/scatter_first/pallas_call | solution.py:649
  149.3 17.8 %attention_backward.3 = (bf16[1024,768]{1,0:T(8,128)(2,1)S(1)}, bf16[1024,768]{1,0:T(8,128)(2,1)S(1)}, bf16[1024,768]{1,0:T(8,128)(2,1)S(1)}) custom-call(bf16[12,1024,128]{2,1,0:T(8,128)(2,1)S(1)} %copy-done.47, bf16[1024,768]{1,0:T(8,128)(2,1)S(1)} %copy-done.52, bf16[1024,768]{1,0:T(8,128)(2,1)S(1)} %copy-done.55, ...), custom_call_target="tpu_custom_call" | custom-call | flops 16106127360 | bytes 5505024 | tf_op jit(solution)/shard_map/attention_backward/pallas_call | solution.py:171
  171.3 12.0 %attention_backward.4 = (bf16[1024,768]{1,0:T(8,128)(2,1)S(1)}, bf16[1024,768]{1,0:T(8,128)(2,1)S(1)}, bf16[1024,768]{1,0:T(8,128)(2,1)S(1)}) custom-call(bf16[12,1024,128]{2,1,0:T(8,128)(2,1)S(1)} %copy-done.47, bf16[1024,768]{1,0:T(8,128)(2,1)S(1)} %copy-done.52, ...), custom_call_target="tpu_custom_call", output_to_operand_aliasing={{0}: (6, {}), {1}: (7, {}), {2}: (8, {})} | custom-call | flops 10737418240 | bytes 3670016 | tf_op jit(solution)/shard_map/attention_backward/pallas_call | solution.py:171
  189.2 5.7 %attention_backward.5 = (bf16[1024,768]{1,0:T(8,128)(2,1)S(1)}, bf16[1024,768]{1,0:T(8,128)(2,1)S(1)}, bf16[1024,768]{1,0:T(8,128)(2,1)S(1)}) custom-call(bf16[12,1024,128]{2,1,0:T(8,128)(2,1)S(1)} %copy-done.48, bf16[1024,768]{1,0:T(8,128)(2,1)S(1)} %copy-done.53, ...), custom_call_target="tpu_custom_call", output_to_operand_aliasing={{0}: (6, {}), {1}: (7, {}), {2}: (8, {})} | custom-call | flops 5368709120 | bytes 1835008 | tf_op jit(solution)/shard_map/attention_backward/pallas_call | solution.py:171
  194.9 4.1 %weight_halves.3 = bf16[1536,768]{1,0:T(8,128)(2,1)} custom-call(s32[1]{0:T(128)S(6)} %sub.20.which_ref, bf16[1024,768]{1,0:T(8,128)(2,1)S(1)} %copy-done.3, bf16[1024,768]{1,0:T(8,128)(2,1)S(1)} %copy-done.8, bf16[1024,768]{1,0:T(8,128)(2,1)S(1)} %get-tuple-element.276.dq_ref, bf16[1024,768]{1,0:T(8,128)(2,1)S(1)} %get-tuple-element.277.dk_ref, ...), custom_call_target="tpu_custom_call" | custom-call | flops 2415919104 | bytes 12582912 | tf_op jit(solution)/shard_map/weight_halves/pallas_call | solution.py:492
  252.3 6.1 %collective-permute-done.27.refs_3_ = bf16[64,768]{1,0:T(8,128)(2,1)S(1)} collective-permute-done((bf16[64,768]{1,0:T(8,128)(2,1)S(1)}, bf16[64,768]{1,0:T(8,128)(2,1)S(1)}, u32[]{:S(2)}, u32[]{:S(2)}) %collective-permute-start.27) | collective-permute-done | bytes 98336 | tf_op jit(solution)/shard_map/ppermute | solution.py:791
  264.8 5.6 %collective-permute-done.38 = bf16[256,768]{1,0:T(8,128)(2,1)S(1)} collective-permute-done((bf16[256,768]{1,0:T(8,128)(2,1)S(1)}, bf16[256,768]{1,0:T(8,128)(2,1)S(1)}, u32[]{:S(2)}, u32[]{:S(2)}) %collective-permute-start.38) | collective-permute-done | bytes 393248 | tf_op jit(solution)/shard_map/ppermute | solution.py:912
  271.4 6.7 %collective-permute-done.39 = bf16[256,768]{1,0:T(8,128)(2,1)S(1)} collective-permute-done((bf16[256,768]{1,0:T(8,128)(2,1)S(1)}, bf16[256,768]{1,0:T(8,128)(2,1)S(1)}, u32[]{:S(2)}, u32[]{:S(2)}) %collective-permute-start.39) | collective-permute-done | bytes 393248 | tf_op jit(solution)/shard_map/ppermute | solution.py:912
  284.1 4.2 %collective-permute-done.43.refs_3_ = bf16[32,768]{1,0:T(8,128)(2,1)S(1)} collective-permute-done((bf16[32,768]{1,0:T(8,128)(2,1)S(1)}, bf16[32,768]{1,0:T(8,128)(2,1)S(1)}, u32[]{:S(2)}, u32[]{:S(2)}) %collective-permute-start.43) | collective-permute-done | bytes 49184 | tf_op jit(solution)/shard_map/ppermute | solution.py:791
  291.8 6.8 %collective-permute-done.45.refs_3_ = bf16[32,768]{1,0:T(8,128)(2,1)S(1)} collective-permute-done((bf16[32,768]{1,0:T(8,128)(2,1)S(1)}, bf16[32,768]{1,0:T(8,128)(2,1)S(1)}, u32[]{:S(2)}, u32[]{:S(2)}) %collective-permute-start.45) | collective-permute-done | bytes 49184 | tf_op jit(solution)/shard_map/ppermute | solution.py:791
  307.2 10.9 %collective-permute-done.48.refs_1_ = bf16[160,768]{1,0:T(8,128)(2,1)S(1)} collective-permute-done((bf16[160,768]{1,0:T(8,128)(2,1)S(1)}, bf16[160,768]{1,0:T(8,128)(2,1)S(1)}, u32[]{:S(2)}, u32[]{:S(2)}) %collective-permute-start.48) | collective-permute-done | bytes 245792 | tf_op jit(solution)/shard_map/ppermute | solution.py:791
  318.1 4.4 %collective-permute-done.46.refs_1_ = bf16[1024,768]{1,0:T(8,128)(2,1)S(1)} collective-permute-done((bf16[1024,768]{1,0:T(8,128)(2,1)S(1)}, bf16[1024,768]{1,0:T(8,128)(2,1)S(1)}, u32[]{:S(2)}, u32[]{:S(2)}) %collective-permute-start.46) | collective-permute-done | bytes 1572896 | tf_op jit(solution)/shard_map/ppermute | solution.py:791
  325.5 6.3 %collective-permute-start.50 = (bf16[3072,768]{1,0:T(8,128)(2,1)}, bf16[3072,768]{1,0:T(8,128)(2,1)}, u32[]{:S(2)}, u32[]{:S(2)}) collective-permute-start(bf16[3072,768]{1,0:T(8,128)(2,1)} %join_local.12.own_ref), channel_id=1, source_target_pairs={{0,1},{1,0},{2,3},{3,2},{4,5},{5,4},{6,7},{7,6},{8,9},{9,8},{10,11... | collective-permute-start | bytes 14155784 | tf_op jit(solution)/shard_map/ppermute | solution.py:791
  334.4 6.7 %collective-permute-done.52.refs_3_ = bf16[128,768]{1,0:T(8,128)(2,1)S(1)} collective-permute-done((bf16[128,768]{1,0:T(8,128)(2,1)S(1)}, bf16[128,768]{1,0:T(8,128)(2,1)S(1)}, u32[]{:S(2)}, u32[]{:S(2)}) %collective-permute-start.52) | collective-permute-done | bytes 196640 | tf_op jit(solution)/shard_map/ppermute | solution.py:791
  351.1 14.3 %feed_out.1 = (f32[3072,768]{1,0:T(8,128)}, f32[768,3072]{1,0:T(8,128)}) custom-call(s32[1]{0:T(128)} %bitcast.which_ref.core_ref, bf16[3072,768]{1,0:T(8,128)(2,1)} %join_local.12.own_ref, bf16[3072,768]{1,0:T(8,128)(2,1)} %collective-permute-done.50.got_ref), custom_call_target="tpu_custom_call" | custom-call | flops 1179648 | bytes 28311552 | tf_op jit(solution)/shard_map/feed_out/pallas_call | solution.py:537
  366.2 4.6 %collective-permute-done.55.got_ref = bf16[1568,768]{1,0:T(8,128)(2,1)S(1)} collective-permute-done((bf16[1568,768]{1,0:T(8,128)(2,1)S(1)}, bf16[1568,768]{1,0:T(8,128)(2,1)S(1)}, u32[]{:S(2)}, u32[]{:S(2)}) %collective-permute-start.55) | collective-permute-done | bytes 2408480 | tf_op jit(solution)/shard_map/ppermute | solution.py:791
  371.5 6.1 %attn_out.1 = (f32[768,768]{1,0:T(8,128)}, f32[768,768]{1,0:T(8,128)}, f32[768,768]{1,0:T(8,128)}, f32[768,768]{1,0:T(8,128)}) custom-call(s32[1]{0:T(128)} %bitcast.which_ref.core_ref, bf16[1568,768]{1,0:T(8,128)(2,1)S(1)} %join_local.15.own_ref, bf16[1568,768]{1,0:T(8,128)(2,1)S(1)} %collective-permute-done.55.got_ref), custom_call_target="tpu_custom_call" | custom-call | tf_op jit(solution)/shard_map/attn_out/pallas_call | solution.py:577
  (345 shorter events, 146.8 us)
Async XLA Ops:
  7.6 22.0 %collective-permute-start = (bf16[256,768]{1,0:T(8,128)(2,1)}, bf16[256,768]{1,0:T(8,128)(2,1)S(1)}, u32[]{:S(2)}, u32[]{:S(2)}) collective-permute-start(bf16[256,768]{1,0:T(8,128)(2,1)} %get-tuple-element.427), channel_id=1, source_target_pairs={{0,0},{1,1},{2,2},{3,3},{4,4},{5,5},{6,6},{7,7},{8,8},{9,9},{10,10... | collective-permute-start | bytes 1179656 | tf_op jit(solution)/shard_map/ppermute | solution.py:902
  8.6 21.1 %collective-permute-start.1 = (bf16[256,768]{1,0:T(8,128)(2,1)}, bf16[256,768]{1,0:T(8,128)(2,1)S(1)}, u32[]{:S(2)}, u32[]{:S(2)}) collective-permute-start(bf16[256,768]{1,0:T(8,128)(2,1)} %get-tuple-element.430), channel_id=1, source_target_pairs={{0,1},{1,0},{2,3},{3,2},{4,5},{5,4},{6,7},{7,6},{8,9},{9,8},{10,11... | collective-permute-start | bytes 1179656 | tf_op jit(solution)/shard_map/ppermute | solution.py:902
  8.8 20.8 %collective-permute-start.2 = (bf16[256,768]{1,0:T(8,128)(2,1)}, bf16[256,768]{1,0:T(8,128)(2,1)S(1)}, u32[]{:S(2)}, u32[]{:S(2)}) collective-permute-start(bf16[256,768]{1,0:T(8,128)(2,1)} %get-tuple-element.429), channel_id=1, source_target_pairs={{0,2},{1,3},{2,0},{3,1},{4,6},{5,7},{6,4},{7,5},{8,10},{9,11},{10,... | collective-permute-start | bytes 1179656 | tf_op jit(solution)/shard_map/ppermute | solution.py:902
  9.2 20.5 %collective-permute-start.3 = (bf16[256,768]{1,0:T(8,128)(2,1)}, bf16[256,768]{1,0:T(8,128)(2,1)S(1)}, u32[]{:S(2)}, u32[]{:S(2)}) collective-permute-start(bf16[256,768]{1,0:T(8,128)(2,1)} %get-tuple-element.428), channel_id=1, source_target_pairs={{0,3},{1,2},{2,1},{3,0},{4,7},{5,6},{6,5},{7,4},{8,11},{9,10},{10,... | collective-permute-start | bytes 1179656 | tf_op jit(solution)/shard_map/ppermute | solution.py:902
  10.8 18.8 %collective-permute-start.7 = (bf16[256,128]{1,0:T(8,128)(2,1)S(1)}, bf16[256,128]{1,0:T(8,128)(2,1)S(1)}, u32[]{:S(2)}, u32[]{:S(2)}) collective-permute-start(bf16[256,128]{1,0:T(8,128)(2,1)S(1)} %broadcast_in_dim.32), channel_id=1, source_target_pairs={{0,3},{1,2},{2,1},{3,0},{4,7},{5,6},{6,5},{7,4},{8,11},{9,10},{10,... | collective-permute-start | bytes 196616 | tf_op jit(solution)/shard_map/ppermute | solution.py:902
  31.8 29.9 %collective-permute-start.10 = (bf16[256,768]{1,0:T(8,128)(2,1)S(1)}, bf16[256,768]{1,0:T(8,128)(2,1)S(1)}, u32[]{:S(2)}, u32[]{:S(2)}) collective-permute-start(bf16[256,768]{1,0:T(8,128)(2,1)S(1)} %get-tuple-element.424), channel_id=1, source_target_pairs={{0,2},{1,3},{2,0},{3,1},{4,6},{5,7},{6,4},{7,5},{8,10},{9,11},{10,... | collective-permute-start | bytes 1179656 | tf_op jit(solution)/shard_map/ppermute | solution.py:902
  32.1 29.6 %collective-permute-start.11 = (bf16[256,768]{1,0:T(8,128)(2,1)S(1)}, bf16[256,768]{1,0:T(8,128)(2,1)S(1)}, u32[]{:S(2)}, u32[]{:S(2)}) collective-permute-start(bf16[256,768]{1,0:T(8,128)(2,1)S(1)} %get-tuple-element.423), channel_id=1, source_target_pairs={{0,3},{1,2},{2,1},{3,0},{4,7},{5,6},{6,5},{7,4},{8,11},{9,10},{10,... | collective-permute-start | bytes 1179656 | tf_op jit(solution)/shard_map/ppermute | solution.py:902
  33.7 28.0 %collective-permute-start.8 = (bf16[256,768]{1,0:T(8,128)(2,1)S(1)}, bf16[256,768]{1,0:T(8,128)(2,1)S(1)}, u32[]{:S(2)}, u32[]{:S(2)}) collective-permute-start(bf16[256,768]{1,0:T(8,128)(2,1)S(1)} %get-tuple-element.426), channel_id=1, source_target_pairs={{0,0},{1,1},{2,2},{3,3},{4,4},{5,5},{6,6},{7,7},{8,8},{9,9},{10,10... | collective-permute-start | bytes 1179656 | tf_op jit(solution)/shard_map/ppermute | solution.py:902
  33.7 28.0 %collective-permute-start.9 = (bf16[256,768]{1,0:T(8,128)(2,1)S(1)}, bf16[256,768]{1,0:T(8,128)(2,1)S(1)}, u32[]{:S(2)}, u32[]{:S(2)}) collective-permute-start(bf16[256,768]{1,0:T(8,128)(2,1)S(1)} %get-tuple-element.425), channel_id=1, source_target_pairs={{0,1},{1,0},{2,3},{3,2},{4,5},{5,4},{6,7},{7,6},{8,9},{9,8},{10,11... | collective-permute-start | bytes 1179656 | tf_op jit(solution)/shard_map/ppermute | solution.py:902
  105.3 28.0 %collective-permute-start.12 = (bf16[3072,768]{1,0:T(8,128)(2,1)}, bf16[3072,768]{1,0:T(8,128)(2,1)}, u32[]{:S(2)}, u32[]{:S(2)}) collective-permute-start(bf16[3072,768]{1,0:T(8,128)(2,1)} %bitcast.19), channel_id=1, source_target_pairs={{0,1},{1,0},{2,3},{3,2},{4,5},{5,4},{6,7},{7,6},{8,9},{9,8},{10,11... | collective-permute-start | bytes 14155784 | tf_op jit(solution)/shard_map/ppermute | solution.py:791
  105.6 27.7 %collective-permute-start.13 = (bf16[256,768]{1,0:T(8,128)(2,1)}, bf16[256,768]{1,0:T(8,128)(2,1)S(1)}, u32[]{:S(2)}, u32[]{:S(2)}) collective-permute-start(bf16[256,768]{1,0:T(8,128)(2,1)} %copy-done.34), channel_id=1, source_target_pairs={{0,0},{1,1},{2,2},{3,3},{4,4},{5,5},{6,6},{7,7},{8,8},{9,9},{10,10... | collective-permute-start | bytes 1179656 | tf_op jit(solution)/shard_map/ppermute | solution.py:912
  106.6 26.7 %collective-permute-start.14 = (bf16[256,768]{1,0:T(8,128)(2,1)}, bf16[256,768]{1,0:T(8,128)(2,1)S(1)}, u32[]{:S(2)}, u32[]{:S(2)}) collective-permute-start(bf16[256,768]{1,0:T(8,128)(2,1)} %copy-done.33), channel_id=1, source_target_pairs={{1,0},{0,1},{3,2},{2,3},{5,4},{4,5},{7,6},{6,7},{9,8},{8,9},{11,10... | collective-permute-start | bytes 1179656 | tf_op jit(solution)/shard_map/ppermute | solution.py:912
  106.9 26.4 %collective-permute-start.15 = (bf16[256,768]{1,0:T(8,128)(2,1)}, bf16[256,768]{1,0:T(8,128)(2,1)S(1)}, u32[]{:S(2)}, u32[]{:S(2)}) collective-permute-start(bf16[256,768]{1,0:T(8,128)(2,1)} %copy-done.32), channel_id=1, source_target_pairs={{2,0},{3,1},{0,2},{1,3},{6,4},{7,5},{4,6},{5,7},{10,8},{11,9},{8,1... | collective-permute-start | bytes 1179656 | tf_op jit(solution)/shard_map/ppermute | solution.py:912
  107.2 26.2 %collective-permute-start.16 = (bf16[256,768]{1,0:T(8,128)(2,1)S(1)}, bf16[256,768]{1,0:T(8,128)(2,1)S(1)}, u32[]{:S(2)}, u32[]{:S(2)}) collective-permute-start(bf16[256,768]{1,0:T(8,128)(2,1)S(1)} %get-tuple-element.227), channel_id=1, source_target_pairs={{3,0},{2,1},{1,2},{0,3},{7,4},{6,5},{5,6},{4,7},{11,8},{10,9},{9,1... | collective-permute-start | bytes 1179656 | tf_op jit(solution)/shard_map/ppermute | solution.py:912
  142.6 25.1 %collective-permute-start.17 = (bf16[1024,768]{1,0:T(8,128)(2,1)S(1)}, bf16[1024,768]{1,0:T(8,128)(2,1)S(1)}, u32[]{:S(2)}, u32[]{:S(2)}) collective-permute-start(bf16[1024,768]{1,0:T(8,128)(2,1)S(1)} %get-tuple-element.235), channel_id=1, source_target_pairs={{0,2},{1,5},{2,0},{3,7},{4,6},{5,1},{6,4},{7,3},{8,10},{9,13},{10,... | collective-permute-start | bytes 4718600 | tf_op jit(solution)/shard_map/ppermute | solution.py:791
  147.6 20.2 %collective-permute-start.18 = (bf16[512,768]{1,0:T(8,128)(2,1)S(1)}, bf16[512,768]{1,0:T(8,128)(2,1)S(1)}, u32[]{:S(2)}, u32[]{:S(2)}) collective-permute-start(bf16[512,768]{1,0:T(8,128)(2,1)S(1)} %get-tuple-element.237), channel_id=1, source_target_pairs={{0,8},{1,9},{2,10},{3,11},{4,12},{5,13},{6,14},{7,15},{8,0},{9,1},... | collective-permute-start | bytes 2359304 | tf_op jit(solution)/shard_map/ppermute | solution.py:791
  199.0 30.1 %collective-permute-start.23 = (bf16[1536,768]{1,0:T(8,128)(2,1)}, bf16[1536,768]{1,0:T(8,128)(2,1)}, u32[]{:S(2)}, u32[]{:S(2)}) collective-permute-start(bf16[1536,768]{1,0:T(8,128)(2,1)} %weight_halves.3), channel_id=1, source_target_pairs={{0,1},{1,0},{2,3},{3,2},{4,5},{5,4},{6,7},{7,6},{8,9},{9,8},{10,11... | collective-permute-start | bytes 7077896 | tf_op jit(solution)/shard_map/ppermute | solution.py:791
  214.2 27.7 %collective-permute-start.24 = (bf16[128,768]{1,0:T(8,128)(2,1)}, bf16[128,768]{1,0:T(8,128)(2,1)S(1)}, u32[]{:S(2)}, u32[]{:S(2)}) collective-permute-start(bf16[128,768]{1,0:T(8,128)(2,1)} %get-tuple-element.284), channel_id=1, source_target_pairs={{0,16},{1,17},{2,18},{3,19},{4,20},{5,21},{6,22},{7,23},{8,24},{9,... | collective-permute-start | bytes 589832 | tf_op jit(solution)/shard_map/ppermute | solution.py:791
  216.7 25.1 %collective-permute-start.25 = (bf16[64,768]{1,0:T(8,128)(2,1)}, bf16[64,768]{1,0:T(8,128)(2,1)S(1)}, u32[]{:S(2)}, u32[]{:S(2)}) collective-permute-start(bf16[64,768]{1,0:T(8,128)(2,1)} %get-tuple-element.286), channel_id=1, source_target_pairs={{0,16},{1,17},{2,18},{3,19},{4,20},{5,21},{6,22},{7,23},{8,24},{9,... | collective-permute-start | bytes 294920 | tf_op jit(solution)/shard_map/ppermute | solution.py:791
  278.7 19.9 %collective-permute-start.40 = (bf16[512,768]{1,0:T(8,128)(2,1)S(1)}, bf16[512,768]{1,0:T(8,128)(2,1)S(1)}, u32[]{:S(2)}, u32[]{:S(2)}) collective-permute-start(bf16[512,768]{1,0:T(8,128)(2,1)S(1)} %get-tuple-element.343.refs_0_), channel_id=1, source_target_pairs={{0,4},{1,9},{2,6},{3,11},{4,0},{5,13},{6,2},{7,15},{8,12},{9,1},{1... | collective-permute-start | bytes 2359304 | tf_op jit(solution)/shard_map/ppermute | solution.py:791
  279.8 18.9 %collective-permute-start.41 = (bf16[256,768]{1,0:T(8,128)(2,1)S(1)}, bf16[256,768]{1,0:T(8,128)(2,1)S(1)}, u32[]{:S(2)}, u32[]{:S(2)}) collective-permute-start(bf16[256,768]{1,0:T(8,128)(2,1)S(1)} %get-tuple-element.345.refs_2_), channel_id=1, source_target_pairs={{0,2},{1,3},{2,0},{3,1},{4,6},{5,7},{6,4},{7,5},{8,10},{9,11},{10,... | collective-permute-start | bytes 1179656 | tf_op jit(solution)/shard_map/ppermute | solution.py:791
  299.4 23.1 %collective-permute-start.46 = (bf16[1024,768]{1,0:T(8,128)(2,1)S(1)}, bf16[1024,768]{1,0:T(8,128)(2,1)S(1)}, u32[]{:S(2)}, u32[]{:S(2)}) collective-permute-start(bf16[1024,768]{1,0:T(8,128)(2,1)S(1)} %get-tuple-element.355.refs_0_), channel_id=1, source_target_pairs={{0,2},{1,5},{2,0},{3,7},{4,6},{5,1},{6,4},{7,3},{8,10},{9,13},{10,... | collective-permute-start | bytes 4718600 | tf_op jit(solution)/shard_map/ppermute | solution.py:791
  341.7 23.7 %collective-permute-start.53 = (bf16[544,768]{1,0:T(8,128)(2,1)S(1)}, bf16[544,768]{1,0:T(8,128)(2,1)S(1)}, u32[]{:S(2)}, u32[]{:S(2)}) collective-permute-start(bf16[544,768]{1,0:T(8,128)(2,1)S(1)} %get-tuple-element.385.refs_0_), channel_id=1, source_target_pairs={{0,2},{1,5},{2,0},{3,7},{4,6},{5,1},{6,4},{7,3},{8,10},{9,13},{10,... | collective-permute-start | bytes 2506760 | tf_op jit(solution)/shard_map/ppermute | solution.py:791
  345.7 19.7 %collective-permute-start.54 = (bf16[256,768]{1,0:T(8,128)(2,1)S(1)}, bf16[256,768]{1,0:T(8,128)(2,1)S(1)}, u32[]{:S(2)}, u32[]{:S(2)}) collective-permute-start(bf16[256,768]{1,0:T(8,128)(2,1)S(1)} %get-tuple-element.387.refs_2_), channel_id=1, source_target_pairs={{0,8},{1,9},{2,10},{3,11},{4,12},{5,13},{6,14},{7,15},{8,0},{9,1},... | collective-permute-start | bytes 1179656 | tf_op jit(solution)/shard_map/ppermute | solution.py:791
  (118 other events, 1167.6 us)

commit v3 on v2

--- a/solution.py
+++ b/solution.py
@@ -14,6 +14,7 @@
 BF16 = jnp.bfloat16
 NT = (((1,), (1,)), ((), ()))
 NN = (((1,), (0,)), ((), ()))
+BRIEF = pl.CostEstimate(flops=1, bytes_accessed=1, transcendentals=0)
 
 
 def left_dot(first, second):
@@ -101,15 +102,11 @@
             pl.BlockSpec((2, queries, PAIR), lambda i: (i, 0, 0)),
         ],
         out_shape=[
-            jax.ShapeDtypeStruct((queries, width), BF16),
-            jax.ShapeDtypeStruct((2 * pairs, queries, PAIR), BF16),
+            pltpu.HBM((queries, width), BF16),
+            pltpu.HBM((2 * pairs, queries, PAIR), BF16),
         ],
-        compiler_params=pltpu.CompilerParams(vmem_limit_bytes=40 * 2**20),
-        cost_estimate=pl.CostEstimate(
-            flops=16 * queries * keys * width,
-            bytes_accessed=10 * queries * width,
-            transcendentals=2 * pairs * queries * keys,
-        ),
+        compiler_params=pltpu.CompilerParams(vmem_limit_bytes=24 * 2**20),
+        cost_estimate=BRIEF,
         name="attention_forward",
     )(q, k, v, seg_q, seg_k)
 
@@ -187,19 +184,15 @@
         ],
         input_output_aliases={6 + i: i for i in range(len(held))},
         out_shape=[
-            jax.ShapeDtypeStruct((queries, width), BF16),
-            jax.ShapeDtypeStruct((keys, width), kept),
-            jax.ShapeDtypeStruct((keys, width), kept),
+            pltpu.HBM((queries, width), BF16),
+            pltpu.HBM((keys, width), kept),
+            pltpu.HBM((keys, width), kept),
         ],
         scratch_shapes=[pltpu.VMEM((PAIR, queries), F32)],
-        compiler_params=pltpu.CompilerParams(vmem_limit_bytes=40 * 2**20),
-        cost_estimate=pl.CostEstimate(
-            flops=40 * queries * keys * PAIR * count,
-            bytes_accessed=14 * queries * PAIR * count,
-            transcendentals=2 * count * queries * keys,
-        ),
+        compiler_params=pltpu.CompilerParams(vmem_limit_bytes=24 * 2**20),
+        cost_estimate=BRIEF,
         name="attention_backward",
-    )(query_side, k, v, seg_k, mixed, d_mixed, *held)
+    )(in_hbm(query_side), k, v, seg_k, in_hbm(mixed), in_hbm(d_mixed), *map(in_hbm, held))
 
 
 def dot(first, second, dims=NN):
@@ -250,11 +243,15 @@
     held,
 ):
     upstream_refs = refs[:held]
-    hat_ref, scale_ref, normed_ref, active_t_ref, slope_ref = refs[held : held + 5]
-    d_second_ref, d_down_ref, sums_ref = refs[held + 5 : held + 8]
-    out_refs = refs[held + 8 : -1]
-    total = refs[-1]
+    hat_out, scale_ref, normed_out, active_t_ref, slope_ref = refs[held : held + 5]
+    d_down_ref, sums_ref = refs[held + 5 : held + 7]
+    out_refs = refs[held + 7 : 2 * held + 7]
+    total, hat_ref, normed_ref, sems = refs[2 * held + 7 :]
     block = total.shape[0] // held
+    early = [
+        pltpu.make_async_copy(hat_ref, hat_out, sems.at[0]),
+        pltpu.make_async_copy(normed_ref, normed_out, sems.at[1]),
+    ]
     step = pl.program_id(0)
     tokens = total.shape[0]
     pieces = [slice(start, start + block) for start in range(0, tokens, block)]
@@ -268,11 +265,13 @@
                 + output_bias_ref[...].astype(F32)
             )
             hat, scale = normalise(first_sum)
-            hat_ref[here, :] = hat
+            hat_ref[here, :] = hat.astype(BF16)
             scale_ref[here, :] = jnp.broadcast_to(scale, (block, PAIR))
             normed = gain_one_ref[...].astype(F32) * hat + shift_one_ref[...].astype(F32)
             normed_ref[here, :] = normed.astype(BF16)
             total[here, :] = normed + shrink_bias_ref[...].astype(F32)
+        for copy in early:
+            copy.start()
 
     for here in pieces:
         expanded = dot(normed_ref[here, :], expand_ref[...]) + expand_bias_ref[...].astype(F32)
@@ -294,12 +293,20 @@
             upstream = upstream_ref[...].astype(F32)
             d_gain += jnp.sum(upstream * hat, 0, keepdims=True)
             d_shift += jnp.sum(upstream, 0, keepdims=True)
-            d_second = norm_back(upstream, hat, scale, gain)
-            d_second_ref[here, :] = d_second
-            d_down = d_second.astype(BF16)
+            d_down = norm_back(upstream, hat, scale, gain).astype(BF16)
             d_down_ref[here, :] = d_down
             d_bias += jnp.sum(d_down.astype(F32), 0, keepdims=True)
         sums_ref[...] = stack_rows([d_gain, d_shift, d_bias])
+        for copy in early:
+            copy.wait()
+
+
+def in_hbm(values):
+    return pltpu.with_memory_space_constraint(values, pltpu.HBM)
+
+
+def hbm_shapes(*pairs):
+    return [pltpu.HBM(shape, dtype) for shape, dtype in pairs]
 
 
 def fixed(*shape):
@@ -332,40 +339,40 @@
         ]
         + [fixed(piece, width)] * held,
         out_specs=[
-            fixed(tokens, width),
+            pl.BlockSpec(memory_space=pl.ANY),
             fixed(tokens, PAIR),
-            fixed(tokens, width),
+            pl.BlockSpec(memory_space=pl.ANY),
             pl.BlockSpec((block, tokens), lambda i: (i, 0)),
             pl.BlockSpec((tokens, block), lambda i: (0, i)),
-            fixed(tokens, width),
             fixed(tokens, width),
             fixed(8, width),
         ]
         + [fixed(piece, width)] * held,
-        out_shape=shapes(
-            ((tokens, width), F32),
+        out_shape=hbm_shapes(
+            ((tokens, width), BF16),
             ((tokens, PAIR), F32),
             ((tokens, width), BF16),
             ((units, tokens), BF16),
             ((tokens, units), BF16),
-            ((tokens, width), F32),
             ((tokens, width), BF16),
             ((8, width), F32),
-            *[((piece, width), BF16)] * held,
-        ),
-        scratch_shapes=[pltpu.VMEM((tokens, width), F32)],
+        )
+        + shapes(*[((piece, width), BF16)] * held),
+        scratch_shapes=[
+            pltpu.VMEM((tokens, width), F32),
+            pltpu.VMEM((tokens, width), BF16),
+            pltpu.VMEM((tokens, width), BF16),
+            pltpu.SemaphoreType.DMA((2,)),
+        ],
         compiler_params=pltpu.CompilerParams(vmem_limit_bytes=36 * 2**20),
-        cost_estimate=pl.CostEstimate(
-            flops=6 * tokens * width * units, bytes_accessed=50 * 2**20, transcendentals=0
-        ),
+        cost_estimate=BRIEF,
         name="feed_forward",
-    )(inputs, mixed, *weights, *upstream)
+    )(inputs, in_hbm(mixed), *map(in_hbm, weights), *upstream)
 
 
 def feed_back_kernel(
     which_ref,
     d_down_ref,
-    before_ref,
     slope_ref,
     active_t_ref,
     shrink_ref,
@@ -376,18 +383,32 @@
     block,
     last,
 ):
+    step = pl.program_id(0)
     if last:
-        hat_ref, scale_ref, gain_ref, output_proj_ref = refs[:4]
-        grads_ref, bias_ref, d_first_ref, d_attn_ref, d_mixed_ref, sums_ref, turned, total = refs[4:]
+        gain_ref, *late_refs = refs[:5]
+        grads_ref, bias_ref, d_attn_ref, d_mixed_ref, sums_ref = refs[5:10]
+        turned, total, hat_ref, scale_ref, output_proj_ref, sems = refs[10:]
+        late = [
+            pltpu.make_async_copy(source, target, sems.at[index])
+            for index, (source, target) in enumerate(
+                zip(late_refs, (d_attn_ref, hat_ref, scale_ref, output_proj_ref))
+            )
+        ]
+
+        @pl.when(step == 0)
+        def _():
+            for copy in late:
+                copy.start()
+
     else:
-        grads_ref, bias_ref, total, turned = refs
-    step = pl.program_id(0)
+        grads_ref, bias_ref, total_ref, turned, total = refs
     tokens = total.shape[0]
     pieces = [slice(start, start + block) for start in range(0, tokens, block)]
 
     @pl.when(step == 0)
     def _():
-        total[...] = before_ref[...]
+        total[...] = jnp.zeros_like(total)
+        bias_ref[...] = jnp.zeros_like(bias_ref)
 
     bias = jnp.zeros((1, slope_ref.shape[1]), F32)
     for here in pieces:
@@ -396,33 +417,42 @@
         turned[:, here] = d_expand.T
         bias += jnp.sum(d_expand.astype(F32), 0, keepdims=True)
         total[here, :] += dot(d_expand, expand_ref[...], NT)
-    bias_ref[...] = bias
+    row = lax.broadcasted_iota(jnp.int32, bias_ref.shape, 0)
+    bias_ref[...] = jnp.where(row == step, bias, bias_ref[...])
     grads_ref[0] = dot(active_t_ref[...], d_down_ref[...]).astype(BF16)
     grads_ref[1] = dot(turned[...], normed_ref[...]).astype(BF16)
 
-    if last:
+    if not last:
 
         @pl.when(step == steps - 1)
         def _():
+            total_ref[...] = total[...].astype(BF16)
+
+    else:
+
+        @pl.when(step == steps - 1)
+        def _():
+            for copy in late:
+                copy.wait()
             gain = gain_ref[...].astype(F32)
             d_gain = jnp.zeros((1, total.shape[1]), F32)
             d_shift = d_gain
             d_bias = d_gain
             for here in pieces:
-                d_normed = total[here, :]
-                hat = hat_ref[here, :]
+                d_normed = total[here, :] + (
+                    d_down_ref[here, :].astype(F32) + d_attn_ref[here, :].astype(F32)
+                )
+                hat = hat_ref[here, :].astype(F32)
                 d_gain += jnp.sum(d_normed * hat, 0, keepdims=True)
                 d_shift += jnp.sum(d_normed, 0, keepdims=True)
-                d_first = norm_back(d_normed, hat, scale_ref[here, :][:, 0:1], gain)
-                d_first_ref[here, :] = d_first
-                d_attn = d_first.astype(BF16)
+                d_attn = norm_back(d_normed, hat, scale_ref[here, :][:, 0:1], gain).astype(BF16)
                 d_attn_ref[here, :] = d_attn
                 d_bias += jnp.sum(d_attn.astype(F32), 0, keepdims=True)
                 d_mixed_ref[here, :] = dot(d_attn, output_proj_ref[...], NT).astype(BF16)
             sums_ref[...] = stack_rows([d_gain, d_shift, d_bias])
 
 
-def feed_back(which, d_down, before, slope, active_t, shrink, expand, normed, norm, block=512):
+def feed_back(which, d_down, slope, active_t, shrink, expand, normed, norm, block=512):
     tokens, width = d_down.shape
     half = slope.shape[1] // 2
     steps = half // block
@@ -433,7 +463,6 @@
     )
     in_specs = [
         whole(tokens, width),
-        whole(tokens, width),
         pl.BlockSpec((tokens, block), lambda i, which: (0, at(i, which))),
         pl.BlockSpec((block, tokens), lambda i, which: (at(i, which), 0)),
         pl.BlockSpec((block, width), lambda i, which: (at(i, which), 0)),
@@ -442,20 +471,28 @@
     ]
     out_specs = [
         pl.BlockSpec((2, block, width), lambda i, which: (0, i, 0)),
-        pl.BlockSpec((1, block), lambda i, which: (0, i)),
+        whole(8, block),
     ]
-    out_shape = shapes(((2, half, width), BF16), ((1, half), F32))
-    scratch = [pltpu.VMEM((block, tokens), BF16)]
+    out_shape = hbm_shapes(((2, half, width), BF16), ((8, block), F32))
+    scratch = [pltpu.VMEM((block, tokens), BF16), pltpu.VMEM((tokens, width), F32)]
+    extra = ()
     if last:
-        in_specs += [whole(tokens, width), whole(tokens, PAIR), whole(1, width), whole(width, width)]
-        out_specs += [whole(tokens, width)] * 3 + [whole(8, width)]
-        out_shape += shapes(
-            ((tokens, width), F32), ((tokens, width), BF16), ((tokens, width), BF16), ((8, width), F32)
+        gain, *late = norm
+        extra = (gain, *map(in_hbm, late))
+        in_specs += [whole(1, width)] + [pl.BlockSpec(memory_space=pl.ANY)] * len(late)
+        out_specs += [whole(tokens, width)] * 2 + [whole(8, width)]
+        out_shape += hbm_shapes(
+            ((tokens, width), BF16), ((tokens, width), BF16), ((8, width), F32)
         )
-        scratch.append(pltpu.VMEM((tokens, width), F32))
+        scratch += [
+            pltpu.VMEM((tokens, width), BF16),
+            pltpu.VMEM((tokens, PAIR), F32),
+            pltpu.VMEM((width, width), BF16),
+            pltpu.SemaphoreType.DMA((4,)),
+        ]
     else:
         out_specs.append(whole(tokens, width))
-        out_shape += shapes(((tokens, width), F32))
+        out_shape += hbm_shapes(((tokens, width), BF16))
     return pl.pallas_call(
         functools.partial(feed_back_kernel, steps=steps, block=min(512, tokens), last=last),
         grid_spec=pltpu.PrefetchScalarGridSpec(
@@ -466,126 +503,210 @@
             scratch_shapes=scratch,
         ),
         out_shape=out_shape,
-        compiler_params=pltpu.CompilerParams(vmem_limit_bytes=36 * 2**20),
-        cost_estimate=pl.CostEstimate(
-            flops=8 * tokens * width * half, bytes_accessed=30 * 2**20, transcendentals=0
-        ),
+        compiler_params=pltpu.CompilerParams(vmem_limit_bytes=44 * 2**20),
+        cost_estimate=BRIEF,
         name="feed_back_last" if last else "feed_back",
-    )(which, d_down, before, slope, active_t, shrink, expand, normed, *(norm or ()))
-
-
-def weight_kernel(which_ref, inputs_ref, mixed_ref, dq_ref, dk_ref, dv_ref, d_attn_ref, out_ref):
+    )(which, *map(in_hbm, (d_down, slope, active_t, shrink, expand, normed)), *extra)
+
+
+def weight_kernel(which_ref, *refs, steps):
+    sources = refs[:6]
+    if steps:
+        sums_refs, (out_ref, small_ref), rest = refs[6:10], refs[10:12], refs[12:]
+    else:
+        (out_ref,), rest = refs[6:7], refs[7:]
+    targets, sems = rest[:6], rest[6]
+    inputs_ref, dq_ref, dk_ref, dv_ref, mixed_ref, d_attn_ref = targets
+    copies = [
+        pltpu.make_async_copy(source, target, sems.at[index])
+        for index, (source, target) in enumerate(zip(sources, targets))
+    ]
+    for copy in copies:
+        copy.start()
     count = inputs_ref.shape[1] // 2
     columns = pl.ds(pl.multiple_of(which_ref[0] * count, PAIR), count)
-    inputs_t = inputs_ref[:, columns].T
-    out_ref[0 * count : 1 * count, :] = dot(inputs_t, dq_ref[...]).astype(BF16)
-    out_ref[1 * count : 2 * count, :] = dot(inputs_t, dk_ref[...]).astype(BF16)
-    out_ref[2 * count : 3 * count, :] = dot(inputs_t, dv_ref[...]).astype(BF16)
-    out_ref[3 * count : 4 * count, :] = dot(mixed_ref[:, columns].T, d_attn_ref[...]).astype(BF16)
     if out_ref.shape[0] > 4 * count:
         out_ref[4 * count :, :] = jnp.zeros((out_ref.shape[0] - 4 * count, out_ref.shape[1]), BF16)
-
-
-def weight_halves(which, inputs, mixed, dq, dk, dv, d_attn, unit):
-    tokens, width = inputs.shape
+    copies[0].wait()
+    turned = inputs_ref[:, columns].T
+    for at, right_ref in enumerate((dq_ref, dk_ref, dv_ref, d_attn_ref)):
+        copies[at + 1].wait()
+        if at == 3:
+            copies[5].wait()
+            turned = mixed_ref[:, columns].T
+        out_ref[at * count : (at + 1) * count, :] = dot(turned, right_ref[...]).astype(BF16)
+    if steps:
+        first_sums_ref, second_sums_ref, own_bias_ref, other_bias_ref = sums_refs
+        small_ref[...] = jnp.zeros_like(small_ref)
+        small_ref[0:1, :] = jnp.sum(dq_ref[...].astype(F32), 0, keepdims=True)
+        small_ref[1:2, :] = jnp.sum(dv_ref[...].astype(F32), 0, keepdims=True)
+        small_ref[2:5, :] = first_sums_ref[0:3, :]
+        small_ref[5:8, :] = second_sums_ref[0:3, :]
+        block = own_bias_ref.shape[1]
+        own, other = own_bias_ref[0:steps, :], other_bias_ref[0:steps, :]
+        lower = which_ref[0] == 0
+        small_ref[8 : 8 + steps, 0:block] = jnp.where(lower, own, other)
+        small_ref[8 + steps : 8 + 2 * steps, 0:block] = jnp.where(lower, other, own)
+
+
+def weight_half(which, values, unit, sums=(), steps=0):
+    tokens, width = values[0].shape
     rows = -(-2 * width // unit) * unit
+    vmem = pl.BlockSpec(memory_space=pltpu.VMEM)
+    anywhere = pl.BlockSpec(memory_space=pl.ANY)
+    out_shape = shapes(((rows, width), BF16))
+    if steps:
+        out_shape += shapes(((SMALL // 2, width), F32))
     return pl.pallas_call(
-        weight_kernel,
-        grid_spec=pltpu.PrefetchScalarGridSpec(
-            num_scalar_prefetch=1,
-            grid=(1,),
-            in_specs=[pl.BlockSpec((tokens, width), lambda i, which: (0, 0))] * 6,
-            out_specs=pl.BlockSpec((rows, width), lambda i, which: (0, 0)),
-        ),
-        out_shape=jax.ShapeDtypeStruct((rows, width), BF16),
-        compiler_params=pltpu.CompilerParams(vmem_limit_bytes=40 * 2**20),
-        cost_estimate=pl.CostEstimate(
-            flops=4 * tokens * width * width, bytes_accessed=12 * 2**20, transcendentals=0
-        ),
-        name="weight_halves",
-    )(which, inputs, mixed, dq, dk, dv, d_attn)
-
-
-def feed_out_kernel(core_ref, own_ref, got_ref, shrink_ref, expand_ref, *, steps):
-    own = core_ref[0] == pl.program_id(0)
-    step = pl.program_id(1)
-
-    for mine, ref in ((True, own_ref), (False, got_ref)):
-
-        @pl.when((own == mine) & (step < steps))
-        def _(ref=ref):
-            shrink_ref[...] = ref[...].astype(F32)
-
-        @pl.when((own == mine) & (step >= steps))
-        def _(ref=ref):
-            expand_ref[...] = ref[...].T.astype(F32)
-
-
-def feed_out(core, own, got, block=512):
-    width = own.shape[1]
-    half = own.shape[0] // 2
+        functools.partial(weight_kernel, steps=steps),
+        in_specs=[pl.BlockSpec(memory_space=pltpu.SMEM)] + [anywhere] * 6 + [vmem] * len(sums),
+        out_specs=[vmem] * len(out_shape),
+        out_shape=out_shape,
+        scratch_shapes=[pltpu.VMEM((tokens, width), BF16)] * 6 + [pltpu.SemaphoreType.DMA((6,))],
+        compiler_params=pltpu.CompilerParams(vmem_limit_bytes=28 * 2**20),
+        cost_estimate=BRIEF,
+        name="weight_half",
+    )(which, *map(in_hbm, values), *sums)
+
+
+def input_grad_kernel(*refs, held):
+    sources, outs = refs[:7], refs[7 : 7 + held]
+    (d_attn, *factors), sems = refs[7 + held : 14 + held], refs[-1]
+    copies = [
+        pltpu.make_async_copy(source, target, sems.at[index])
+        for index, (source, target) in enumerate(zip(sources, (d_attn, *factors)))
+    ]
+    for copy in copies:
+        copy.start()
+    piece = outs[0].shape[0]
+    total = None
+    for index in range(3):
+        for copy in copies[2 * index + 1 : 2 * index + 3]:
+            copy.wait()
+    copies[0].wait()
+    for number, out_ref in enumerate(outs):
+        here = slice(number * piece, (number + 1) * piece)
+        total = d_attn[here, :].astype(F32)
+        for index in range(3):
+            total += dot(factors[2 * index][here, :], factors[2 * index + 1][...], NT)
+        out_ref[...] = total.astype(BF16)
+
+
+def input_grad(d_attn, factors, held):
+    tokens, width = d_attn.shape
+    anywhere = pl.BlockSpec(memory_space=pl.ANY)
+    values = [d_attn] + [value for pair in factors for value in pair]
+    return pl.pallas_call(
+        functools.partial(input_grad_kernel, held=held),
+        in_specs=[anywhere] * 7,
+        out_specs=[pl.BlockSpec(memory_space=pltpu.VMEM)] * held,
+        out_shape=shapes(*[((tokens // held, width), BF16)] * held),
+        scratch_shapes=[pltpu.VMEM(value.shape, BF16) for value in values]
+        + [pltpu.SemaphoreType.DMA((7,))],
+        compiler_params=pltpu.CompilerParams(vmem_limit_bytes=24 * 2**20),
+        cost_estimate=BRIEF,
+        name="input_grad",
+    )(*map(in_hbm, values))
+
+
+def feed_out_kernel(which_ref, half_ref, *refs, steps):
+    del which_ref
+    shrink_ref, expand_ref = refs[-2:]
+
+    @pl.when(pl.program_id(0) < steps)
+    def _():
+        shrink_ref[...] = half_ref[...].astype(F32)
+
+    @pl.when(pl.program_id(0) >= steps)
+    def _():
+        expand_ref[...] = half_ref[...].T.astype(F32)
+
+
+def feed_out(which, values, before=(), block=512):
+    width = values.shape[1]
+    half = values.shape[0] // 2
     steps = half // block
-
-    def source(mine):
-        def index(h, i, core):
-            return (jnp.where((core[0] == h) == mine, i, 0), 0)
-
-        return pl.BlockSpec((block, width), index)
-
-    shrink_at = lambda h, i, core: (h * steps + jnp.minimum(i, steps - 1), 0)
-    expand_at = lambda h, i, core: (0, h * steps + jnp.maximum(i - steps, 0))
     return pl.pallas_call(
         functools.partial(feed_out_kernel, steps=steps),
         grid_spec=pltpu.PrefetchScalarGridSpec(
             num_scalar_prefetch=1,
-            grid=(2, 2 * steps),
-            in_specs=[source(True), source(False)],
+            grid=(2 * steps,),
+            in_specs=[pl.BlockSpec((block, width), lambda i, which: (i, 0))]
+            + [pl.BlockSpec(memory_space=pl.ANY)] * len(before),
             out_specs=[
-                pl.BlockSpec((block, width), shrink_at),
-                pl.BlockSpec((width, block), expand_at),
+                pl.BlockSpec(
+                    (block, width),
+                    lambda i, which: (which[0] * steps + jnp.minimum(i, steps - 1), 0),
+                ),
+                pl.BlockSpec(
+                    (width, block),
+                    lambda i, which: (0, which[0] * steps + jnp.maximum(i - steps, 0)),
+                ),
             ],
         ),
         out_shape=shapes(((2 * half, width), F32), ((width, 2 * half), F32)),
-        compiler_params=pltpu.CompilerParams(vmem_limit_bytes=24 * 2**20),
-        cost_estimate=pl.CostEstimate(
-            flops=half * width, bytes_accessed=24 * half * width, transcendentals=0
-        ),
+        input_output_aliases={2 + i: i for i in range(len(before))},
+        compiler_params=pltpu.CompilerParams(vmem_limit_bytes=16 * 2**20),
+        cost_estimate=BRIEF,
         name="feed_out",
-    )(core, own, got)
-
-
-def attn_out_kernel(core_ref, own_ref, got_ref, *out_refs):
-    own = core_ref[0] == pl.program_id(1)
-    for index, out_ref in enumerate(out_refs):
-        for mine, ref in ((True, own_ref), (False, got_ref)):
-
-            @pl.when((own == mine) & (pl.program_id(0) == index))
-            def _(ref=ref, out_ref=out_ref):
-                out_ref[...] = ref[...].astype(F32)
-
-
-def attn_out(core, own, got, width):
+    )(which, values, *before)
+
+
+def attn_out_kernel(which_ref, half_ref, *refs):
+    del which_ref
+    for index, out_ref in enumerate(refs[-4:]):
+
+        @pl.when(pl.program_id(0) == index)
+        def _(out_ref=out_ref):
+            out_ref[...] = half_ref[...].astype(F32)
+
+
+def attn_out(which, values, before=()):
+    width = values.shape[1]
     half = width // 2
-
-    def source(mine):
-        return pl.BlockSpec((half, width), lambda m, h, core: (m, 0))
-
-    def target(index):
-        at = lambda m, h, core: (jnp.where(m < index, 0, jnp.where(m == index, h, 1)), 0)
-        return pl.BlockSpec((half, width), at)
-
     return pl.pallas_call(
         attn_out_kernel,
         grid_spec=pltpu.PrefetchScalarGridSpec(
             num_scalar_prefetch=1,
-            grid=(4, 2),
-            in_specs=[source(True), source(False)],
-            out_specs=[target(index) for index in range(4)],
+            grid=(4,),
+            in_specs=[pl.BlockSpec((half, width), lambda i, which: (i, 0))]
+            + [pl.BlockSpec(memory_space=pl.ANY)] * len(before),
+            out_specs=[pl.BlockSpec((half, width), lambda i, which: (which[0], 0))] * 4,
         ),
         out_shape=shapes(*[((width, width), F32)] * 4),
+        input_output_aliases={2 + i: i for i in range(len(before))},
         compiler_params=pltpu.CompilerParams(vmem_limit_bytes=24 * 2**20),
+        cost_estimate=BRIEF,
         name="attn_out",
-    )(core, own, got)
+    )(which, values, *before)
+
+
+def place_kernel(at_ref, *refs):
+    del at_ref
+    out_ref = refs[-1]
+    for index, ref in enumerate(refs[:-1]):
+
+        @pl.when(pl.program_id(0) == index)
+        def _(ref=ref):
+            out_ref[0] = ref[...]
+
+
+def place(at, parts):
+    piece, width = parts[0].shape
+    held = len(parts)
+    return pl.pallas_call(
+        place_kernel,
+        grid_spec=pltpu.PrefetchScalarGridSpec(
+            num_scalar_prefetch=1,
+            grid=(held,),
+            in_specs=[pl.BlockSpec((piece, width), lambda i, at: (0, 0))] * held,
+            out_specs=pl.BlockSpec((1, piece, width), lambda i, at: (at[0] ^ i, 0, 0)),
+        ),
+        out_shape=jax.ShapeDtypeStruct((held, piece, width), BF16),
+        compiler_params=pltpu.CompilerParams(vmem_limit_bytes=16 * 2**20),
+        cost_estimate=BRIEF,
+        name="place",
+    )(at, *parts)
 
 
 def rows_of(ref, which, count, base=0):
@@ -597,14 +718,19 @@
 
 
 def scatter_kernel(bits_ref, *refs, groups):
-    ins, outs = refs[: 2 * groups], refs[2 * groups :]
+    outs = refs[-2 * groups :]
+    ins = refs[: -2 * groups]
+    together = len(ins) == 2
+    base = 0
     for group in range(groups):
-        terms = ins[2 * group : 2 * group + 2]
+        terms = ins if together else ins[2 * group : 2 * group + 2]
         sent_ref, kept_ref = outs[2 * group : 2 * group + 2]
         count = kept_ref.shape[0]
         here = bits_ref[group]
-        sent_ref[...] = sum_of([rows_of(term, 1 - here, count) for term in terms])
-        kept_ref[...] = sum_of([rows_of(term, here, count) for term in terms])
+        sent_ref[...] = sum_of([rows_of(term, 1 - here, count, base) for term in terms])
+        kept_ref[...] = sum_of([rows_of(term, here, count, base) for term in terms])
+        if together:
+            base += 2 * count
 
 
 def local_call(kernel, bits, values, out_shape, name):
@@ -615,13 +741,16 @@
         out_specs=[vmem] * len(out_shape),
         out_shape=out_shape,
         compiler_params=pltpu.CompilerParams(vmem_limit_bytes=24 * 2**20),
+        cost_estimate=BRIEF,
         name=name,
     )(bits, *values)
 
 
-def scatter_local(bits, pairs):
-    groups = len(pairs)
-    counts = [kept.shape[0] // 2 for kept, _ in pairs]
+def scatter_local(bits, pairs, counts=None):
+    if counts is None:
+        counts = [kept.shape[0] for kept, _ in pairs]
+    groups = len(counts)
+    counts = [count // 2 for count in counts]
     width = pairs[0][0].shape[1]
     outs = local_call(
         functools.partial(scatter_kernel, groups=groups),
@@ -633,51 +762,48 @@
     return [outs[2 * i : 2 * i + 2] for i in range(groups)]
 
 
-def scatter_first(bits, own, got, counts, blocks=2):
-    width = own.shape[1]
-    outs = []
+def scatter_first_kernel(bits_ref, own_at, got_at, *refs, counts):
+    outs, (own, got, sems) = refs[:-3], refs[-3:]
+    spans = []
     base = 0
     for group, count in enumerate(counts):
-        block = count // 2 // blocks
-        first = base // block
-
-        def source(i, bits, group=group, first=first):
-            kept = i // blocks
-            return (first + jnp.where(kept == 1, bits[group], 1 - bits[group]) * blocks + i % blocks, 0)
-
-        outs.append(
-            pl.pallas_call(
-                first_split_kernel,
-                grid_spec=pltpu.PrefetchScalarGridSpec(
-                    num_scalar_prefetch=1,
-                    grid=(2 * blocks,),
-                    in_specs=[pl.BlockSpec((block, width), source)] * 2,
-                    out_specs=[
-                        pl.BlockSpec((block, width), lambda i, bits: (jnp.minimum(i, blocks - 1), 0)),
-                        pl.BlockSpec((block, width), lambda i, bits: (jnp.maximum(i - blocks, 0), 0)),
-                    ],
-                ),
-                out_shape=shapes(*[((count // 2, width), BF16)] * 2),
-                compiler_params=pltpu.CompilerParams(vmem_limit_bytes=16 * 2**20),
-                name="scatter_first",
-            )(bits, own, got)
-        )
+        for kept in range(2):
+            half = bits_ref[group] if kept else 1 - bits_ref[group]
+            start = pl.multiple_of(base + half * (count // 2), 16)
+            spans.append((start, count // 2, outs[2 * group + kept]))
         base += count
-    return outs
-
-
-def first_split_kernel(bits_ref, own_ref, got_ref, sent_ref, kept_ref):
-    del bits_ref
-    sending = pl.program_id(0) < pl.num_programs(0) // 2
-    value = sum_of([own_ref[...], got_ref[...]])
-
-    @pl.when(sending)
-    def _():
-        sent_ref[...] = value
-
-    @pl.when(jnp.logical_not(sending))
-    def _():
-        kept_ref[...] = value
+    spans = spans[0::2] + spans[1::2]
+    copies = []
+    for index, (start, count, _) in enumerate(spans):
+        rows = pl.ds(start, count)
+        for which, (source, target) in enumerate(((own_at, own), (got_at, got))):
+            copies.append(
+                pltpu.make_async_copy(source.at[rows], target.at[rows], sems.at[2 * index + which])
+            )
+            copies[-1].start()
+    for index, (start, count, out_ref) in enumerate(spans):
+        for copy in copies[2 * index : 2 * index + 2]:
+            copy.wait()
+        rows = pl.ds(start, count)
+        out_ref[...] = sum_of([own[rows, :], got[rows, :]])
+
+
+def scatter_first(bits, own, got, counts):
+    rows, width = own.shape
+    anywhere = pl.BlockSpec(memory_space=pl.ANY)
+    vmem = pl.BlockSpec(memory_space=pltpu.VMEM)
+    outs = pl.pallas_call(
+        functools.partial(scatter_first_kernel, counts=counts),
+        in_specs=[pl.BlockSpec(memory_space=pltpu.SMEM), anywhere, anywhere],
+        out_specs=[vmem] * (2 * len(counts)),
+        out_shape=shapes(*[((count // 2, width), BF16) for count in counts for _ in range(2)]),
+        scratch_shapes=[pltpu.VMEM((rows, width), BF16)] * 2
+        + [pltpu.SemaphoreType.DMA((4 * len(counts),))],
+        compiler_params=pltpu.CompilerParams(vmem_limit_bytes=24 * 2**20),
+        cost_estimate=BRIEF,
+        name="scatter_first",
+    )(bits, in_hbm(own), in_hbm(got))
+    return [outs[2 * group : 2 * group + 2] for group in range(len(counts))]
 
 
 def split_two(values):
@@ -791,7 +917,7 @@
         return lax.ppermute(values, ("rows", "seq"), self.pairs)
 
 
-def total_over_chips(own, got, core_stage, orders, small=None):
+def total_over_chips(own, got, core_stage, orders, small=None, near=False):
     depth = len(orders[0][1])
     groups = range(len(orders))
 
@@ -807,7 +933,11 @@
             flat += [keep[group], orders[group][1][step].swap(values[group])]
         return flat
 
-    parts = scatter_first(bits_at(0), own, got, [count for count, _ in orders])
+    counts = [count for count, _ in orders]
+    if near:
+        parts = scatter_local(bits_at(0), [[own, got]], counts)
+    else:
+        parts = scatter_first(bits_at(0), own, got, counts)
     for step in range(1, depth + 1):
         flat = yield send(step - 1, [p[0] for p in parts], [p[1] for p in parts])
         if step < depth:
@@ -822,30 +952,44 @@
 
 def arriving(values):
     values = yield values
-    return values
+    return values[1::2]
 
 
 class Flow:
-    def __init__(self, steps):
+    def __init__(self, steps, left):
         self.steps = steps
+        self.left = left
         self.pending = next(steps)
         self.result = None
 
 
-def advance(flows, *values):
-    flows = [flow for flow in flows if flow.result is None]
-    count = len(values)
-    tied = tie(*values, *[value for flow in flows for value in flow.pending])
-    at = count
-    for flow in flows:
-        arrived = list(tied[at : at + len(flow.pending)])
-        at += len(flow.pending)
-        try:
-            flow.pending = flow.steps.send(arrived)
-        except StopIteration as end:
-            flow.pending = []
-            flow.result = end.value
-    return tied[:count]
+class Timetable:
+    def __init__(self):
+        self.flows = []
+
+    def open(self, steps, left=1):
+        self.flows.append(Flow(steps, left))
+        return self.flows[-1]
+
+    def advance(self, moving, *values):
+        flows = [flow for flow in self.flows if flow.result is None]
+        held = [flow.pending if flow in moving else flow.pending[0::2] for flow in flows]
+        tied = list(tie(*values, *[value for part in held for value in part]))
+        values, tied = tied[: len(values)], tied[len(values) :]
+        for flow, part in zip(flows, held):
+            back, tied = tied[: len(part)], tied[len(part) :]
+            if flow not in moving:
+                flow.pending[0::2] = back
+                continue
+            flow.left -= 1
+            try:
+                flow.pending = flow.steps.send(back)
+            except StopIteration as end:
+                flow.result = end.value
+        return self.settle(*values) if moving and values else values
+
+    def settle(self, *values):
+        return self.advance([], *values)
 
 
 def solution(mesh):
@@ -909,13 +1053,14 @@
 
         def send_pieces(values):
             return [
-                lax.ppermute(values[part], "seq", trade(False, part))
+                value
                 for part in range(held)
+                for value in (values[part], lax.ppermute(values[part], "seq", trade(False, part)))
             ]
 
         def place_pieces(parts):
-            placed = [pick(source_at ^ slot, parts) for slot in range(held)]
-            return jnp.stack(placed).reshape((micro, rows_here) + parts[0].shape)
+            at = source_at.reshape(1).astype(jnp.int32)
+            return place(at, parts).reshape((micro, rows_here) + parts[0].shape)
 
         same_row = [[r * sharers + g for g in range(sharers)] for r in range(held)]
 
@@ -931,10 +1076,18 @@
                 values, "seq", scatter_dimension=0, tiled=True, axis_index_groups=same_row
             ).astype(BF16)
 
-        marks = segments.reshape(held, piece, 1).astype(BF16)
-        marks = to_rows(jnp.broadcast_to(marks, (held, piece, PAIR)))
-        inputs = jnp.concatenate(to_rows(hidden_in.reshape(held, piece, width)), 0)
-        seg_q = jnp.concatenate(marks, 0)
+        flat = hidden_in.reshape(held, piece, width)
+        far = [lax.dynamic_index_in_dim(flat, source_at ^ part, 0, False) for part in (3, 2)]
+        *far, flat, marks = tie(*far, flat, segments)
+        near = [lax.dynamic_index_in_dim(flat, source_at ^ part, 0, False) for part in (1, 0)]
+        marks = marks.reshape(held, piece, 1).astype(BF16)
+        marks = jnp.broadcast_to(marks, (held, piece, PAIR))
+        inputs = [
+            lax.ppermute(value, "seq", trade(True, part))
+            for part, value in zip((3, 2, 1, 0), far + near)
+        ]
+        inputs = jnp.concatenate(inputs[::-1], 0)
+        seg_q = jnp.concatenate(to_rows(marks), 0)
         masked = (grad_out * grad_mask[..., None].astype(BF16)).reshape(held, piece, width)
         masked, inputs, seg_q = tie(masked, inputs, seg_q)
         upstream = to_rows(masked)
@@ -947,7 +1100,7 @@
         seg_k = all_keys(seg_q)
         mixed, query_side = attention_forward(queries, keys, values, seg_q, seg_k)
         row = lambda vector: vector.reshape(1, -1)
-        hat, scale, normed, active_t, slope, d_second, d_down, second_sums, *result = feed_forward(
+        hat, scale, normed, active_t, slope, d_down, second_sums, *result = feed_forward(
             inputs,
             mixed,
             upstream,
@@ -964,10 +1117,14 @@
                 row(second_shift),
             ),
         )
-        layer_flow = Flow(arriving(send_pieces(result)))
+        table = Timetable()
+        advance = table.advance
+        layer_flow = table.open(arriving(send_pieces(result)))
 
         def chips(own, got, orders, small=None):
-            return Flow(total_over_chips(own, got, core_stage, orders, small))
+            near = small is not None
+            steps = total_over_chips(own, got, core_stage, orders, small, near)
+            return table.open(steps, 2 * len(wide) + 1)
 
         back = functools.partial(
             feed_back,
@@ -977,11 +1134,11 @@
             expand=expand_proj,
             normed=normed,
         )
-        other, other_bias, d_normed = back(1 - core_at, d_down, d_second, norm=None)
+        other, other_bias, d_normed = back(1 - core_at, d_down, norm=None)
         half = other.shape[1]
         got = core_stage.swap(other.reshape(2 * half, width))
-        own, own_bias, d_first, d_attn, d_mixed, first_sums = back(
-            core_at, d_down, d_normed, norm=(hat, scale, row(first_gain), output_proj)
+        own, own_bias, d_attn, d_mixed, first_sums = back(
+            core_at, d_down, norm=(row(first_gain), d_normed, hat, scale, output_proj)
         )
         own, got, d_mixed = advance([layer_flow], own.reshape(2 * half, width), got, d_mixed)
         unit = 16 << len(off_chip)
@@ -1004,77 +1161,68 @@
         d_query, d_keys, d_values = grads
         d_key = own_keys(d_keys)
         d_value = own_keys(d_values)
-        four = (inputs, mixed, d_query, d_key, d_value, d_attn, unit)
-        other = weight_halves(1 - core_at, *four)
+        steps = half // other_bias.shape[1]
+        values = (inputs, d_query, d_key, d_value, mixed, d_attn)
+        (other,) = weight_half(1 - core_at, values, unit)
+        other, *values = advance([], other, *values)
         got = core_stage.swap(other)
-        own = weight_halves(core_at, *four)
-        rows = [
-            column_sum(d_query).reshape(1, width),
-            column_sum(d_value).reshape(1, width),
-            first_sums[2:3],
-            first_sums[0:2],
-            pick(core, [own_bias, other_bias]).reshape(-1, width),
-            pick(core, [other_bias, own_bias]).reshape(-1, width),
-            second_sums[2:3],
-            second_sums[0:2],
-        ]
-        filled = sum(r.shape[0] for r in rows)
-        small = jnp.concatenate(rows + [jnp.zeros((SMALL // 2 - filled, width), F32)], 0)
-        own, got, small, d_query, d_key, d_value = tie(own, got, small, d_query, d_key, d_value)
+        own, small = weight_half(
+            core_at, values, unit, (first_sums, second_sums, own_bias, other_bias), steps
+        )
+        own, got, small = advance([feed_flow], own, got, small)
         attn_flow = chips(own, got, thirds(own.shape[0]), small)
-        d_input = (
-            d_first
-            + right_dot(d_query, query_proj)
-            + right_dot(d_key, key_proj)
-            + right_dot(d_value, value_proj)
-        ).astype(BF16)
-        (d_input,) = advance([feed_flow], d_input)
-        piece_flow = Flow(
-            arriving(send_pieces([d_input[i * piece : (i + 1) * piece] for i in range(held)]))
+        d_query, d_key, d_value = advance([], d_query, d_key, d_value)
+        d_input = input_grad(
+            d_attn, ((d_query, query_proj), (d_key, key_proj), (d_value, value_proj)), held
         )
-
+        d_input = advance([feed_flow], *d_input)
+        piece_flow = table.open(arriving(send_pieces(d_input)))
+
+        layer_out = place_pieces(layer_flow.result)
+        (layer_out,) = advance([attn_flow], layer_out)
+        advance([feed_flow])
         advance([attn_flow])
-        advance([feed_flow, attn_flow])
-        advance([feed_flow, attn_flow, piece_flow])
         advance([attn_flow])
-        advance([feed_flow, attn_flow])
-        while feed_flow.result is None:
-            advance([feed_flow, attn_flow])
-        shrink_grad, expand_grad = feed_out(core_at, *feed_flow.result)
+        advance([feed_flow, piece_flow])
         grad_in = place_pieces(piece_flow.result)
-        layer_out = place_pieces(layer_flow.result)
-        shrink_grad, expand_grad, grad_in, layer_out = advance(
-            [attn_flow], shrink_grad, expand_grad, grad_in, layer_out
-        )
-        while attn_flow.result is None:
+        (grad_in,) = advance([attn_flow], grad_in)
+        advance([attn_flow])
+        while feed_flow.left > 1:
+            advance([feed_flow])
+        feed_grads = feed_out(core_at, feed_flow.pending[0])
+        feed_grads = advance([attn_flow], *feed_grads)
+        advance([feed_flow])
+        feed_grads = feed_out(1 - core_at, feed_flow.result[1], feed_grads)
+        feed_grads = advance([], *feed_grads)
+        while attn_flow.left > 1:
             advance([attn_flow])
+        attn_grads = attn_out(core_at, attn_flow.pending[0])
+        attn_grads = advance([attn_flow], *attn_grads)
         own, got = attn_flow.result
-        attn_grads = attn_out(core_at, own, got, width)
-        tail = [value[-SMALL:].astype(F32) for value in (own, got)]
-        tail = [value[: SMALL // 2] + value[SMALL // 2 :] for value in tail]
-        totals = tail[0] + tail[1]
-        ff_rows = 2 * half // width
-        vectors = [totals[i] for i in range(5)]
-        vectors.append(totals[5 : 5 + ff_rows].reshape(-1))
-        vectors += [totals[i] for i in range(5 + ff_rows, 8 + ff_rows)]
+        attn_grads = attn_out(1 - core_at, got, attn_grads)
+        totals = [value[-SMALL:].astype(F32) for value in (own, got)]
+        totals = [value[: SMALL // 2] + value[SMALL // 2 :] for value in totals]
+        totals = totals[0] + totals[1]
+        shrink_grad, expand_grad = feed_grads
+        expand_bias_grad = totals[8 : 8 + 2 * steps, : other_bias.shape[1]].reshape(-1)
         return (
             layer_out,
             grad_in,
             attn_grads[0],
-            vectors[0],
+            totals[0],
             attn_grads[1],
             attn_grads[2],
-            vectors[1],
+            totals[1],
             attn_grads[3],
-            vectors[2],
-            vectors[3],
-            vectors[4],
+            totals[4],
+            totals[2],
+            totals[3],
             expand_grad,
-            vectors[5],
+            expand_bias_grad,
             shrink_grad,
-            vectors[6],
-            vectors[7],
-            vectors[8],
+            totals[7],
+            totals[5],
+            totals[6],
         )
 
     split = P(None, "rows", "seq", None)

time: 384 us -> 354 us (0.922)
  local copies, waits for them, and re-layouts: 49.4 us -> 14.4 us
  Pallas kernels: 168 us -> 181 us
  waiting for transfers between devices: 79.3 us -> 87.8 us
  other arithmetic: 9.96 us -> 2.78 us
  starting transfers between devices: 60.9 us -> 54.6 us
  matrix products: 8.45 us -> 4.21 us
    unnamed x172 -> x74, local copies, waits for them, and re-layouts: 33.4 us -> 5.39 us
    ppermute x36, waiting for transfers between devices: 50.2 us -> 71.1 us  [swap(): return lax.ppermute(values, ('rows', 'seq'), self.pairs)]
    ppermute x12 -> x8, waiting for transfers between devices: 16.8 us -> 0.02 us  [to_rows(): lax.ppermute(lax.dynamic_index_in_dim(values, source_at ^ part, 0, False)...]
    ppermute x36, starting transfers between devices: 47.3 us -> 39.5 us  [swap(): return lax.ppermute(values, ('rows', 'seq'), self.pairs)]
    ppermute x0 -> x4, waiting for transfers between devices: none -> 7.14 us  [body(): lax.ppermute(value, 'seq', trade(True, part))]
    ppermute x0 -> x4, starting transfers between devices: none -> 6.08 us  [body(): lax.ppermute(value, 'seq', trade(True, part))]
    pallas_call x6, Pallas kernels: 21.5 us -> 27.5 us  [the longest x2 11.8 us: weight_half(): pl.pallas_call(functools.partial(weight_kernel, steps=steps), in_specs=[p...]
    slice x7 -> x2, local copies, waits for them, and re-layouts: 6.06 us -> 0.67 us  [the longest x1 0.66 us: body(): totals[6]]
  transfers between devices with their start and end apart: 56 -> 56, of which waited for: 13 -> 17; matrix products, arithmetic and copies ran while one was open for 8% -> 3% of each run, Pallas kernels for 29% -> 34%
where the time goes in v3:
time: 354 us; the launch traced here: 347 us
  Pallas kernels  181 us (51%)
  waiting for transfers between devices  87.8 us (25%)
  starting transfers between devices  54.6 us (15%)
  local copies, waits for them, and re-layouts  14.4 us (4%)
  matrix products  4.21 us (1%)
    ppermute x36, waiting for transfers between devices, swap(): return lax.ppermute(values, ('rows', 'seq'), self.pairs)  71.1 us
    pallas_call x3, Pallas kernels, attention_backward(): pl.pallas_call(functools.partial(backward_kernel, block=min(512, keys)),...  39.9 us
    ppermute x36, starting transfers between devices, swap(): return lax.ppermute(values, ('rows', 'seq'), self.pairs)  39.5 us
    pallas_call x2, Pallas kernels, feed_back(): pl.pallas_call(functools.partial(feed_back_kernel, steps=steps, block=min...  36.5 us
    pallas_call x1, Pallas kernels, feed_forward(): pl.pallas_call(functools.partial(feed_forward_kernel, steps=steps, held=h...  25.1 us
    pallas_call x1, Pallas kernels, attention_forward(): pl.pallas_call(functools.partial(forward_kernel, block=min(512, queries))...  22.3 us
    pallas_call x17, Pallas kernels, local_call(): pl.pallas_call(kernel, in_specs=[pl.BlockSpec(memory_space=pltpu.SMEM)] +...  14.2 us
    pallas_call x2, Pallas kernels, weight_half(): pl.pallas_call(functools.partial(weight_kernel, steps=steps), in_specs=[p...  11.8 us
  transfers between devices with their start and end apart: 56, of which 17 were waited for; matrix products, arithmetic and copies ran while one was open for 3% of the time, Pallas kernels for 34%

profile of v3, /device:TPU:0, one launch (start us, length us, event | category | flops | bytes accessed | tf_op | source)
XLA Modules:
  0.0 346.8 jit_solution(9200445929686139622)
XLA Ops:
  10.1 3.8 %collective-permute-start = (bf16[256,768]{1,0:T(8,128)(2,1)}, bf16[256,768]{1,0:T(8,128)(2,1)}, u32[]{:S(2)}, u32[]{:S(2)}) collective-permute-start(bf16[256,768]{1,0:T(8,128)(2,1)} %get-tuple-element.629), channel_id=1, source_target_pairs={{0,0},{1,1},{2,2},{3,3},{4,4},{5,5},{6,6},{7,7},{8,8},{9,9},{10,10... | collective-permute-start | bytes 1179656 | tf_op jit(solution)/shard_map/ppermute | solution.py:1086
  20.4 7.1 %collective-permute-done.3 = bf16[256,768]{1,0:T(8,128)(2,1)} collective-permute-done((bf16[256,768]{1,0:T(8,128)(2,1)}, bf16[256,768]{1,0:T(8,128)(2,1)}, u32[]{:S(2)}, u32[]{:S(2)}) %collective-permute-start.3) | collective-permute-done | bytes 393248 | tf_op jit(solution)/shard_map/ppermute | solution.py:1086
  35.4 22.3 %attention_forward.1 = (bf16[1024,768]{1,0:T(8,128)(2,1)}, bf16[12,1024,128]{2,1,0:T(8,128)(2,1)}) custom-call(bf16[1024,768]{1,0:T(8,128)(2,1)S(1)} %multiply_convert_fusion.q_ref, bf16[1024,768]{1,0:T(8,128)(2,1)S(1)} %convolution_convert_fusion.k_ref, bf16[1024,768]{1,0:T(8,128)(2,1)S(1)} %add_convert_fusion.v_ref, ...), custom_call_target="tpu_custom_call" | custom-call | flops 1 | bytes 1 | tf_op jit(solution)/shard_map/attention_forward/pallas_call | solution.py:90
  57.7 25.1 %feed_forward.1 = (bf16[1024,768]{1,0:T(8,128)(2,1)}, f32[1024,128]{1,0:T(8,128)}, bf16[1024,768]{1,0:T(8,128)(2,1)}, bf16[3072,1024]{1,0:T(8,128)(2,1)}, bf16[1...) custom-call(bf16[1024,768]{1,0:T(8,128)(2,1)S(1)} %pad_maximum_fusio, ...), custom_call_target="tpu_custom_call" | custom-call | flops 1 | bytes 1 | tf_op jit(solution)/shard_map/feed_forward/pallas_call | solution.py:327
  82.8 16.3 %feed_back.1 = (bf16[2,1536,768]{2,1,0:T(8,128)(2,1)}, f32[8,512]{1,0:T(8,128)}, bf16[1024,768]{1,0:T(8,128)(2,1)}) custom-call(s32[1]{0:T(128)S(6)} %sub.2.which_ref, bf16[1024,768]{1,0:T(8,128)(2,1)} %get-tuple-element.323.d_down_ref, bf16[1024,3072]{1,0:T(8,128)(2,1)} %get-tuple-element.324.slope_ref, bf16[3072,1024]{1,0:T(8,128)(2,1)} %get-tuple-element.325.active_t_ref, ...), custom_call_target="tpu_custom_call" | custom-call | flops 1 | bytes 1 | tf_op jit(solution)/shard_map/feed_back/pallas_call | solution.py:496
  102.5 20.2 %feed_back_last.1 = (bf16[2,1536,768]{2,1,0:T(8,128)(2,1)}, f32[8,512]{1,0:T(8,128)}, bf16[1024,768]{1,0:T(8,128)(2,1)}, bf16[1024,768]{1,0:T(8,128)(2,1)}, f32[8,768]{1,0:T(8,128)}) custom-call(s32[1]{0:T(128)} %bitcast.1.which_ref, bf16[1024,768]{1,0:T(8,128)(2,1)} %get-tuple-element.323.d_down_ref, bf16[1024,3072]{1,0:T(8,128)(2,1)} %get-tuple-element.324.slope_ref, ...), custom_call_target="tpu_custom_call" | custom-call | flops 1 | bytes 1 | tf_op jit(solution)/shard_map/feed_back_last/pallas_call | solution.py:496
  125.8 4.5 %scatter_first.1 = (bf16[1024,768]{1,0:T(8,128)(2,1)S(1)}, bf16[1024,768]{1,0:T(8,128)(2,1)S(1)}, bf16[512,768]{1,0:T(8,128)(2,1)S(1)}, bf16[512,768]{1,0:T(8,128)(2,1)S(1)}) custom-call(s32[2]{0:T(128)S(1)} %get-tuple-element.633.bits_ref, bf16[3072,768]{1,0:T(8,128)(2,1)} %bitcast.38, bf16[3072,768]{1,0:T(8,128)(2,1)} %collective-permute-done.12.got_at), custom_call_target="tpu_custom_call" | custom-call | flops 1 | bytes 1 | tf_op jit(solution)/shard_map/scatter_first/pallas_call | solution.py:795
  133.2 19.0 %attention_backward.3 = (bf16[1024,768]{1,0:T(8,128)(2,1)}, bf16[1024,768]{1,0:T(8,128)(2,1)}, bf16[1024,768]{1,0:T(8,128)(2,1)}) custom-call(bf16[12,1024,128]{2,1,0:T(8,128)(2,1)} %get-tuple-element.342.query_ref, bf16[1024,768]{1,0:T(8,128)(2,1)S(1)} %convolution_convert_fusion.k_ref, bf16[1024,768]{1,0:T(8,128)(2,1)S(1)} %copy-done.2, ...), custom_call_target="tpu_custom_call" | custom-call | flops 1 | bytes 1 | tf_op jit(solution)/shard_map/attention_backward/pallas_call | solution.py:168
  158.1 13.4 %attention_backward.4 = (bf16[1024,768]{1,0:T(8,128)(2,1)}, bf16[1024,768]{1,0:T(8,128)(2,1)}, bf16[1024,768]{1,0:T(8,128)(2,1)}) custom-call(bf16[12,1024,128]{2,1,0:T(8,128)(2,1)} %get-tuple-element.342.query_ref, bf16[1024,768]{1,0:T(8,128)(2,1)S(1)} %convolution_convert_fusion.k_ref, ...), custom_call_target="tpu_custom_call", output_to_operand_aliasing={{0}: (6, {}), {1}: (7, {}), {2}: (8, {})} | custom-call | flops 1 | bytes 1 | tf_op jit(solution)/shard_map/attention_backward/pallas_call | solution.py:168
  175.0 7.6 %attention_backward.5 = (bf16[1024,768]{1,0:T(8,128)(2,1)}, bf16[1024,768]{1,0:T(8,128)(2,1)}, bf16[1024,768]{1,0:T(8,128)(2,1)}) custom-call(bf16[12,1024,128]{2,1,0:T(8,128)(2,1)} %get-tuple-element.342.query_ref, bf16[1024,768]{1,0:T(8,128)(2,1)S(1)} %convolution_convert_fusion.k_ref, ...), custom_call_target="tpu_custom_call", output_to_operand_aliasing={{0}: (6, {}), {1}: (7, {}), {2}: (8, {})} | custom-call | flops 1 | bytes 1 | tf_op jit(solution)/shard_map/attention_backward/pallas_call | solution.py:168
  183.3 5.9 %weight_half.2 = bf16[1536,768]{1,0:T(8,128)(2,1)S(1)} custom-call(s32[1]{0:T(128)S(6)} %sub.2.which_ref, bf16[1024,768]{1,0:T(8,128)(2,1)} %copy-done, bf16[1024,768]{1,0:T(8,128)(2,1)} %get-tuple-element.444.refs_1_, bf16[1024,768]{1,0:T(8,128)(2,1)} %get-tuple-element.445.refs_2_.refs_3_, bf16[1024,768]{1,0:T(8,128)(2,1)} %get-tuple-element.446.refs_3_.refs_5_, ...), custom_call_target="tpu_custom_call" | custom-call | flops 1 | bytes 1 | tf_op jit(solution)/shard_map/weight_half/pallas_call | solution.py:560
  192.2 5.9 %weight_half.3 = (bf16[1536,768]{1,0:T(8,128)(2,1)S(1)}, f32[16,768]{1,0:T(8,128)S(1)}) custom-call(s32[1]{0:T(128)} %bitcast.1.which_ref, bf16[1024,768]{1,0:T(8,128)(2,1)} %copy-done, bf16[1024,768]{1,0:T(8,128)(2,1)} %get-tuple-element.444.refs_1_, bf16[1024,768]{1,0:T(8,128)(2,1)} %get-tuple-element.445.refs_2_.refs_3_, ...), custom_call_target="tpu_custom_call" | custom-call | flops 1 | bytes 1 | tf_op jit(solution)/shard_map/weight_half/pallas_call | solution.py:560
  198.2 7.7 %collective-permute-done.25.refs_3_ = bf16[64,768]{1,0:T(8,128)(2,1)S(1)} collective-permute-done((bf16[64,768]{1,0:T(8,128)(2,1)S(1)}, bf16[64,768]{1,0:T(8,128)(2,1)S(1)}, u32[]{:S(2)}, u32[]{:S(2)}) %collective-permute-start.25) | collective-permute-done | bytes 98336 | tf_op jit(solution)/shard_map/ppermute | solution.py:917
  212.5 7.8 %input_grad.1 = (bf16[256,768]{1,0:T(8,128)(2,1)S(1)}, bf16[256,768]{1,0:T(8,128)(2,1)S(1)}, bf16[256,768]{1,0:T(8,128)(2,1)S(1)}, bf16[256,768]{1,0:T(8,128)(2,1)S(1)}) custom-call(bf16[1024,768]{1,0:T(8,128)(2,1)} %get-tuple-element.417.refs_5_.refs_0_, bf16[1024,768]{1,0:T(8,128)(2,1)} %get-tuple-element.444.refs_1_, bf16[768,768]{1,0:T(8,128)(2,1)} %refs_2_.1, ...), custom_call_target="tpu_custom_call" | custom-call | flops 1 | bytes 1 | tf_op jit(solution)/shard_map/input_grad/pallas_call | solution.py:599
  224.3 4.2 %collective-permute-start.30 = (bf16[256,768]{1,0:T(8,128)(2,1)S(1)}, bf16[256,768]{1,0:T(8,128)(2,1)S(1)}, u32[]{:S(2)}, u32[]{:S(2)}) collective-permute-start(bf16[256,768]{1,0:T(8,128)(2,1)S(1)} %get-tuple-element.491.refs_0_), channel_id=1, source_target_pairs={{0,8},{1,3},{2,10},{3,1},{4,12},{5,7},{6,14},{7,5},{8,0},{9,11},{1... | collective-permute-start | bytes 1179656 | tf_op jit(solution)/shard_map/ppermute | solution.py:917
  243.7 7.0 %collective-permute-done.35.refs_3_ = bf16[64,768]{1,0:T(8,128)(2,1)S(1)} collective-permute-done((bf16[64,768]{1,0:T(8,128)(2,1)S(1)}, bf16[64,768]{1,0:T(8,128)(2,1)S(1)}, u32[]{:S(2)}, u32[]{:S(2)}) %collective-permute-start.35) | collective-permute-done | bytes 98336 | tf_op jit(solution)/shard_map/ppermute | solution.py:917
  255.3 7.7 %collective-permute-done.41.refs_3_ = bf16[256,768]{1,0:T(8,128)(2,1)S(1)} collective-permute-done((bf16[256,768]{1,0:T(8,128)(2,1)S(1)}, bf16[256,768]{1,0:T(8,128)(2,1)S(1)}, u32[]{:S(2)}, u32[]{:S(2)}) %collective-permute-start.41) | collective-permute-done | bytes 393248 | tf_op jit(solution)/shard_map/ppermute | solution.py:1058
  262.9 8.8 %collective-permute-done.37.refs_3_ = bf16[256,768]{1,0:T(8,128)(2,1)S(1)} collective-permute-done((bf16[256,768]{1,0:T(8,128)(2,1)S(1)}, bf16[256,768]{1,0:T(8,128)(2,1)S(1)}, u32[]{:S(2)}, u32[]{:S(2)}) %collective-permute-start.37) | collective-permute-done | bytes 393248 | tf_op jit(solution)/shard_map/ppermute | solution.py:917
  278.1 16.0 %collective-permute-done.43.refs_3_ = bf16[32,768]{1,0:T(8,128)(2,1)S(1)} collective-permute-done((bf16[32,768]{1,0:T(8,128)(2,1)S(1)}, bf16[32,768]{1,0:T(8,128)(2,1)S(1)}, u32[]{:S(2)}, u32[]{:S(2)}) %collective-permute-start.43) | collective-permute-done | bytes 49184 | tf_op jit(solution)/shard_map/ppermute | solution.py:917
  294.7 3.4 collective-permute-start.44
  298.2 8.9 %collective-permute-done.45.refs_3_ = bf16[32,768]{1,0:T(8,128)(2,1)S(1)} collective-permute-done((bf16[32,768]{1,0:T(8,128)(2,1)S(1)}, bf16[32,768]{1,0:T(8,128)(2,1)S(1)}, u32[]{:S(2)}, u32[]{:S(2)}) %collective-permute-start.45) | collective-permute-done | bytes 49184 | tf_op jit(solution)/shard_map/ppermute | solution.py:917
  308.7 5.2 %feed_out.2 = (f32[3072,768]{1,0:T(8,128)}, f32[768,3072]{1,0:T(8,128)}) custom-call(s32[1]{0:T(128)} %bitcast.1.which_ref, bf16[3072,768]{1,0:T(8,128)(2,1)S(1)} %join_local.12.half_ref), custom_call_target="tpu_custom_call" | custom-call | flops 1 | bytes 1 | tf_op jit(solution)/shard_map/feed_out/pallas_call | solution.py:629
  317.1 5.2 %feed_out.3 = (f32[3072,768]{1,0:T(8,128)}, f32[768,3072]{1,0:T(8,128)}) custom-call(s32[1]{0:T(128)S(6)} %sub.2.which_ref, bf16[3072,768]{1,0:T(8,128)(2,1)S(1)} %collective-permute-done.48.half_ref, f32[3072,768]{1,0:T(8,128)} %get-tuple-element.575.refs_0_, f32[768,3072]{1,0:T(8,128)} %get-tuple-element.576.refs_1_), custom_call_target="tpu_custom_call", output_to_operand_aliasing={{0}: (2, {}), {1}: (3, {})} | custom-call | flops 1 | bytes 1 | tf_op jit(solution)/shard_map/feed_out/pallas_call | solution.py:629
  326.4 9.3 %collective-permute-done.54.refs_3_ = bf16[256,768]{1,0:T(8,128)(2,1)S(1)} collective-permute-done((bf16[256,768]{1,0:T(8,128)(2,1)S(1)}, bf16[256,768]{1,0:T(8,128)(2,1)S(1)}, u32[]{:S(2)}, u32[]{:S(2)}) %collective-permute-start.54) | collective-permute-done | bytes 393248 | tf_op jit(solution)/shard_map/ppermute | solution.py:917
  (230 shorter events, 102.8 us)
Async XLA Ops:
  10.0 17.5 %collective-permute-start.3 = (bf16[256,768]{1,0:T(8,128)(2,1)}, bf16[256,768]{1,0:T(8,128)(2,1)}, u32[]{:S(2)}, u32[]{:S(2)}) collective-permute-start(bf16[256,768]{1,0:T(8,128)(2,1)} %get-tuple-element.317), channel_id=1, source_target_pairs={{0,3},{1,2},{2,1},{3,0},{4,7},{5,6},{6,5},{7,4},{8,11},{9,10},{10,... | collective-permute-start | bytes 1179656 | tf_op jit(solution)/shard_map/ppermute | solution.py:1086
  10.1 17.4 %collective-permute-start = (bf16[256,768]{1,0:T(8,128)(2,1)}, bf16[256,768]{1,0:T(8,128)(2,1)}, u32[]{:S(2)}, u32[]{:S(2)}) collective-permute-start(bf16[256,768]{1,0:T(8,128)(2,1)} %get-tuple-element.629), channel_id=1, source_target_pairs={{0,0},{1,1},{2,2},{3,3},{4,4},{5,5},{6,6},{7,7},{8,8},{9,9},{10,10... | collective-permute-start | bytes 1179656 | tf_op jit(solution)/shard_map/ppermute | solution.py:1086
  29.1 28.5 %collective-permute-start.11 = (bf16[256,768]{1,0:T(8,128)(2,1)S(1)}, bf16[256,768]{1,0:T(8,128)(2,1)S(1)}, u32[]{:S(2)}, u32[]{:S(2)}) collective-permute-start(bf16[256,768]{1,0:T(8,128)(2,1)S(1)} %get-tuple-element.625), channel_id=1, source_target_pairs={{0,3},{1,2},{2,1},{3,0},{4,7},{5,6},{6,5},{7,4},{8,11},{9,10},{10,... | collective-permute-start | bytes 1179656 | tf_op jit(solution)/shard_map/ppermute | solution.py:1046
  30.2 27.4 %collective-permute-start.10 = (bf16[256,768]{1,0:T(8,128)(2,1)S(1)}, bf16[256,768]{1,0:T(8,128)(2,1)S(1)}, u32[]{:S(2)}, u32[]{:S(2)}) collective-permute-start(bf16[256,768]{1,0:T(8,128)(2,1)S(1)} %get-tuple-element.626), channel_id=1, source_target_pairs={{0,2},{1,3},{2,0},{3,1},{4,6},{5,7},{6,4},{7,5},{8,10},{9,11},{10,... | collective-permute-start | bytes 1179656 | tf_op jit(solution)/shard_map/ppermute | solution.py:1046
  31.0 26.7 %collective-permute-start.9 = (bf16[256,768]{1,0:T(8,128)(2,1)S(1)}, bf16[256,768]{1,0:T(8,128)(2,1)S(1)}, u32[]{:S(2)}, u32[]{:S(2)}) collective-permute-start(bf16[256,768]{1,0:T(8,128)(2,1)S(1)} %get-tuple-element.627), channel_id=1, source_target_pairs={{0,1},{1,0},{2,3},{3,2},{4,5},{5,4},{6,7},{7,6},{8,9},{9,8},{10,11... | collective-permute-start | bytes 1179656 | tf_op jit(solution)/shard_map/ppermute | solution.py:1046
  31.0 26.6 %collective-permute-start.8 = (bf16[256,768]{1,0:T(8,128)(2,1)S(1)}, bf16[256,768]{1,0:T(8,128)(2,1)S(1)}, u32[]{:S(2)}, u32[]{:S(2)}) collective-permute-start(bf16[256,768]{1,0:T(8,128)(2,1)S(1)} %get-tuple-element.628), channel_id=1, source_target_pairs={{0,0},{1,1},{2,2},{3,3},{4,4},{5,5},{6,6},{7,7},{8,8},{9,9},{10,10... | collective-permute-start | bytes 1179656 | tf_op jit(solution)/shard_map/ppermute | solution.py:1046
  99.0 26.7 %collective-permute-start.12 = (bf16[3072,768]{1,0:T(8,128)(2,1)}, bf16[3072,768]{1,0:T(8,128)(2,1)}, u32[]{:S(2)}, u32[]{:S(2)}) collective-permute-start(bf16[3072,768]{1,0:T(8,128)(2,1)} %bitcast.43), channel_id=1, source_target_pairs={{0,1},{1,0},{2,3},{3,2},{4,5},{5,4},{6,7},{7,6},{8,9},{9,8},{10,11... | collective-permute-start | bytes 14155784 | tf_op jit(solution)/shard_map/ppermute | solution.py:917
  99.6 23.2 %collective-permute-start.13 = (bf16[256,768]{1,0:T(8,128)(2,1)}, bf16[256,768]{1,0:T(8,128)(2,1)S(1)}, u32[]{:S(2)}, u32[]{:S(2)}) collective-permute-start(bf16[256,768]{1,0:T(8,128)(2,1)} %get-tuple-element.333), channel_id=1, source_target_pairs={{0,0},{1,1},{2,2},{3,3},{4,4},{5,5},{6,6},{7,7},{8,8},{9,9},{10,10... | collective-permute-start | bytes 1179656 | tf_op jit(solution)/shard_map/ppermute | solution.py:1058
  100.5 22.9 %collective-permute-start.14 = (bf16[256,768]{1,0:T(8,128)(2,1)}, bf16[256,768]{1,0:T(8,128)(2,1)S(1)}, u32[]{:S(2)}, u32[]{:S(2)}) collective-permute-start(bf16[256,768]{1,0:T(8,128)(2,1)} %get-tuple-element.334), channel_id=1, source_target_pairs={{1,0},{0,1},{3,2},{2,3},{5,4},{4,5},{7,6},{6,7},{9,8},{8,9},{11,10... | collective-permute-start | bytes 1179656 | tf_op jit(solution)/shard_map/ppermute | solution.py:1058
  100.6 23.6 %collective-permute-start.15 = (bf16[256,768]{1,0:T(8,128)(2,1)}, bf16[256,768]{1,0:T(8,128)(2,1)S(1)}, u32[]{:S(2)}, u32[]{:S(2)}) collective-permute-start(bf16[256,768]{1,0:T(8,128)(2,1)} %get-tuple-element.335), channel_id=1, source_target_pairs={{2,0},{3,1},{0,2},{1,3},{6,4},{7,5},{4,6},{5,7},{10,8},{11,9},{8,1... | collective-permute-start | bytes 1179656 | tf_op jit(solution)/shard_map/ppermute | solution.py:1058
  101.9 23.1 %collective-permute-start.16 = (bf16[256,768]{1,0:T(8,128)(2,1)}, bf16[256,768]{1,0:T(8,128)(2,1)S(1)}, u32[]{:S(2)}, u32[]{:S(2)}) collective-permute-start(bf16[256,768]{1,0:T(8,128)(2,1)} %get-tuple-element.336), channel_id=1, source_target_pairs={{3,0},{2,1},{1,2},{0,3},{7,4},{6,5},{5,6},{4,7},{11,8},{10,9},{9,1... | collective-permute-start | bytes 1179656 | tf_op jit(solution)/shard_map/ppermute | solution.py:1058
  130.2 21.9 %collective-permute-start.17 = (bf16[1024,768]{1,0:T(8,128)(2,1)S(1)}, bf16[1024,768]{1,0:T(8,128)(2,1)S(1)}, u32[]{:S(2)}, u32[]{:S(2)}) collective-permute-start(bf16[1024,768]{1,0:T(8,128)(2,1)S(1)} %get-tuple-element.353), channel_id=1, source_target_pairs={{0,2},{1,5},{2,0},{3,7},{4,6},{5,1},{6,4},{7,3},{8,10},{9,13},{10,... | collective-permute-start | bytes 4718600 | tf_op jit(solution)/shard_map/ppermute | solution.py:917
  131.6 20.5 %collective-permute-start.18 = (bf16[512,768]{1,0:T(8,128)(2,1)S(1)}, bf16[512,768]{1,0:T(8,128)(2,1)S(1)}, u32[]{:S(2)}, u32[]{:S(2)}) collective-permute-start(bf16[512,768]{1,0:T(8,128)(2,1)S(1)} %get-tuple-element.355), channel_id=1, source_target_pairs={{0,8},{1,9},{2,10},{3,11},{4,12},{5,13},{6,14},{7,15},{8,0},{9,1},... | collective-permute-start | bytes 2359304 | tf_op jit(solution)/shard_map/ppermute | solution.py:917
  155.8 15.7 %collective-permute-start.19 = (bf16[512,768]{1,0:T(8,128)(2,1)}, bf16[512,768]{1,0:T(8,128)(2,1)}, u32[]{:S(2)}, u32[]{:S(2)}) collective-permute-start(bf16[512,768]{1,0:T(8,128)(2,1)} %get-tuple-element.374), channel_id=1, source_target_pairs={{0,4},{1,9},{2,6},{3,11},{4,0},{5,13},{6,2},{7,15},{8,12},{9,1},{1... | collective-permute-start | bytes 2359304 | tf_op jit(solution)/shard_map/ppermute | solution.py:917
  189.2 16.7 %collective-permute-start.23 = (bf16[1536,768]{1,0:T(8,128)(2,1)S(1)}, bf16[1536,768]{1,0:T(8,128)(2,1)S(1)}, u32[]{:S(2)}, u32[]{:S(2)}) collective-permute-start(bf16[1536,768]{1,0:T(8,128)(2,1)S(1)} %weight_half.2), channel_id=1, source_target_pairs={{0,1},{1,0},{2,3},{3,2},{4,5},{5,4},{6,7},{7,6},{8,9},{9,8},{10,11... | collective-permute-start | bytes 7077896 | tf_op jit(solution)/shard_map/ppermute | solution.py:917
  189.2 16.6 %collective-permute-start.24 = (bf16[128,768]{1,0:T(8,128)(2,1)S(1)}, bf16[128,768]{1,0:T(8,128)(2,1)S(1)}, u32[]{:S(2)}, u32[]{:S(2)}) collective-permute-start(bf16[128,768]{1,0:T(8,128)(2,1)S(1)} %get-tuple-element.426), channel_id=1, source_target_pairs={{0,16},{1,17},{2,18},{3,19},{4,20},{5,21},{6,22},{7,23},{8,24},{9,... | collective-permute-start | bytes 589832 | tf_op jit(solution)/shard_map/ppermute | solution.py:917
  207.8 22.8 %collective-permute-start.28 = (bf16[512,768]{1,0:T(8,128)(2,1)S(1)}, bf16[512,768]{1,0:T(8,128)(2,1)S(1)}, u32[]{:S(2)}, u32[]{:S(2)}) collective-permute-start(bf16[512,768]{1,0:T(8,128)(2,1)S(1)} %get-tuple-element.470), channel_id=1, source_target_pairs={{0,2},{1,5},{2,0},{3,7},{4,6},{5,1},{6,4},{7,3},{8,10},{9,13},{10,... | collective-permute-start | bytes 2359304 | tf_op jit(solution)/shard_map/ppermute | solution.py:917
  208.6 22.0 %collective-permute-start.29 = (bf16[256,768]{1,0:T(8,128)(2,1)S(1)}, bf16[256,768]{1,0:T(8,128)(2,1)S(1)}, u32[]{:S(2)}, u32[]{:S(2)}) collective-permute-start(bf16[256,768]{1,0:T(8,128)(2,1)S(1)} %get-tuple-element.472), channel_id=1, source_target_pairs={{0,8},{1,9},{2,10},{3,11},{4,12},{5,13},{6,14},{7,15},{8,0},{9,1},... | collective-permute-start | bytes 1179656 | tf_op jit(solution)/shard_map/ppermute | solution.py:917
  236.5 35.2 %collective-permute-start.36 = (bf16[512,768]{1,0:T(8,128)(2,1)S(1)}, bf16[512,768]{1,0:T(8,128)(2,1)S(1)}, u32[]{:S(2)}, u32[]{:S(2)}) collective-permute-start(bf16[512,768]{1,0:T(8,128)(2,1)S(1)} %get-tuple-element.523.refs_0_), channel_id=1, source_target_pairs={{0,4},{1,9},{2,6},{3,11},{4,0},{5,13},{6,2},{7,15},{8,12},{9,1},{1... | collective-permute-start | bytes 2359304 | tf_op jit(solution)/shard_map/ppermute | solution.py:917
  250.7 21.1 %collective-permute-start.37 = (bf16[256,768]{1,0:T(8,128)(2,1)S(1)}, bf16[256,768]{1,0:T(8,128)(2,1)S(1)}, u32[]{:S(2)}, u32[]{:S(2)}) collective-permute-start(bf16[256,768]{1,0:T(8,128)(2,1)S(1)} %get-tuple-element.525.refs_2_), channel_id=1, source_target_pairs={{0,2},{1,3},{2,0},{3,1},{4,6},{5,7},{6,4},{7,5},{8,10},{9,11},{10,... | collective-permute-start | bytes 1179656 | tf_op jit(solution)/shard_map/ppermute | solution.py:917
  272.5 35.2 %collective-permute-start.46 = (bf16[1024,768]{1,0:T(8,128)(2,1)S(1)}, bf16[1024,768]{1,0:T(8,128)(2,1)S(1)}, u32[]{:S(2)}, u32[]{:S(2)}) collective-permute-start(bf16[1024,768]{1,0:T(8,128)(2,1)S(1)} %get-tuple-element.556.refs_0_), channel_id=1, source_target_pairs={{0,2},{1,5},{2,0},{3,7},{4,6},{5,1},{6,4},{7,3},{8,10},{9,13},{10,... | collective-permute-start | bytes 4718600 | tf_op jit(solution)/shard_map/ppermute | solution.py:917
  272.6 35.1 %collective-permute-start.47 = (bf16[512,768]{1,0:T(8,128)(2,1)S(1)}, bf16[512,768]{1,0:T(8,128)(2,1)S(1)}, u32[]{:S(2)}, u32[]{:S(2)}) collective-permute-start(bf16[512,768]{1,0:T(8,128)(2,1)S(1)} %get-tuple-element.558.refs_2_), channel_id=1, source_target_pairs={{0,8},{1,9},{2,10},{3,11},{4,12},{5,13},{6,14},{7,15},{8,0},{9,1},... | collective-permute-start | bytes 2359304 | tf_op jit(solution)/shard_map/ppermute | solution.py:917
  273.5 20.6 %collective-permute-start.42 = (bf16[64,768]{1,0:T(8,128)(2,1)S(1)}, bf16[64,768]{1,0:T(8,128)(2,1)S(1)}, u32[]{:S(2)}, u32[]{:S(2)}) collective-permute-start(bf16[64,768]{1,0:T(8,128)(2,1)S(1)} %get-tuple-element.530), channel_id=1, source_target_pairs={{0,16},{1,17},{2,18},{3,19},{4,20},{5,21},{6,22},{7,23},{8,24},{9,... | collective-permute-start | bytes 294920 | tf_op jit(solution)/shard_map/ppermute | solution.py:917
  273.9 20.2 %collective-permute-start.43 = (bf16[32,768]{1,0:T(8,128)(2,1)S(1)}, bf16[32,768]{1,0:T(8,128)(2,1)S(1)}, u32[]{:S(2)}, u32[]{:S(2)}) collective-permute-start(bf16[32,768]{1,0:T(8,128)(2,1)S(1)} %get-tuple-element.532), channel_id=1, source_target_pairs={{0,16},{1,17},{2,18},{3,19},{4,20},{5,21},{6,22},{7,23},{8,24},{9,... | collective-permute-start | bytes 147464 | tf_op jit(solution)/shard_map/ppermute | solution.py:917
  (69 other events, 563.0 us)
